TPU v7x, 256 devices: a whole 4x4x8 slice. The times are simulated.
256 devices in a mesh: gx: 32 (over z, y_hi, core), gy: 8 (over x, y_lo).
Axes of the slice: x: 4, y: 4 (y_hi: 2, y_lo: 2; y = y_hi * 2 + y_lo), z: 8, core: 2. Of those that a mesh axis runs over, the one named last changes fastest.
Arguments:
- courant: float32 [512, 128, 256], P('gx', 'gy'), may hold values from 0.05 to 0.18
- vel_entering: float32 [16, 128, 256], P(None, 'gy'), may hold values from 0.05 to 0.18
- image: float32 [512, 128, 256], P('gx', 'gy'), may hold values from -6 to 6
- src_prev: float32 [512, 128, 256], P('gx', 'gy'), may hold values from -6 to 6
- src_cur: float32 [512, 128, 256], P('gx', 'gy'), may hold values from -6 to 6
- rcv_prev: float32 [512, 128, 256], P('gx', 'gy'), may hold values from -6 to 6
- rcv_cur: float32 [512, 128, 256], P('gx', 'gy'), may hold values from -6 to 6
- global_image: float32 [512, 128, 256], P('gx', 'gy'), may hold values from -6 to 6
- shift_map: int32 [128], P('gy'), may hold values from 0 to 1, as said below
- image_owner: int32 [8, 32], P('gy'), may hold values from 0 to 31, each once within a row
Outputs:
- global_out: float32 [512, 128, 256], P('gx', 'gy')
- image_out: float32 [512, 128, 256], P('gx', 'gy')
- src_prev_out: float32 [512, 128, 256], P('gx', 'gy')
- src_cur_out: float32 [512, 128, 256], P('gx', 'gy')
- rcv_prev_out: float32 [512, 128, 256], P('gx', 'gy')
- rcv_cur_out: float32 [512, 128, 256], P('gx', 'gy')
Inputs may be any that keep to these rules, and one draw needn't show every extreme that they name: `shift_map`: exactly 64 crosslines move, which ones varies. Each row of image_owner names every index along gx once.
All inputs are finite; a program needn't handle non-finite values.
Results may differ from a plain program's by a relative error of at most 0.00002.
Values sent between devices are 32-bit elements; how exact they have to be, the bound alone decides.
No kernel may reach another device: no remote copies, remote signals or barrier semaphores. Data moves between devices by JAX's collectives and lax.ppermute only.
A program may use at most 64 MiB of HBM per device.

v0:
```python
import jax
import jax.numpy as jnp
from jax import lax
from jax.sharding import PartitionSpec as P

STEPS = 4


STENCIL = (-205.0 / 72.0, 8.0 / 5.0, -1.0 / 5.0, 8.0 / 315.0, -1.0 / 560.0)


def spread(shard, axis, root):
    mine = lax.axis_index(axis) == root
    return lax.psum(jnp.where(mine, shard, jnp.zeros_like(shard)), axis)


def from_behind(value, axis, steps):
    count = lax.axis_size(axis)
    initial, last = (max(0, -steps), min(count, count - steps))
    return lax.ppermute(value, axis, [(source, source + steps) for source in range(initial, last)])


def extended(block, sides, width):
    for axis, dim in sides:
        count = lax.axis_size(axis)
        forward = [(i, i + 1) for i in range(count - 1)]
        backward = [(target, source) for source, target in forward]
        low = lax.ppermute(
            lax.slice_in_dim(block, block.shape[dim] - width, None, axis=dim), axis, forward
        )
        high = lax.ppermute(lax.slice_in_dim(block, 0, width, axis=dim), axis, backward)
        block = jnp.concatenate([low, block, high], axis=dim)
    return block


def shifted_view(padded, which_axis, reach):
    leading = padded.ndim - 3
    selector = [slice(None)] * padded.ndim
    for each_axis in range(3):
        extent = padded.shape[leading + each_axis]
        displacement = reach if each_axis == which_axis else 0
        selector[leading + each_axis] = slice(4 + displacement, extent - 4 + displacement)
    return padded[tuple(selector)]


def laplace(padded):
    accumulated = 3.0 * STENCIL[0] * shifted_view(padded, 0, 0)
    for reach in range(1, 5):
        for which_axis in range(3):
            accumulated = accumulated + STENCIL[reach] * (
                shifted_view(padded, which_axis, reach) + shifted_view(padded, which_axis, -reach)
            )
    return accumulated


def depth_padded(field):
    return jnp.pad(field, ((0, 0), (0, 0), (0, 0), (4, 4)))


def body(
    courant,
    vel_entering,
    image,
    src_prev,
    src_cur,
    rcv_prev,
    rcv_cur,
    global_image,
    shift_map,
    image_owner,
):
    column = lax.axis_index("gx")
    cycle_size = lax.axis_size("gx")
    moved = (shift_map == 1)[None, :, None]
    slab_cells = image.shape[2] // cycle_size
    slab_owner = jnp.repeat(image_owner[0], slab_cells)
    leaving = spread(jnp.where(moved, image, jnp.float32(0.0)), "gx", 0)
    global_out = global_image + jnp.where(
        (slab_owner == column)[None, None, :], leaving, jnp.float32(0.0)
    )
    previous = jnp.stack([src_prev, rcv_prev])
    current = jnp.stack([src_cur, rcv_cur])
    arrived = from_behind((courant, image, previous, current), "gx", -1)
    is_last = column == cycle_size - 1
    velocity = jnp.where(moved, jnp.where(is_last, vel_entering, arrived[0]), courant)
    picture = jnp.where(moved, arrived[1], image)
    previous = jnp.where(moved[None], arrived[2], previous)
    current = jnp.where(moved[None], arrived[3], current)
    for step_index in range(STEPS):
        padded = extended(current, (("gx", 1), ("gy", 2)), 4)
        following = 2.0 * current - previous + velocity * laplace(depth_padded(padded))
        previous, current = (current, following)
        picture = picture + following[0] * following[1]
    return (global_out, picture, previous[0], current[0], previous[1], current[1])


def solution(mesh):
    in_specs = (
        P("gx", "gy", None),
        P(None, "gy", None),
        P("gx", "gy", None),
        P("gx", "gy", None),
        P("gx", "gy", None),
        P("gx", "gy", None),
        P("gx", "gy", None),
        P("gx", "gy", None),
        P("gy"),
        P("gy", None),
    )
    out_specs = (
        P("gx", "gy", None),
        P("gx", "gy", None),
        P("gx", "gy", None),
        P("gx", "gy", None),
        P("gx", "gy", None),
        P("gx", "gy", None),
    )
    return jax.shard_map(body, mesh=mesh, in_specs=in_specs, out_specs=out_specs, check_vma=False)
```

profile of v0, /device:TPU:1, one launch (start us, length us, event | category | flops | bytes accessed | tf_op | source)
XLA Modules:
  0.0 415.7 jit_solution(785867634265281817)
XLA Ops:
  7.2 0.0 all-reduce.6.cloned.1.call-start
  7.2 1.1 pad_maximum_fusion.12
  8.3 5.1 %collective-permute-start.1 = (f32[2,16,16,256]{3,2,1,0:T(8,128)S(1)}, f32[2,16,16,256]{3,2,1,0:T(8,128)S(1)}, u32[]{:S(2)}, u32[]{:S(2)}) collective-permute-start(f32[2,16,16,256]{3,2,1,0:T(8,128)S(1)} %pad_maximum_fusion.12), channel_id=1, source_target_pairs={{8,0},{16,8},{24,16},{32,24},{40,32},{48,40},{56,48},{64,56},{72,6... | collective-permute-start | bytes 1572872 | tf_op jit(solution)/shard_map/ppermute | solution.py:20
  13.5 1.9 collective-permute-start.3
  15.4 0.7 broadcast_compare_fusion
  16.1 5.3 %collective-permute-done.1 = f32[2,16,16,256]{3,2,1,0:T(8,128)S(1)} collective-permute-done((f32[2,16,16,256]{3,2,1,0:T(8,128)S(1)}, f32[2,16,16,256]{3,2,1,0:T(8,128)S(1)}, u32[]{:S(2)}, u32[]{:S(2)}) %collective-permute-start.1) | collective-permute-done | bytes 524320 | tf_op jit(solution)/shard_map/ppermute | solution.py:20
  21.4 1.2 broadcast_select_fusion
  22.6 2.1 collective-permute-start.4
  24.7 5.1 %collective-permute-start.5 = (f32[2,4,16,256]{3,2,1,0:T(8,128)S(1)}, f32[2,4,16,256]{3,2,1,0:T(8,128)S(1)}, u32[]{:S(2)}, u32[]{:S(2)}) collective-permute-start(f32[2,4,16,256]{3,2,1,0:T(8,128)S(1)} %get-tuple-element.34), channel_id=1, source_target_pairs={{0,8},{8,16},{16,24},{24,32},{32,40},{40,48},{48,56},{56,64},{64,7... | collective-permute-start | bytes 393224 | tf_op jit(solution)/shard_map/ppermute | solution.py:28
  29.9 1.9 collective-permute-start.2
  31.9 1.2 collective-permute-done.5
  33.0 0.1 pad_maximum_fusion.23
  33.1 1.3 collective-permute-start.6
  34.4 4.0 collective-permute-start.7
  38.4 1.1 select_select_fusion
  39.5 5.6 %collective-permute-done.6 = f32[2,24,4,256]{3,2,1,0:T(4,128)S(1)} collective-permute-done((f32[2,24,4,256]{3,2,1,0:T(4,128)S(1)}, f32[2,24,4,256]{3,2,1,0:T(4,128)S(1)}, u32[]{:S(2)}, u32[]{:S(2)}) %collective-permute-start.6) | collective-permute-done | bytes 196640 | tf_op jit(solution)/shard_map/ppermute | solution.py:31
  45.1 2.3 collective-permute-done.7
  47.5 0.2 pad_maximum_fusion
  47.7 0.9 select_maximum_fusion.12
  48.6 2.0 fusion.89
  50.7 1.9 collective-permute-start.8
  52.6 5.1 %collective-permute-start.9 = (f32[2,4,16,256]{3,2,1,0:T(8,128)S(1)}, f32[2,4,16,256]{3,2,1,0:T(8,128)S(1)}, u32[]{:S(2)}, u32[]{:S(2)}) collective-permute-start(f32[2,4,16,256]{3,2,1,0:T(8,128)S(1)} %get-tuple-element.32), channel_id=1, source_target_pairs={{0,8},{8,16},{16,24},{24,32},{32,40},{40,48},{48,56},{56,64},{64,7... | collective-permute-start | bytes 393224 | tf_op jit(solution)/shard_map/ppermute | solution.py:28
  57.8 0.7 collective-permute-done.8
  58.5 2.6 collective-permute-done.9
  61.0 0.1 pad_maximum_fusion.20
  61.1 1.3 collective-permute-start.10
  62.4 5.5 %collective-permute-start.11 = (f32[2,24,4,256]{3,2,1,0:T(4,128)S(1)}, f32[2,24,4,256]{3,2,1,0:T(4,128)S(1)}, u32[]{:S(2)}, u32[]{:S(2)}) collective-permute-start(f32[2,24,4,256]{3,2,1,0:T(4,128)S(1)} %get-tuple-element.21), channel_id=1, source_target_pairs={{0,1},{1,2},{2,3},{3,4},{4,5},{5,6},{6,7},{8,9},{9,10},{10,11},{11... | collective-permute-start | bytes 589832 | tf_op jit(solution)/shard_map/ppermute | solution.py:28
  67.9 1.1 collective-permute-done.10
  69.0 2.8 collective-permute-done.11
  71.8 0.2 pad_maximum_fusion.1
  72.1 0.9 select_maximum_fusion.8
  73.0 0.1 copy-done.1
  73.1 2.0 fusion.63
  75.1 1.9 collective-permute-start.12
  77.0 9.4 %collective-permute-start.13 = (f32[2,4,16,256]{3,2,1,0:T(8,128)S(1)}, f32[2,4,16,256]{3,2,1,0:T(8,128)S(1)}, u32[]{:S(2)}, u32[]{:S(2)}) collective-permute-start(f32[2,4,16,256]{3,2,1,0:T(8,128)S(1)} %get-tuple-element.30), channel_id=1, source_target_pairs={{0,8},{8,16},{16,24},{24,32},{32,40},{40,48},{48,56},{56,64},{64,7... | collective-permute-start | bytes 393224 | tf_op jit(solution)/shard_map/ppermute | solution.py:28
  86.4 0.7 collective-permute-done.12
  87.1 5.2 %collective-permute-done.13 = f32[2,4,16,256]{3,2,1,0:T(8,128)S(1)} collective-permute-done((f32[2,4,16,256]{3,2,1,0:T(8,128)S(1)}, f32[2,4,16,256]{3,2,1,0:T(8,128)S(1)}, u32[]{:S(2)}, u32[]{:S(2)}) %collective-permute-start.13) | collective-permute-done | bytes 131104 | tf_op jit(solution)/shard_map/ppermute | solution.py:28
  92.4 0.1 pad_maximum_fusion.17
  92.4 1.3 collective-permute-start.14
  93.7 4.0 collective-permute-start.15
  97.7 1.1 collective-permute-done.14
  98.9 1.5 collective-permute-done.15
  100.3 0.2 pad_maximum_fusion.2
  100.5 0.9 select_maximum_fusion.4
  101.5 1.5 fusion.37
  103.0 1.9 collective-permute-start.16
  105.0 8.0 %collective-permute-start.17 = (f32[2,4,16,256]{3,2,1,0:T(8,128)S(1)}, f32[2,4,16,256]{3,2,1,0:T(8,128)S(1)}, u32[]{:S(2)}, u32[]{:S(2)}) collective-permute-start(f32[2,4,16,256]{3,2,1,0:T(8,128)S(1)} %get-tuple-element.28), channel_id=1, source_target_pairs={{0,8},{8,16},{16,24},{24,32},{32,40},{40,48},{48,56},{56,64},{64,7... | collective-permute-start | bytes 393224 | tf_op jit(solution)/shard_map/ppermute | solution.py:28
  112.9 0.7 collective-permute-done.16
  113.6 3.9 collective-permute-done.17
  117.5 0.1 pad_maximum_fusion.14
  117.6 1.3 collective-permute-start.18
  118.9 4.0 collective-permute-start.19
  122.9 1.9 collective-permute-start
  124.8 2.5 collective-permute-done.19
  127.3 0.2 pad_maximum_fusion.3
  127.5 0.9 select_maximum_fusion
  128.5 1.5 fusion.11
  130.0 4.8 %collective-permute-done = f32[16,16,256]{2,1,0:T(8,128)S(1)} collective-permute-done((f32[16,16,256]{2,1,0:T(8,128)S(1)}, f32[16,16,256]{2,1,0:T(8,128)S(1)}, u32[]{:S(2)}, u32[]{:S(2)}) %collective-permute-start) | collective-permute-done | bytes 262176 | tf_op jit(solution)/shard_map/ppermute | solution.py:20
  134.9 1.2 fusion.148
  136.1 0.0 all-reduce.6.cloned.1.call-update
  136.1 0.1 broadcast_in_dim.52
  136.2 0.1 eq.29
  136.3 270.8 %all-reduce.6.cloned.1.call-done = f32[16,16,256]{2,1,0:T(8,128)} async-done(((f32[16,16,256]{2,1,0:T(8,128)}), f32[16,16,256]{2,1,0:T(8,128)}) %all-reduce.6.cloned.1.call-update) | async-done | bytes 262160 | tf_op jit(solution)/shard_map/psum | solution.py:14
  407.1 1.7 select_add_fusion
  (25 shorter events, 0.2 us)
Async XLA Ops:
  7.2 22.7 %copy-start.3 = (f32[16,16,256]{2,1,0:T(8,128)S(1)}, f32[16,16,256]{2,1,0:T(8,128)}, u32[]{:S(2)}) copy-start(f32[16,16,256]{2,1,0:T(8,128)} %param.13) | copy-start | bytes 786436
  7.2 22.7 %copy-start.2 = (f32[16,16,256]{2,1,0:T(8,128)S(1)}, f32[16,16,256]{2,1,0:T(8,128)}, u32[]{:S(2)}) copy-start(f32[16,16,256]{2,1,0:T(8,128)} %param.15) | copy-start | bytes 786436
  7.2 400.0 %all-reduce.6.cloned.1.call-start = ((), (), s32[]{:S(2)}) async-start(), calls=%async_computation | async-start | bytes 524288 | tf_op jit(solution)/shard_map/psum | solution.py:14
  8.3 13.1 %collective-permute-start.1 = (f32[2,16,16,256]{3,2,1,0:T(8,128)S(1)}, f32[2,16,16,256]{3,2,1,0:T(8,128)S(1)}, u32[]{:S(2)}, u32[]{:S(2)}) collective-permute-start(f32[2,16,16,256]{3,2,1,0:T(8,128)S(1)} %pad_maximum_fusion.12), channel_id=1, source_target_pairs={{8,0},{16,8},{24,16},{32,24},{40,32},{48,40},{56,48},{64,56},{72,6... | collective-permute-start | bytes 1572872 | tf_op jit(solution)/shard_map/ppermute | solution.py:20
  13.5 24.9 %collective-permute-start.3 = (f32[16,16,256]{2,1,0:T(8,128)}, f32[16,16,256]{2,1,0:T(8,128)}, u32[]{:S(2)}, u32[]{:S(2)}) collective-permute-start(f32[16,16,256]{2,1,0:T(8,128)} %param.10), channel_id=1, source_target_pairs={{8,0},{16,8},{24,16},{32,24},{40,32},{48,40},{56,48},{64,56},{72,6... | collective-permute-start | bytes 786440 | tf_op jit(solution)/shard_map/ppermute | solution.py:20
  22.6 15.8 %copy-start.4 = (f32[16,16,256]{2,1,0:T(8,128)S(1)}, f32[16,16,256]{2,1,0:T(8,128)}, u32[]{:S(2)}) copy-start(f32[16,16,256]{2,1,0:T(8,128)} %param.10) | copy-start | bytes 786436
  22.6 9.2 %collective-permute-start.4 = (f32[2,4,16,256]{3,2,1,0:T(8,128)S(1)}, f32[2,4,16,256]{3,2,1,0:T(8,128)S(1)}, u32[]{:S(2)}, u32[]{:S(2)}) collective-permute-start(f32[2,4,16,256]{3,2,1,0:T(8,128)S(1)} %get-tuple-element.33), channel_id=1, source_target_pairs={{8,0},{16,8},{24,16},{32,24},{40,32},{48,40},{56,48},{64,56},{72,6... | collective-permute-start | bytes 393224 | tf_op jit(solution)/shard_map/ppermute | solution.py:31
  24.7 8.3 %collective-permute-start.5 = (f32[2,4,16,256]{3,2,1,0:T(8,128)S(1)}, f32[2,4,16,256]{3,2,1,0:T(8,128)S(1)}, u32[]{:S(2)}, u32[]{:S(2)}) collective-permute-start(f32[2,4,16,256]{3,2,1,0:T(8,128)S(1)} %get-tuple-element.34), channel_id=1, source_target_pairs={{0,8},{8,16},{16,24},{24,32},{32,40},{40,48},{48,56},{56,64},{64,7... | collective-permute-start | bytes 393224 | tf_op jit(solution)/shard_map/ppermute | solution.py:28
  29.9 18.7 %collective-permute-start.2 = (f32[2,16,16,256]{3,2,1,0:T(8,128)S(1)}, f32[2,16,16,256]{3,2,1,0:T(8,128)S(1)}, u32[]{:S(2)}, u32[]{:S(2)}) collective-permute-start(f32[2,16,16,256]{3,2,1,0:T(8,128)S(1)} %pad_maximum_fusion.13), channel_id=1, source_target_pairs={{8,0},{16,8},{24,16},{32,24},{40,32},{48,40},{56,48},{64,56},{72,6... | collective-permute-start | bytes 1572872 | tf_op jit(solution)/shard_map/ppermute | solution.py:20
  33.1 12.0 %collective-permute-start.6 = (f32[2,24,4,256]{3,2,1,0:T(4,128)S(1)}, f32[2,24,4,256]{3,2,1,0:T(4,128)S(1)}, u32[]{:S(2)}, u32[]{:S(2)}) collective-permute-start(f32[2,24,4,256]{3,2,1,0:T(4,128)S(1)} %get-tuple-element.26), channel_id=1, source_target_pairs={{1,0},{2,1},{3,2},{4,3},{5,4},{6,5},{7,6},{9,8},{10,9},{11,10},{12... | collective-permute-start | bytes 589832 | tf_op jit(solution)/shard_map/ppermute | solution.py:31
  34.4 13.1 %collective-permute-start.7 = (f32[2,24,4,256]{3,2,1,0:T(4,128)S(1)}, f32[2,24,4,256]{3,2,1,0:T(4,128)S(1)}, u32[]{:S(2)}, u32[]{:S(2)}) collective-permute-start(f32[2,24,4,256]{3,2,1,0:T(4,128)S(1)} %get-tuple-element.25), channel_id=1, source_target_pairs={{0,1},{1,2},{2,3},{3,4},{4,5},{5,6},{6,7},{8,9},{9,10},{10,11},{11... | collective-permute-start | bytes 589832 | tf_op jit(solution)/shard_map/ppermute | solution.py:28
  50.7 7.8 %collective-permute-start.8 = (f32[2,4,16,256]{3,2,1,0:T(8,128)S(1)}, f32[2,4,16,256]{3,2,1,0:T(8,128)S(1)}, u32[]{:S(2)}, u32[]{:S(2)}) collective-permute-start(f32[2,4,16,256]{3,2,1,0:T(8,128)S(1)} %get-tuple-element.31), channel_id=1, source_target_pairs={{8,0},{16,8},{24,16},{32,24},{40,32},{48,40},{56,48},{64,56},{72,6... | collective-permute-start | bytes 393224 | tf_op jit(solution)/shard_map/ppermute | solution.py:31
  52.6 8.4 %collective-permute-start.9 = (f32[2,4,16,256]{3,2,1,0:T(8,128)S(1)}, f32[2,4,16,256]{3,2,1,0:T(8,128)S(1)}, u32[]{:S(2)}, u32[]{:S(2)}) collective-permute-start(f32[2,4,16,256]{3,2,1,0:T(8,128)S(1)} %get-tuple-element.32), channel_id=1, source_target_pairs={{0,8},{8,16},{16,24},{24,32},{32,40},{40,48},{48,56},{56,64},{64,7... | collective-permute-start | bytes 393224 | tf_op jit(solution)/shard_map/ppermute | solution.py:28
  61.1 7.9 %collective-permute-start.10 = (f32[2,24,4,256]{3,2,1,0:T(4,128)S(1)}, f32[2,24,4,256]{3,2,1,0:T(4,128)S(1)}, u32[]{:S(2)}, u32[]{:S(2)}) collective-permute-start(f32[2,24,4,256]{3,2,1,0:T(4,128)S(1)} %get-tuple-element.22), channel_id=1, source_target_pairs={{1,0},{2,1},{3,2},{4,3},{5,4},{6,5},{7,6},{9,8},{10,9},{11,10},{12... | collective-permute-start | bytes 589832 | tf_op jit(solution)/shard_map/ppermute | solution.py:31
  62.4 9.4 %collective-permute-start.11 = (f32[2,24,4,256]{3,2,1,0:T(4,128)S(1)}, f32[2,24,4,256]{3,2,1,0:T(4,128)S(1)}, u32[]{:S(2)}, u32[]{:S(2)}) collective-permute-start(f32[2,24,4,256]{3,2,1,0:T(4,128)S(1)} %get-tuple-element.21), channel_id=1, source_target_pairs={{0,1},{1,2},{2,3},{3,4},{4,5},{5,6},{6,7},{8,9},{9,10},{10,11},{11... | collective-permute-start | bytes 589832 | tf_op jit(solution)/shard_map/ppermute | solution.py:28
  72.1 1.0 copy-start
  72.1 1.0 copy-start.1
  75.1 12.0 %collective-permute-start.12 = (f32[2,4,16,256]{3,2,1,0:T(8,128)S(1)}, f32[2,4,16,256]{3,2,1,0:T(8,128)S(1)}, u32[]{:S(2)}, u32[]{:S(2)}) collective-permute-start(f32[2,4,16,256]{3,2,1,0:T(8,128)S(1)} %get-tuple-element.29), channel_id=1, source_target_pairs={{8,0},{16,8},{24,16},{32,24},{40,32},{48,40},{56,48},{64,56},{72,6... | collective-permute-start | bytes 393224 | tf_op jit(solution)/shard_map/ppermute | solution.py:31
  77.0 15.3 %collective-permute-start.13 = (f32[2,4,16,256]{3,2,1,0:T(8,128)S(1)}, f32[2,4,16,256]{3,2,1,0:T(8,128)S(1)}, u32[]{:S(2)}, u32[]{:S(2)}) collective-permute-start(f32[2,4,16,256]{3,2,1,0:T(8,128)S(1)} %get-tuple-element.30), channel_id=1, source_target_pairs={{0,8},{8,16},{16,24},{24,32},{32,40},{40,48},{48,56},{56,64},{64,7... | collective-permute-start | bytes 393224 | tf_op jit(solution)/shard_map/ppermute | solution.py:28
  92.4 6.4 %collective-permute-start.14 = (f32[2,24,4,256]{3,2,1,0:T(4,128)S(1)}, f32[2,24,4,256]{3,2,1,0:T(4,128)S(1)}, u32[]{:S(2)}, u32[]{:S(2)}) collective-permute-start(f32[2,24,4,256]{3,2,1,0:T(4,128)S(1)} %get-tuple-element.18), channel_id=1, source_target_pairs={{1,0},{2,1},{3,2},{4,3},{5,4},{6,5},{7,6},{9,8},{10,9},{11,10},{12... | collective-permute-start | bytes 589832 | tf_op jit(solution)/shard_map/ppermute | solution.py:31
  93.7 6.6 %collective-permute-start.15 = (f32[2,24,4,256]{3,2,1,0:T(4,128)S(1)}, f32[2,24,4,256]{3,2,1,0:T(4,128)S(1)}, u32[]{:S(2)}, u32[]{:S(2)}) collective-permute-start(f32[2,24,4,256]{3,2,1,0:T(4,128)S(1)} %get-tuple-element.17), channel_id=1, source_target_pairs={{0,1},{1,2},{2,3},{3,4},{4,5},{5,6},{6,7},{8,9},{9,10},{10,11},{11... | collective-permute-start | bytes 589832 | tf_op jit(solution)/shard_map/ppermute | solution.py:28
  101.5 21.4 %copy-start.5 = (f32[16,16,256]{2,1,0:T(8,128)S(1)}, f32[16,16,256]{2,1,0:T(8,128)}, u32[]{:S(2)}) copy-start(f32[16,16,256]{2,1,0:T(8,128)} %param.12) | copy-start | bytes 786436
  103.0 10.6 %collective-permute-start.16 = (f32[2,4,16,256]{3,2,1,0:T(8,128)S(1)}, f32[2,4,16,256]{3,2,1,0:T(8,128)S(1)}, u32[]{:S(2)}, u32[]{:S(2)}) collective-permute-start(f32[2,4,16,256]{3,2,1,0:T(8,128)S(1)} %get-tuple-element.27), channel_id=1, source_target_pairs={{8,0},{16,8},{24,16},{32,24},{40,32},{48,40},{56,48},{64,56},{72,6... | collective-permute-start | bytes 393224 | tf_op jit(solution)/shard_map/ppermute | solution.py:31
  105.0 12.5 %collective-permute-start.17 = (f32[2,4,16,256]{3,2,1,0:T(8,128)S(1)}, f32[2,4,16,256]{3,2,1,0:T(8,128)S(1)}, u32[]{:S(2)}, u32[]{:S(2)}) collective-permute-start(f32[2,4,16,256]{3,2,1,0:T(8,128)S(1)} %get-tuple-element.28), channel_id=1, source_target_pairs={{0,8},{8,16},{16,24},{24,32},{32,40},{40,48},{48,56},{56,64},{64,7... | collective-permute-start | bytes 393224 | tf_op jit(solution)/shard_map/ppermute | solution.py:28
  117.6 7.3 %collective-permute-start.18 = (f32[2,24,4,256]{3,2,1,0:T(4,128)S(1)}, f32[2,24,4,256]{3,2,1,0:T(4,128)S(1)}, u32[]{:S(2)}, u32[]{:S(2)}) collective-permute-start(f32[2,24,4,256]{3,2,1,0:T(4,128)S(1)} %get-tuple-element.14), channel_id=1, source_target_pairs={{1,0},{2,1},{3,2},{4,3},{5,4},{6,5},{7,6},{9,8},{10,9},{11,10},{12... | collective-permute-start | bytes 589832 | tf_op jit(solution)/shard_map/ppermute | solution.py:31
  118.9 8.5 %collective-permute-start.19 = (f32[2,24,4,256]{3,2,1,0:T(4,128)S(1)}, f32[2,24,4,256]{3,2,1,0:T(4,128)S(1)}, u32[]{:S(2)}, u32[]{:S(2)}) collective-permute-start(f32[2,24,4,256]{3,2,1,0:T(4,128)S(1)} %get-tuple-element.13), channel_id=1, source_target_pairs={{0,1},{1,2},{2,3},{3,4},{4,5},{5,6},{6,7},{8,9},{9,10},{10,11},{11... | collective-permute-start | bytes 589832 | tf_op jit(solution)/shard_map/ppermute | solution.py:28
  122.9 12.0 %collective-permute-start = (f32[16,16,256]{2,1,0:T(8,128)S(1)}, f32[16,16,256]{2,1,0:T(8,128)S(1)}, u32[]{:S(2)}, u32[]{:S(2)}) collective-permute-start(f32[16,16,256]{2,1,0:T(8,128)S(1)} %copy-done.5), channel_id=1, source_target_pairs={{8,0},{16,8},{24,16},{32,24},{40,32},{48,40},{56,48},{64,56},{72,6... | collective-permute-start | bytes 786440 | tf_op jit(solution)/shard_map/ppermute | solution.py:20
  130.0 6.1 %copy-start.7 = (s32[1,32]{1,0:T(1,128)S(1)}, s32[1,32]{1,0:T(1,128)}, u32[]{:S(2)}) copy-start(s32[1,32]{1,0:T(1,128)} %param.19) | copy-start | bytes 388
  130.0 277.1 %copy-start.6 = (f32[16,16,256]{2,1,0:T(8,128)S(1)}, f32[16,16,256]{2,1,0:T(8,128)}, u32[]{:S(2)}) copy-start(f32[16,16,256]{2,1,0:T(8,128)} %param.17) | copy-start | bytes 786436
Sparse Core Ops, SparseCore 0:
  136.2 270.8 all-reduce.5
where the time goes:
time: 416 us
  waiting for transfers between devices  313 us (75%)
  starting transfers between devices  69.1 us (17%)
  other arithmetic  18.7 us (4%)
  between operations  14.5 us (3%)
    psum x1, waiting for transfers between devices, spread(): return lax.psum(jnp.where(mine, shard, jnp.zeros_like(shard)), axis)  271 us
    ppermute x8, starting transfers between devices, extended(): lax.ppermute(lax.slice_in_dim(block, block.shape[dim] - width, None, axis...  45.1 us
    ppermute x8, waiting for transfers between devices, extended(): lax.ppermute(lax.slice_in_dim(block, block.shape[dim] - width, None, axis...  22 us
    ppermute x8, starting transfers between devices, extended(): lax.ppermute(lax.slice_in_dim(block, 0, width, axis=dim), axis, backward)  13 us
    ppermute x4, starting transfers between devices, from_behind(): lax.ppermute(value, axis, [(source, source + steps) for source in range(i...  10.9 us
    ppermute x4, waiting for transfers between devices, from_behind(): lax.ppermute(value, axis, [(source, source + steps) for source in range(i...  10.2 us
    ppermute x8, waiting for transfers between devices, extended(): lax.ppermute(lax.slice_in_dim(block, 0, width, axis=dim), axis, backward)  9.99 us
  transfers between devices with their start and end apart: 21, of which 17 were waited for; matrix products, arithmetic and copies ran while one was open for 2% of the time, Pallas kernels for 0%

commit v1 on v0

v1 whole, which is shorter than its diff:
```python
import functools

import jax
import jax.numpy as jnp
from jax import lax
from jax.experimental import pallas as pl
from jax.experimental.pallas import tpu as pltpu
from jax.sharding import PartitionSpec as P

STEPS = 4
STENCIL = (-205.0 / 72.0, 8.0 / 5.0, -1.0 / 5.0, 8.0 / 315.0, -1.0 / 560.0)
F32 = jnp.float32
HIGHEST = lax.Precision.HIGHEST


def sds(*shape):
    return jax.ShapeDtypeStruct(shape, F32)


def call(kernel, outs, scratch, flops, *args):
    specs = [
        pl.BlockSpec(memory_space=pltpu.SMEM if a.ndim == 1 else pltpu.VMEM) for a in args
    ]
    return pl.pallas_call(
        kernel,
        out_shape=outs,
        in_specs=specs,
        out_specs=[pl.BlockSpec(memory_space=pltpu.VMEM)] * len(outs),
        scratch_shapes=scratch,
        compiler_params=pltpu.CompilerParams(vmem_limit_bytes=24 * 1024 * 1024),
        cost_estimate=pl.CostEstimate(flops=flops, bytes_accessed=1 << 20, transcendentals=0),
    )(*args)


def send_faces(here, fields, sends):
    x1, od, y1, yo = sends
    even_x, even_y = lax.rem(here[0], 2) == 0, lax.rem(here[1], 2) == 0
    toward = jnp.where(even_x, 12, 0)
    for f, field in enumerate(fields):
        x1[f] = field[pl.ds(toward, 4)]
        od[f] = field[pl.ds(12 - toward, 4)]
        for half in range(2):
            block = field[8 * half : 8 * half + 8]
            low, high = block[:, 0:4, :], block[:, 12:16, :]
            rows = slice(4 * half, 4 * half + 4)
            y1[f, :, rows, :] = jnp.where(even_y, high, low)
            yo[f, :, rows, :] = jnp.where(even_y, low, high)


def extend(here, field, halos, f, ext):
    x1, od, y1, yo = halos
    gx, gy = here[0], here[1]
    even_x, even_y = lax.rem(gx, 2) == 0, lax.rem(gy, 2) == 0
    zero = F32(0.0)
    ext[4:20, 8:24, :] = field[...]
    a, b = x1[f], od[f]
    ext[0:4, 8:24, :] = jnp.where(gx > 0, jnp.where(even_x, b, a), zero)
    ext[20:24, 8:24, :] = jnp.where(gx < 31, jnp.where(even_x, a, b), zero)
    a, b = y1[f], yo[f]
    low = jnp.where(gy > 0, jnp.where(even_y, b, a), zero)
    high = jnp.where(gy < 7, jnp.where(even_y, a, b), zero)
    for half in range(2):
        rows = slice(4 * half, 4 * half + 4)
        xs = slice(4 + 8 * half, 12 + 8 * half)
        ext[xs, 4:8, :] = low[:, rows, :]
        ext[xs, 24:28, :] = high[:, rows, :]


def depth_matrix():
    i = lax.broadcasted_iota(jnp.int32, (256, 256), 0)
    j = lax.broadcasted_iota(jnp.int32, (256, 256), 1)
    apart = jnp.abs(i - j)
    m = jnp.where(apart == 0, F32(3.0 * STENCIL[0]), F32(0.0))
    for k in range(1, 5):
        m = jnp.where(apart == k, F32(STENCIL[k]), m)
    return m


def advance(field, prev_of, vel, ext, depth, out):
    for x in range(0, 16, 2):
        lap = depth[x : x + 2]
        for k in range(1, 5):
            pair = ext[4 + x + k : 6 + x + k, 8:24, :] + ext[4 + x - k : 6 + x - k, 8:24, :]
            pair = pair + (ext[4 + x : 6 + x, 8 + k : 24 + k, :] + ext[4 + x : 6 + x, 8 - k : 24 - k, :])
            lap = lap + F32(STENCIL[k]) * pair
        out[x : x + 2] = 2.0 * field[x : x + 2] - prev_of(x) + vel[x : x + 2] * lap


def move_kernel(here, moves, s, r, s_in, r_in, s_out, r_out, *sends):
    arrives = here[0] < 31
    moved = moves[...] == 1
    for own, come, out in ((s, s_in, s_out), (r, r_in, r_out)):
        for x in range(0, 16, 2):
            out[x : x + 2] = jnp.where(
                moved[None], jnp.where(arrives, come[x : x + 2], F32(0.0)), own[x : x + 2]
            )
    send_faces(here, (s_out, r_out), sends)


def step_kernel(step, *refs):
    refs = list(refs)
    take = lambda n: [refs.pop(0) for _ in range(n)]
    (here,) = take(1)
    s, r = take(2)
    halos = take(4)
    if step == 0:
        moves, s_prev, r_prev, vel_own, vel_end, come = take(6)
    else:
        s_prev, r_prev, vel, picture = take(4)
    if step == STEPS - 1:
        moves, image, image_come = take(3)
    s_out, r_out, picture_out = take(3)
    if step < STEPS - 1:
        sends = take(4)
    if step == 0:
        (vel,) = take(1)
    ext_s, ext_r, depth_s, depth_r = take(4)

    if step in (0, STEPS - 1):
        moved = (moves[...] == 1)[None]
        arrives = here[0] < 31
    if step == 0:
        for x in range(0, 16, 2):
            new = jnp.where(arrives, come[2, x : x + 2], vel_end[x : x + 2])
            vel[x : x + 2] = jnp.where(moved, new, vel_own[x : x + 2])
    matrix = depth_matrix()
    for f, (field, prev, ext, depth, out) in enumerate(
        ((s, s_prev, ext_s, depth_s, s_out), (r, r_prev, ext_r, depth_r, r_out))
    ):
        extend(here, field, halos, f, ext)
        flat = field[...].reshape(256, 256)
        depth[...] = jnp.dot(
            flat, matrix, precision=HIGHEST, preferred_element_type=F32
        ).reshape(16, 16, 256)
        if step == 0:
            prev_of = lambda x, f=f, prev=prev: jnp.where(
                moved, jnp.where(arrives, come[f, x : x + 2], F32(0.0)), prev[x : x + 2]
            )
        else:
            prev_of = lambda x, prev=prev: prev[x : x + 2]
        advance(field, prev_of, vel, ext, depth, out)
    for x in range(0, 16, 2):
        product = s_out[x : x + 2] * r_out[x : x + 2]
        if step > 0:
            product = picture[x : x + 2] + product
        if step == STEPS - 1:
            product = product + jnp.where(
                moved, jnp.where(arrives, image_come[x : x + 2], F32(0.0)), image[x : x + 2]
            )
        picture_out[x : x + 2] = product
    if step < STEPS - 1:
        send_faces(here, (s_out, r_out), sends)


def scatter_kernel(moves, target, image, out):
    rows = lax.broadcasted_iota(jnp.int32, (256, 256), 0)
    pick = jnp.where(rows == target[0:1, :], F32(1.0), F32(0.0))
    leaving = jnp.where((moves[...] == 1)[None], image[...], F32(0.0)).reshape(256, 256)
    out[...] = lax.dot_general(
        pick, leaving, (((1,), (1,)), ((), ())), precision=HIGHEST, preferred_element_type=F32
    )


def gather_kernel(slab, source, base, out):
    rows = lax.broadcasted_iota(jnp.int32, (8, 256), 0)
    place = jnp.where(rows == source[...], F32(1.0), F32(0.0))
    out[...] = base[...] + lax.dot_general(
        slab[...], place, (((0,), (0,)), ((), ())), precision=HIGHEST, preferred_element_type=F32
    ).reshape(16, 16, 256)


def body(
    courant,
    vel_entering,
    image,
    src_prev,
    src_cur,
    rcv_prev,
    rcv_cur,
    global_image,
    shift_map,
    image_owner,
):
    gx, gy = lax.axis_index("gx"), lax.axis_index("gy")
    here = jnp.stack([gx, gy]).astype(jnp.int32)
    n, m = 32, 8
    west = [(i, (i - 1) % n) for i in range(n)]
    pair_x = [(i, i ^ 1) for i in range(n)]
    odd_x = [(i, (i + (1 if i % 2 else -1)) % n) for i in range(n)]
    pair_y = [(i, i ^ 1) for i in range(m)]
    odd_y = [(i, (i + (1 if i % 2 else -1)) % m) for i in range(m)]

    def swap(x1, od, y1, yo):
        x1 = lax.ppermute(x1, "gx", pair_x)
        od = lax.ppermute(od, "gx", odd_x)
        yo = lax.ppermute(yo, "gy", odd_y)
        y1 = lax.ppermute(y1, "gy", pair_y)
        return x1, od, y1, yo

    moves = jnp.broadcast_to(shift_map[:, None], (16, 256))
    z = jnp.arange(256, dtype=jnp.int32)
    owner = jnp.repeat(image_owner[0], 8)
    target = jnp.broadcast_to((owner * 8 + z % 8)[None], (8, 256))
    source = jnp.broadcast_to(jnp.where(owner == gx, z % 8, -1)[None], (8, 256))

    s_come = lax.ppermute(src_cur, "gx", west)
    r_come = lax.ppermute(rcv_cur, "gx", west)
    come = lax.ppermute(jnp.stack([src_prev, rcv_prev, courant]), "gx", west)
    image_come = lax.ppermute(image, "gx", west)

    (slabs,) = call(scatter_kernel, [sds(256, 256)], [], 1 << 24, moves, target, image)
    for reach in (16, 8, 4, 2, 1):
        if reach > 1:
            pairs = [(i, i + reach) for i in range(0, n, 2 * reach)]
            got = lax.ppermute(slabs[8 * reach :], "gx", pairs)
            slabs = jnp.where(lax.rem(gx, 2 * reach) == 0, slabs[: 8 * reach], got)
        else:
            got = lax.ppermute(slabs[8:], "gx", pair_x)
            slabs = jnp.where(lax.rem(gx, 2) == 0, slabs[:8], got)
    (global_out,) = call(
        gather_kernel, [sds(16, 16, 256)], [], 1 << 22, slabs, source, global_image
    )

    tile = sds(16, 16, 256)
    faces = [sds(2, 4, 16, 256), sds(2, 4, 16, 256), sds(2, 8, 8, 256), sds(2, 8, 8, 256)]
    scratch = [pltpu.VMEM((24, 32, 256), F32)] * 2 + [pltpu.VMEM((16, 16, 256), F32)] * 2
    s, r, *sends = call(
        move_kernel, [tile, tile] + faces, [], 1 << 20, here, moves, src_cur, rcv_cur, s_come, r_come
    )
    for step in range(STEPS):
        halos = swap(*sends)
        ins = [here, s, r, *halos]
        outs = [tile, tile, tile]
        if step == 0:
            ins += [moves, src_prev, rcv_prev, courant, vel_entering, come]
        else:
            ins += [s_old, r_old, velocity, picture]
        if step == STEPS - 1:
            ins += [moves, image, image_come]
        else:
            outs = outs + faces
        if step == 0:
            outs = outs + [tile]
        got = call(functools.partial(step_kernel, step), outs, scratch, 1 << 25, *ins)
        s_old, r_old = s, r
        s, r, picture, *sends = got
        if step == 0:
            velocity = sends.pop()
    return (global_out, picture, s_old, s, r_old, r)


def solution(mesh):
    tiled = P("gx", "gy", None)
    in_specs = (
        tiled,
        P(None, "gy", None),
        tiled,
        tiled,
        tiled,
        tiled,
        tiled,
        tiled,
        P("gy"),
        P("gy", None),
    )
    return jax.shard_map(
        body, mesh=mesh, in_specs=in_specs, out_specs=(tiled,) * 6, check_vma=False
    )
```

time: 416 us -> 94.3 us (0.23)
  waiting for transfers between devices: 313 us -> 33 us
  starting transfers between devices: 69.1 us -> 41.5 us
  other arithmetic: 18.7 us -> 1.76 us
  Pallas kernels: 0 us -> 14.2 us
  between operations: 14.5 us -> 0.88 us
    psum x1 -> x0, waiting for transfers between devices: 271 us -> none  [spread(): return lax.psum(jnp.where(mine, shard, jnp.zeros_like(shard)), axis)]
    ppermute x20 -> x25, starting transfers between devices: 69 us -> 41.5 us  [the longest x4 10.9 us: swap(): x1 = lax.ppermute(x1, 'gx', pair_x)]
    pallas_call x0 -> x7, Pallas kernels: none -> 14.2 us  [call(): pl.pallas_call(kernel, out_shape=outs, in_specs=specs, out_specs=[pl.Bloc...]
    add x6 -> x1, other arithmetic: 9.88 us -> 0.01 us  [body(): target = jnp.broadcast_to((owner * 8 + z % 8)[None], (8, 256))]
    ppermute x20 -> x25, waiting for transfers between devices: 42.1 us -> 33 us  [the longest x4 19.2 us: swap(): od = lax.ppermute(od, 'gx', odd_x)]
    concatenate x12 -> x0, other arithmetic: 4.82 us -> none  [extended(): block = jnp.concatenate([low, block, high], axis=dim)]
  transfers between devices with their start and end apart: 21 -> 25, of which waited for: 17 -> 8; matrix products, arithmetic and copies ran while one was open for 2% -> 1% of each run, Pallas kernels for 0% -> 12%
where the time goes in v1:
time: 94.3 us; the launch traced here: 93.7 us
  starting transfers between devices  41.5 us (44%)
  waiting for transfers between devices  33 us (35%)
  Pallas kernels  14.2 us (15%)
  local copies, waits for them, and re-layouts  2.31 us (2%)
  other arithmetic  1.76 us (2%)
    ppermute x4, waiting for transfers between devices, swap(): od = lax.ppermute(od, 'gx', odd_x)  19.2 us
    pallas_call x7, Pallas kernels, call(): pl.pallas_call(kernel, out_shape=outs, in_specs=specs, out_specs=[pl.Bloc...  14.2 us
    ppermute x4, starting transfers between devices, swap(): x1 = lax.ppermute(x1, 'gx', pair_x)  10.9 us
    ppermute x1, starting transfers between devices, body(): come = lax.ppermute(jnp.stack([src_prev, rcv_prev, courant]), 'gx', west)  9.82 us
    ppermute x4, starting transfers between devices, swap(): yo = lax.ppermute(yo, 'gy', odd_y)  8.47 us
    ppermute x4, waiting for transfers between devices, swap(): y1 = lax.ppermute(y1, 'gy', pair_y)  6.25 us
    ppermute x1, waiting for transfers between devices, body(): s_come = lax.ppermute(src_cur, 'gx', west)  4.44 us
    ppermute x1, starting transfers between devices, body(): image_come = lax.ppermute(image, 'gx', west)  3.77 us
  transfers between devices with their start and end apart: 25, of which 8 were waited for; matrix products, arithmetic and copies ran while one was open for 1% of the time, Pallas kernels for 12%

profile of v1, /device:TPU:1, one launch (start us, length us, event | category | flops | bytes accessed | tf_op | source)
XLA Modules:
  0.0 93.7 jit_solution(15998659072694276241)
XLA Ops:
  0.6 0.7 multiply_bitcast_fusion
  1.3 0.1 broadcast_in_dim.28
  1.4 0.1 mul.22
  1.5 0.0 copy-start.11
  1.5 0.6 copy-done.11
  2.1 0.1 broadcast_in_dim.14.moves.refs_7_.refs_11_
  2.2 0.9 %copy-done = f32[16,16,256]{2,1,0:T(8,128)S(1)} copy-done((f32[16,16,256]{2,1,0:T(8,128)S(1)}, f32[16,16,256]{2,1,0:T(8,128)}, u32[]{:S(2)}) %copy-start) | copy-done | bytes 262168
  3.1 0.4 shard_map.145
  3.6 0.0 copy-start.2
  3.6 0.8 collective-permute-start
  4.4 0.1 copy-done.2
  4.6 1.0 %pad_maximum_fusion = f32[3,16,16,256]{3,2,1,0:T(8,128)} fusion(f32[1,16,16,256]{3,2,1,0:T(8,128)S(1)} %bitcast.11, f32[1,16,16,256]{3,2,1,0:T(8,128)S(1)} %bitcast.10, f32[1,16,16,256]{3,2,1,0:T(8,128)S(1)} %bitcast.9), kind=kLoop, calls=%fused_computation | loop fusion | flops 393216 | bytes 1572864 | tf_op jit(solution)/shard_map/stack | solution.py:208
  5.5 9.8 %collective-permute-start.11 = (f32[3,16,16,256]{3,2,1,0:T(8,128)}, f32[3,16,16,256]{3,2,1,0:T(8,128)S(1)}, u32[]{:S(2)}, u32[]{:S(2)}) collective-permute-start(f32[3,16,16,256]{3,2,1,0:T(8,128)} %pad_maximum_fusion), channel_id=1, source_target_pairs={{0,248},{8,0},{16,8},{24,16},{32,24},{40,32},{48,40},{56,48},{64,5... | collective-permute-start | bytes 2359304 | tf_op jit(solution)/shard_map/ppermute | solution.py:208
  15.3 0.0 collective-permute-done
  15.4 0.8 collective-permute-start.1
  16.2 0.1 copy-done.9
  16.3 2.0 %collective-permute-start.5 = (f32[16,16,256]{2,1,0:T(8,128)S(1)}, f32[16,16,256]{2,1,0:T(8,128)S(1)}, u32[]{:S(2)}, u32[]{:S(2)}) collective-permute-start(f32[16,16,256]{2,1,0:T(8,128)S(1)} %copy-done.9), channel_id=1, source_target_pairs={{0,248},{8,0},{16,8},{24,16},{32,24},{40,32},{48,40},{56,48},{64,5... | collective-permute-start | bytes 786440 | tf_op jit(solution)/shard_map/ppermute | solution.py:206
  18.3 0.1 collective-permute-start.6
  18.4 0.0 collective-permute-done.1
  18.4 0.7 collective-permute-start.2
  19.1 0.1 pad_add_fusion.here.refs_0_
  19.1 4.4 %collective-permute-done.5.s_in = f32[16,16,256]{2,1,0:T(8,128)S(1)} collective-permute-done((f32[16,16,256]{2,1,0:T(8,128)S(1)}, f32[16,16,256]{2,1,0:T(8,128)S(1)}, u32[]{:S(2)}, u32[]{:S(2)}) %collective-permute-start.5) | collective-permute-done | bytes 262176 | tf_op jit(solution)/shard_map/ppermute | solution.py:206
  23.6 2.8 %collective-permute-done.6.r_in = f32[16,16,256]{2,1,0:T(8,128)S(1)} collective-permute-done((f32[16,16,256]{2,1,0:T(8,128)S(1)}, f32[16,16,256]{2,1,0:T(8,128)S(1)}, u32[]{:S(2)}, u32[]{:S(2)}) %collective-permute-start.6) | collective-permute-done | bytes 262176 | tf_op jit(solution)/shard_map/ppermute | solution.py:207
  26.4 0.7 shard_map.147
  27.1 3.6 %collective-permute-start.10 = (f32[2,8,8,256]{3,2,1,0:T(8,128)S(1)}, f32[2,8,8,256]{3,2,1,0:T(8,128)S(1)}, u32[]{:S(2)}, u32[]{:S(2)}) collective-permute-start(f32[2,8,8,256]{3,2,1,0:T(8,128)S(1)} %get-tuple-element.42), channel_id=1, source_target_pairs={{0,7},{1,2},{2,1},{3,4},{4,3},{5,6},{6,5},{7,0},{8,15},{9,10},{10,... | collective-permute-start | bytes 393224 | tf_op jit(solution)/shard_map/ppermute | solution.py:196
  30.7 4.6 %collective-permute-start.7 = (f32[2,4,16,256]{3,2,1,0:T(8,128)S(1)}, f32[2,4,16,256]{3,2,1,0:T(8,128)S(1)}, u32[]{:S(2)}, u32[]{:S(2)}) collective-permute-start(f32[2,4,16,256]{3,2,1,0:T(8,128)S(1)} %get-tuple-element.39), channel_id=1, source_target_pairs={{0,8},{8,0},{16,24},{24,16},{32,40},{40,32},{48,56},{56,48},{64,72... | collective-permute-start | bytes 393224 | tf_op jit(solution)/shard_map/ppermute | solution.py:194
  35.2 0.0 collective-permute-done.2
  35.2 0.0 collective-permute-start.9
  35.3 0.7 collective-permute-start.3
  36.0 0.3 collective-permute-done.7.refs_3_
  36.2 4.9 %collective-permute-done.8.refs_4_ = f32[2,4,16,256]{3,2,1,0:T(8,128)S(1)} collective-permute-done((f32[2,4,16,256]{3,2,1,0:T(8,128)S(1)}, f32[2,4,16,256]{3,2,1,0:T(8,128)S(1)}, u32[]{:S(2)}, u32[]{:S(2)}) %collective-permute-start.8) | collective-permute-done | bytes 131104 | tf_op jit(solution)/shard_map/ppermute | solution.py:195
  41.1 0.0 collective-permute-done.9.refs_5_
  41.1 0.0 collective-permute-done.11.refs_12_
  41.2 0.0 copy-start.1
  41.2 3.1 %shard_map.148 = (f32[16,16,256]{2,1,0:T(8,128)S(1)}, f32[16,16,256]{2,1,0:T(8,128)S(1)}, f32[16,16,256]{2,1,0:T(8,128)S(1)}, f32[2,4,16,256]{3,2,1,0:T(8,128)},...) custom-call(s32[2]{0:T(128)S(1)} %pad_add_fusion.here.refs_0_, ...), custom_call_target="tpu_custom_call" | custom-call | flops 33554432 | bytes 1048576 | tf_op jit(solution)/shard_map/pallas_call | solution.py:24
  44.2 4.9 %collective-permute-start.12 = (f32[2,4,16,256]{3,2,1,0:T(8,128)}, f32[2,4,16,256]{3,2,1,0:T(8,128)S(1)}, u32[]{:S(2)}, u32[]{:S(2)}) collective-permute-start(f32[2,4,16,256]{3,2,1,0:T(8,128)} %get-tuple-element.45), channel_id=1, source_target_pairs={{0,8},{8,0},{16,24},{24,16},{32,40},{40,32},{48,56},{56,48},{64,72... | collective-permute-start | bytes 393224 | tf_op jit(solution)/shard_map/ppermute | solution.py:194
  49.1 1.7 %collective-permute-start.15 = (f32[2,8,8,256]{3,2,1,0:T(8,128)}, f32[2,8,8,256]{3,2,1,0:T(8,128)S(1)}, u32[]{:S(2)}, u32[]{:S(2)}) collective-permute-start(f32[2,8,8,256]{3,2,1,0:T(8,128)} %get-tuple-element.48), channel_id=1, source_target_pairs={{0,7},{1,2},{2,1},{3,4},{4,3},{5,6},{6,5},{7,0},{8,15},{9,10},{10,... | collective-permute-start | bytes 393224 | tf_op jit(solution)/shard_map/ppermute | solution.py:196
  50.9 0.1 broadcast_in_dim.30
  51.0 0.1 eq.43
  51.1 3.8 %collective-permute-start.24 = (f32[16,16,256]{2,1,0:T(8,128)S(1)}, f32[16,16,256]{2,1,0:T(8,128)S(1)}, u32[]{:S(2)}, u32[]{:S(2)}) collective-permute-start(f32[16,16,256]{2,1,0:T(8,128)S(1)} %copy-done.1), channel_id=1, source_target_pairs={{0,248},{8,0},{16,8},{24,16},{32,24},{40,32},{48,40},{56,48},{64,5... | collective-permute-start | bytes 786440 | tf_op jit(solution)/shard_map/ppermute | solution.py:209
  54.8 0.4 collective-permute-done.13.refs_4_
  55.2 6.2 %collective-permute-done.14.refs_5_ = f32[2,8,8,256]{3,2,1,0:T(8,128)S(1)} collective-permute-done((f32[2,8,8,256]{3,2,1,0:T(8,128)}, f32[2,8,8,256]{3,2,1,0:T(8,128)S(1)}, u32[]{:S(2)}, u32[]{:S(2)}) %collective-permute-start.14) | collective-permute-done | bytes 131104 | tf_op jit(solution)/shard_map/ppermute | solution.py:197
  61.5 0.0 collective-permute-done.15.refs_6_
  61.5 2.9 %shard_map.149 = (f32[16,16,256]{2,1,0:T(8,128)S(1)}, f32[16,16,256]{2,1,0:T(8,128)S(1)}, f32[16,16,256]{2,1,0:T(8,128)S(1)}, f32[2,4,16,256]{3,2,1,0:T(8,128)S(...) custom-call(s32[2]{0:T(128)S(1)} %pad_add_fusion.here.refs_0_, ...), custom_call_target="tpu_custom_call" | custom-call | flops 33554432 | bytes 1048576 | tf_op jit(solution)/shard_map/pallas_call | solution.py:24
  64.4 0.4 collective-permute-start.16
  64.8 0.2 collective-permute-start.4
  65.0 0.3 collective-permute-start.17
  65.3 1.2 %collective-permute-start.18 = (f32[2,8,8,256]{3,2,1,0:T(8,128)}, f32[2,8,8,256]{3,2,1,0:T(8,128)S(1)}, u32[]{:S(2)}, u32[]{:S(2)}) collective-permute-start(f32[2,8,8,256]{3,2,1,0:T(8,128)} %get-tuple-element.55), channel_id=1, source_target_pairs={{0,1},{1,0},{2,3},{3,2},{4,5},{5,4},{6,7},{7,6},{8,9},{9,8},{10,11... | collective-permute-start | bytes 393224 | tf_op jit(solution)/shard_map/ppermute | solution.py:197
  66.5 0.0 collective-permute-done.16.refs_3_
  66.5 1.4 %collective-permute-start.19 = (f32[2,8,8,256]{3,2,1,0:T(8,128)}, f32[2,8,8,256]{3,2,1,0:T(8,128)S(1)}, u32[]{:S(2)}, u32[]{:S(2)}) collective-permute-start(f32[2,8,8,256]{3,2,1,0:T(8,128)} %get-tuple-element.56), channel_id=1, source_target_pairs={{0,7},{1,2},{2,1},{3,4},{4,3},{5,6},{6,5},{7,0},{8,15},{9,10},{10,... | collective-permute-start | bytes 393224 | tf_op jit(solution)/shard_map/ppermute | solution.py:196
  67.9 8.5 %collective-permute-done.17.refs_4_ = f32[2,4,16,256]{3,2,1,0:T(8,128)S(1)} collective-permute-done((f32[2,4,16,256]{3,2,1,0:T(8,128)}, f32[2,4,16,256]{3,2,1,0:T(8,128)S(1)}, u32[]{:S(2)}, u32[]{:S(2)}) %collective-permute-start.17) | collective-permute-done | bytes 131104 | tf_op jit(solution)/shard_map/ppermute | solution.py:195
  76.4 0.0 collective-permute-done.18.refs_5_
  76.4 0.0 collective-permute-done.19.refs_6_
  76.4 3.0 %shard_map.150 = (f32[16,16,256]{2,1,0:T(8,128)}, f32[16,16,256]{2,1,0:T(8,128)}, f32[16,16,256]{2,1,0:T(8,128)S(1)}, f32[2,4,16,256]{3,2,1,0:T(8,128)S(1)}, f32...) custom-call(s32[2]{0:T(128)S(1)} %pad_add_fusion.here.refs_0_, ...), custom_call_target="tpu_custom_call" | custom-call | flops 33554432 | bytes 1048576 | tf_op jit(solution)/shard_map/pallas_call | solution.py:24
  79.4 1.0 %collective-permute-start.20 = (f32[2,4,16,256]{3,2,1,0:T(8,128)S(1)}, f32[2,4,16,256]{3,2,1,0:T(8,128)S(1)}, u32[]{:S(2)}, u32[]{:S(2)}) collective-permute-start(f32[2,4,16,256]{3,2,1,0:T(8,128)S(1)} %get-tuple-element.60), channel_id=1, source_target_pairs={{0,8},{8,0},{16,24},{24,16},{32,40},{40,32},{48,56},{56,48},{64,72... | collective-permute-start | bytes 393224 | tf_op jit(solution)/shard_map/ppermute | solution.py:194
  80.4 1.9 %collective-permute-start.21 = (f32[2,4,16,256]{3,2,1,0:T(8,128)S(1)}, f32[2,4,16,256]{3,2,1,0:T(8,128)S(1)}, u32[]{:S(2)}, u32[]{:S(2)}) collective-permute-start(f32[2,4,16,256]{3,2,1,0:T(8,128)S(1)} %get-tuple-element.61), channel_id=1, source_target_pairs={{0,248},{8,16},{16,8},{24,32},{32,24},{40,48},{48,40},{56,64},{64,... | collective-permute-start | bytes 393224 | tf_op jit(solution)/shard_map/ppermute | solution.py:195
  82.3 1.8 %collective-permute-start.23 = (f32[2,8,8,256]{3,2,1,0:T(8,128)S(1)}, f32[2,8,8,256]{3,2,1,0:T(8,128)S(1)}, u32[]{:S(2)}, u32[]{:S(2)}) collective-permute-start(f32[2,8,8,256]{3,2,1,0:T(8,128)S(1)} %get-tuple-element.63), channel_id=1, source_target_pairs={{0,7},{1,2},{2,1},{3,4},{4,3},{5,6},{6,5},{7,0},{8,15},{9,10},{10,... | collective-permute-start | bytes 393224 | tf_op jit(solution)/shard_map/ppermute | solution.py:196
  84.1 0.0 copy-start.6
  84.1 0.0 copy-start.7
  84.1 1.1 %shard_map.146 = f32[16,16,256]{2,1,0:T(8,128)} custom-call(f32[8,256]{1,0:T(8,128)S(1)} %slice_select_fusion.4.slab, s32[8,256]{1,0:T(8,128)S(1)} %broadcast_in_dim.32.source, f32[16,16,256]{2,1,0:T(8,128)S(1)} %copy-done.8), custom_call_target="tpu_custom_call" | custom-call | flops 4194304 | bytes 1048576 | tf_op jit(solution)/shard_map/pallas_call | solution.py:24
  85.3 0.0 collective-permute-done.24.refs_13_
  85.3 0.0 collective-permute-done.20.refs_3_
  85.3 5.4 %collective-permute-done.21.refs_4_ = f32[2,4,16,256]{3,2,1,0:T(8,128)S(1)} collective-permute-done((f32[2,4,16,256]{3,2,1,0:T(8,128)S(1)}, f32[2,4,16,256]{3,2,1,0:T(8,128)S(1)}, u32[]{:S(2)}, u32[]{:S(2)}) %collective-permute-start.21) | collective-permute-done | bytes 131104 | tf_op jit(solution)/shard_map/ppermute | solution.py:195
  90.6 3.0 %shard_map.151 = (f32[16,16,256]{2,1,0:T(8,128)}, f32[16,16,256]{2,1,0:T(8,128)}, f32[16,16,256]{2,1,0:T(8,128)}) custom-call(s32[2]{0:T(128)S(1)} %pad_add_fusion.here.refs_0_, f32[16,16,256]{2,1,0:T(8,128)S(1)} %copy-done.6, f32[16,16,256]{2,1,0:T(8,128)S(1)} %copy-done.7, f32[2,4,16,256]{3,2,1,0:T(8,128)S(1)} %collective-permute-done.20.refs_3_, ...), custom_call_target="tpu_custom_call" | custom-call | flops 33554432 | bytes 1048576 | tf_op jit(solution)/shard_map/pallas_call | solution.py:24
  (42 shorter events, 0.1 us)
Async XLA Ops:
  1.5 0.7 copy-start.11
  2.2 1.0 %copy-start = (f32[16,16,256]{2,1,0:T(8,128)S(1)}, f32[16,16,256]{2,1,0:T(8,128)}, u32[]{:S(2)}) copy-start(f32[16,16,256]{2,1,0:T(8,128)} %refs_12_.1) | copy-start | bytes 786436
  3.1 1.3 %copy-start.3 = (f32[16,16,256]{2,1,0:T(8,128)S(1)}, f32[16,16,256]{2,1,0:T(8,128)}, u32[]{:S(2)}) copy-start(f32[16,16,256]{2,1,0:T(8,128)} %refs_9_.1) | copy-start | bytes 786436
  3.1 1.3 %copy-start.4 = (f32[16,16,256]{2,1,0:T(8,128)S(1)}, f32[16,16,256]{2,1,0:T(8,128)}, u32[]{:S(2)}) copy-start(f32[16,16,256]{2,1,0:T(8,128)} %refs_10_.1) | copy-start | bytes 786436
  3.6 1.0 %copy-start.2 = (f32[16,16,256]{2,1,0:T(8,128)S(1)}, f32[16,16,256]{2,1,0:T(8,128)}, u32[]{:S(2)}) copy-start(f32[16,16,256]{2,1,0:T(8,128)} %refs_8_.1) | copy-start | bytes 786436
  3.6 11.7 %collective-permute-start = (f32[128,256]{1,0:T(8,128)S(1)}, f32[128,256]{1,0:T(8,128)S(1)}, u32[]{:S(2)}, u32[]{:S(2)}) collective-permute-start(f32[128,256]{1,0:T(8,128)S(1)} %slice.41), channel_id=1, source_target_pairs={{0,128},{1,129},{2,130},{3,131},{4,132},{5,133},{6,134},{7,135}} | collective-permute-start | bytes 393224 | tf_op jit(solution)/shard_map/ppermute | solution.py:215
  5.5 35.6 %collective-permute-start.11 = (f32[3,16,16,256]{3,2,1,0:T(8,128)}, f32[3,16,16,256]{3,2,1,0:T(8,128)S(1)}, u32[]{:S(2)}, u32[]{:S(2)}) collective-permute-start(f32[3,16,16,256]{3,2,1,0:T(8,128)} %pad_maximum_fusion), channel_id=1, source_target_pairs={{0,248},{8,0},{16,8},{24,16},{32,24},{40,32},{48,40},{56,48},{64,5... | collective-permute-start | bytes 2359304 | tf_op jit(solution)/shard_map/ppermute | solution.py:208
  15.3 0.9 %copy-start.9 = (f32[16,16,256]{2,1,0:T(8,128)S(1)}, f32[16,16,256]{2,1,0:T(8,128)}, u32[]{:S(2)}) copy-start(f32[16,16,256]{2,1,0:T(8,128)} %s.1) | copy-start | bytes 786436
  15.3 2.9 %copy-start.10 = (f32[16,16,256]{2,1,0:T(8,128)S(1)}, f32[16,16,256]{2,1,0:T(8,128)}, u32[]{:S(2)}) copy-start(f32[16,16,256]{2,1,0:T(8,128)} %r.1) | copy-start | bytes 786436
  15.4 3.0 %collective-permute-start.1 = (f32[64,256]{1,0:T(8,128)S(1)}, f32[64,256]{1,0:T(8,128)S(1)}, u32[]{:S(2)}, u32[]{:S(2)}) collective-permute-start(f32[64,256]{1,0:T(8,128)S(1)} %slice.43), channel_id=1, source_target_pairs={{0,64},{128,192},{1,65},{129,193},{2,66},{130,194},{3,67},{131,195... | collective-permute-start | bytes 196616 | tf_op jit(solution)/shard_map/ppermute | solution.py:215
  16.3 7.3 %collective-permute-start.5 = (f32[16,16,256]{2,1,0:T(8,128)S(1)}, f32[16,16,256]{2,1,0:T(8,128)S(1)}, u32[]{:S(2)}, u32[]{:S(2)}) collective-permute-start(f32[16,16,256]{2,1,0:T(8,128)S(1)} %copy-done.9), channel_id=1, source_target_pairs={{0,248},{8,0},{16,8},{24,16},{32,24},{40,32},{48,40},{56,48},{64,5... | collective-permute-start | bytes 786440 | tf_op jit(solution)/shard_map/ppermute | solution.py:206
  18.3 8.1 %collective-permute-start.6 = (f32[16,16,256]{2,1,0:T(8,128)S(1)}, f32[16,16,256]{2,1,0:T(8,128)S(1)}, u32[]{:S(2)}, u32[]{:S(2)}) collective-permute-start(f32[16,16,256]{2,1,0:T(8,128)S(1)} %copy-done.10), channel_id=1, source_target_pairs={{0,248},{8,0},{16,8},{24,16},{32,24},{40,32},{48,40},{56,48},{64,5... | collective-permute-start | bytes 786440 | tf_op jit(solution)/shard_map/ppermute | solution.py:207
  18.4 16.9 %collective-permute-start.2 = (f32[32,256]{1,0:T(8,128)S(1)}, f32[32,256]{1,0:T(8,128)S(1)}, u32[]{:S(2)}, u32[]{:S(2)}) collective-permute-start(f32[32,256]{1,0:T(8,128)S(1)} %slice.45), channel_id=1, source_target_pairs={{0,32},{64,96},{128,160},{192,224},{1,33},{65,97},{129,161},{193,2... | collective-permute-start | bytes 98312 | tf_op jit(solution)/shard_map/ppermute | solution.py:215
  26.4 14.8 %copy-start.5 = (f32[16,16,256]{2,1,0:T(8,128)S(1)}, f32[16,16,256]{2,1,0:T(8,128)}, u32[]{:S(2)}) copy-start(f32[16,16,256]{2,1,0:T(8,128)} %refs_11_.1) | copy-start | bytes 786436
  27.1 8.2 %collective-permute-start.10 = (f32[2,8,8,256]{3,2,1,0:T(8,128)S(1)}, f32[2,8,8,256]{3,2,1,0:T(8,128)S(1)}, u32[]{:S(2)}, u32[]{:S(2)}) collective-permute-start(f32[2,8,8,256]{3,2,1,0:T(8,128)S(1)} %get-tuple-element.42), channel_id=1, source_target_pairs={{0,7},{1,2},{2,1},{3,4},{4,3},{5,6},{6,5},{7,0},{8,15},{9,10},{10,... | collective-permute-start | bytes 393224 | tf_op jit(solution)/shard_map/ppermute | solution.py:196
  30.7 5.5 %collective-permute-start.7 = (f32[2,4,16,256]{3,2,1,0:T(8,128)S(1)}, f32[2,4,16,256]{3,2,1,0:T(8,128)S(1)}, u32[]{:S(2)}, u32[]{:S(2)}) collective-permute-start(f32[2,4,16,256]{3,2,1,0:T(8,128)S(1)} %get-tuple-element.39), channel_id=1, source_target_pairs={{0,8},{8,0},{16,24},{24,16},{32,40},{40,32},{48,56},{56,48},{64,72... | collective-permute-start | bytes 393224 | tf_op jit(solution)/shard_map/ppermute | solution.py:194
  35.2 5.9 %collective-permute-start.8 = (f32[2,4,16,256]{3,2,1,0:T(8,128)S(1)}, f32[2,4,16,256]{3,2,1,0:T(8,128)S(1)}, u32[]{:S(2)}, u32[]{:S(2)}) collective-permute-start(f32[2,4,16,256]{3,2,1,0:T(8,128)S(1)} %get-tuple-element.40), channel_id=1, source_target_pairs={{0,248},{8,16},{16,8},{24,32},{32,24},{40,48},{48,40},{56,64},{64,... | collective-permute-start | bytes 393224 | tf_op jit(solution)/shard_map/ppermute | solution.py:195
  35.2 5.9 %collective-permute-start.9 = (f32[2,8,8,256]{3,2,1,0:T(8,128)S(1)}, f32[2,8,8,256]{3,2,1,0:T(8,128)S(1)}, u32[]{:S(2)}, u32[]{:S(2)}) collective-permute-start(f32[2,8,8,256]{3,2,1,0:T(8,128)S(1)} %get-tuple-element.41), channel_id=1, source_target_pairs={{0,1},{1,0},{2,3},{3,2},{4,5},{5,4},{6,7},{7,6},{8,9},{9,8},{10,11... | collective-permute-start | bytes 393224 | tf_op jit(solution)/shard_map/ppermute | solution.py:197
  35.3 29.5 %collective-permute-start.3 = (f32[16,256]{1,0:T(8,128)S(1)}, f32[16,256]{1,0:T(8,128)S(1)}, u32[]{:S(2)}, u32[]{:S(2)}) collective-permute-start(f32[16,256]{1,0:T(8,128)S(1)} %slice.47), channel_id=1, source_target_pairs={{0,16},{32,48},{64,80},{96,112},{128,144},{160,176},{192,208},{224... | collective-permute-start | bytes 49160 | tf_op jit(solution)/shard_map/ppermute | solution.py:215
  41.2 9.9 %copy-start.1 = (f32[16,16,256]{2,1,0:T(8,128)S(1)}, f32[16,16,256]{2,1,0:T(8,128)}, u32[]{:S(2)}) copy-start(f32[16,16,256]{2,1,0:T(8,128)} %refs_12_.1) | copy-start | bytes 786436
  44.2 6.8 %collective-permute-start.12 = (f32[2,4,16,256]{3,2,1,0:T(8,128)}, f32[2,4,16,256]{3,2,1,0:T(8,128)S(1)}, u32[]{:S(2)}, u32[]{:S(2)}) collective-permute-start(f32[2,4,16,256]{3,2,1,0:T(8,128)} %get-tuple-element.45), channel_id=1, source_target_pairs={{0,8},{8,0},{16,24},{24,16},{32,40},{40,32},{48,56},{56,48},{64,72... | collective-permute-start | bytes 393224 | tf_op jit(solution)/shard_map/ppermute | solution.py:194
  49.1 6.1 %collective-permute-start.13 = (f32[2,4,16,256]{3,2,1,0:T(8,128)}, f32[2,4,16,256]{3,2,1,0:T(8,128)S(1)}, u32[]{:S(2)}, u32[]{:S(2)}) collective-permute-start(f32[2,4,16,256]{3,2,1,0:T(8,128)} %get-tuple-element.46), channel_id=1, source_target_pairs={{0,248},{8,16},{16,8},{24,32},{32,24},{40,48},{48,40},{56,64},{64,... | collective-permute-start | bytes 393224 | tf_op jit(solution)/shard_map/ppermute | solution.py:195
  49.1 1.7 %copy-start.12 = (s32[1,32]{1,0:T(1,128)S(1)}, s32[1,32]{1,0:T(1,128)}, u32[]{:S(2)}) copy-start(s32[1,32]{1,0:T(1,128)} %param.19) | copy-start | bytes 388
  49.1 12.3 %collective-permute-start.14 = (f32[2,8,8,256]{3,2,1,0:T(8,128)}, f32[2,8,8,256]{3,2,1,0:T(8,128)S(1)}, u32[]{:S(2)}, u32[]{:S(2)}) collective-permute-start(f32[2,8,8,256]{3,2,1,0:T(8,128)} %get-tuple-element.47), channel_id=1, source_target_pairs={{0,1},{1,0},{2,3},{3,2},{4,5},{5,4},{6,7},{7,6},{8,9},{9,8},{10,11... | collective-permute-start | bytes 393224 | tf_op jit(solution)/shard_map/ppermute | solution.py:197
  49.1 12.3 %collective-permute-start.15 = (f32[2,8,8,256]{3,2,1,0:T(8,128)}, f32[2,8,8,256]{3,2,1,0:T(8,128)S(1)}, u32[]{:S(2)}, u32[]{:S(2)}) collective-permute-start(f32[2,8,8,256]{3,2,1,0:T(8,128)} %get-tuple-element.48), channel_id=1, source_target_pairs={{0,7},{1,2},{2,1},{3,4},{4,3},{5,6},{6,5},{7,0},{8,15},{9,10},{10,... | collective-permute-start | bytes 393224 | tf_op jit(solution)/shard_map/ppermute | solution.py:196
  51.1 34.2 %collective-permute-start.24 = (f32[16,16,256]{2,1,0:T(8,128)S(1)}, f32[16,16,256]{2,1,0:T(8,128)S(1)}, u32[]{:S(2)}, u32[]{:S(2)}) collective-permute-start(f32[16,16,256]{2,1,0:T(8,128)S(1)} %copy-done.1), channel_id=1, source_target_pairs={{0,248},{8,0},{16,8},{24,16},{32,24},{40,32},{48,40},{56,48},{64,5... | collective-permute-start | bytes 786440 | tf_op jit(solution)/shard_map/ppermute | solution.py:209
  64.4 2.1 %collective-permute-start.16 = (f32[2,4,16,256]{3,2,1,0:T(8,128)S(1)}, f32[2,4,16,256]{3,2,1,0:T(8,128)S(1)}, u32[]{:S(2)}, u32[]{:S(2)}) collective-permute-start(f32[2,4,16,256]{3,2,1,0:T(8,128)S(1)} %get-tuple-element.53), channel_id=1, source_target_pairs={{0,8},{8,0},{16,24},{24,16},{32,40},{40,32},{48,56},{56,48},{64,72... | collective-permute-start | bytes 393224 | tf_op jit(solution)/shard_map/ppermute | solution.py:194
  64.8 17.5 %collective-permute-start.4 = (f32[8,256]{1,0:T(8,128)S(1)}, f32[8,256]{1,0:T(8,128)S(1)}, u32[]{:S(2)}, u32[]{:S(2)}) collective-permute-start(f32[8,256]{1,0:T(8,128)S(1)} %slice.49), channel_id=1, source_target_pairs={{0,8},{8,0},{16,24},{24,16},{32,40},{40,32},{48,56},{56,48},{64,72... | collective-permute-start | bytes 24584 | tf_op jit(solution)/shard_map/ppermute | solution.py:218
  65.0 11.4 %collective-permute-start.17 = (f32[2,4,16,256]{3,2,1,0:T(8,128)}, f32[2,4,16,256]{3,2,1,0:T(8,128)S(1)}, u32[]{:S(2)}, u32[]{:S(2)}) collective-permute-start(f32[2,4,16,256]{3,2,1,0:T(8,128)} %get-tuple-element.54), channel_id=1, source_target_pairs={{0,248},{8,16},{16,8},{24,32},{32,24},{40,48},{48,40},{56,64},{64,... | collective-permute-start | bytes 393224 | tf_op jit(solution)/shard_map/ppermute | solution.py:195
  65.3 11.1 %collective-permute-start.18 = (f32[2,8,8,256]{3,2,1,0:T(8,128)}, f32[2,8,8,256]{3,2,1,0:T(8,128)S(1)}, u32[]{:S(2)}, u32[]{:S(2)}) collective-permute-start(f32[2,8,8,256]{3,2,1,0:T(8,128)} %get-tuple-element.55), channel_id=1, source_target_pairs={{0,1},{1,0},{2,3},{3,2},{4,5},{5,4},{6,7},{7,6},{8,9},{9,8},{10,11... | collective-permute-start | bytes 393224 | tf_op jit(solution)/shard_map/ppermute | solution.py:197
  66.5 9.9 %collective-permute-start.19 = (f32[2,8,8,256]{3,2,1,0:T(8,128)}, f32[2,8,8,256]{3,2,1,0:T(8,128)S(1)}, u32[]{:S(2)}, u32[]{:S(2)}) collective-permute-start(f32[2,8,8,256]{3,2,1,0:T(8,128)} %get-tuple-element.56), channel_id=1, source_target_pairs={{0,7},{1,2},{2,1},{3,4},{4,3},{5,6},{6,5},{7,0},{8,15},{9,10},{10,... | collective-permute-start | bytes 393224 | tf_op jit(solution)/shard_map/ppermute | solution.py:196
  76.4 7.7 %copy-start.8 = (f32[16,16,256]{2,1,0:T(8,128)S(1)}, f32[16,16,256]{2,1,0:T(8,128)}, u32[]{:S(2)}) copy-start(f32[16,16,256]{2,1,0:T(8,128)} %base.1) | copy-start | bytes 786436
  79.4 5.9 %collective-permute-start.20 = (f32[2,4,16,256]{3,2,1,0:T(8,128)S(1)}, f32[2,4,16,256]{3,2,1,0:T(8,128)S(1)}, u32[]{:S(2)}, u32[]{:S(2)}) collective-permute-start(f32[2,4,16,256]{3,2,1,0:T(8,128)S(1)} %get-tuple-element.60), channel_id=1, source_target_pairs={{0,8},{8,0},{16,24},{24,16},{32,40},{40,32},{48,56},{56,48},{64,72... | collective-permute-start | bytes 393224 | tf_op jit(solution)/shard_map/ppermute | solution.py:194
  80.4 10.2 %collective-permute-start.21 = (f32[2,4,16,256]{3,2,1,0:T(8,128)S(1)}, f32[2,4,16,256]{3,2,1,0:T(8,128)S(1)}, u32[]{:S(2)}, u32[]{:S(2)}) collective-permute-start(f32[2,4,16,256]{3,2,1,0:T(8,128)S(1)} %get-tuple-element.61), channel_id=1, source_target_pairs={{0,248},{8,16},{16,8},{24,32},{32,24},{40,48},{48,40},{56,64},{64,... | collective-permute-start | bytes 393224 | tf_op jit(solution)/shard_map/ppermute | solution.py:195
  82.3 8.3 %collective-permute-start.22 = (f32[2,8,8,256]{3,2,1,0:T(8,128)S(1)}, f32[2,8,8,256]{3,2,1,0:T(8,128)S(1)}, u32[]{:S(2)}, u32[]{:S(2)}) collective-permute-start(f32[2,8,8,256]{3,2,1,0:T(8,128)S(1)} %get-tuple-element.62), channel_id=1, source_target_pairs={{0,1},{1,0},{2,3},{3,2},{4,5},{5,4},{6,7},{7,6},{8,9},{9,8},{10,11... | collective-permute-start | bytes 393224 | tf_op jit(solution)/shard_map/ppermute | solution.py:197
  82.3 8.3 %collective-permute-start.23 = (f32[2,8,8,256]{3,2,1,0:T(8,128)S(1)}, f32[2,8,8,256]{3,2,1,0:T(8,128)S(1)}, u32[]{:S(2)}, u32[]{:S(2)}) collective-permute-start(f32[2,8,8,256]{3,2,1,0:T(8,128)S(1)} %get-tuple-element.63), channel_id=1, source_target_pairs={{0,7},{1,2},{2,1},{3,4},{4,3},{5,6},{6,5},{7,0},{8,15},{9,10},{10,... | collective-permute-start | bytes 393224 | tf_op jit(solution)/shard_map/ppermute | solution.py:196
  84.1 6.5 %copy-start.6 = (f32[16,16,256]{2,1,0:T(8,128)S(1)}, f32[16,16,256]{2,1,0:T(8,128)}, u32[]{:S(2)}) copy-start(f32[16,16,256]{2,1,0:T(8,128)} %get-tuple-element.33.refs_1_) | copy-start | bytes 786436
  84.1 6.5 %copy-start.7 = (f32[16,16,256]{2,1,0:T(8,128)S(1)}, f32[16,16,256]{2,1,0:T(8,128)}, u32[]{:S(2)}) copy-start(f32[16,16,256]{2,1,0:T(8,128)} %get-tuple-element.35.refs_2_) | copy-start | bytes 786436

commit v2 on v1

v2 whole, which is shorter than its diff:
```python
import functools

import jax
import jax.numpy as jnp
from jax import lax
from jax.experimental import pallas as pl
from jax.experimental.pallas import tpu as pltpu
from jax.sharding import PartitionSpec as P

STEPS = 4
STENCIL = (-205.0 / 72.0, 8.0 / 5.0, -1.0 / 5.0, 8.0 / 315.0, -1.0 / 560.0)
F32 = jnp.float32
HIGHEST = lax.Precision.HIGHEST
LIMIT = 12 * 1024 * 1024


def sds(*shape):
    return jax.ShapeDtypeStruct(shape, F32)


def call(kernel, outs, scratch, *args, after=()):
    specs = [pl.BlockSpec(memory_space=pl.ANY)] * len(after)
    for a in args:
        space = pltpu.SMEM if a.dtype == jnp.int32 else pltpu.VMEM
        specs.append(pl.BlockSpec(memory_space=space))
    return pl.pallas_call(
        kernel,
        out_shape=outs,
        in_specs=specs,
        out_specs=[pl.BlockSpec(memory_space=pltpu.VMEM)] * len(outs),
        scratch_shapes=scratch,
        compiler_params=pltpu.CompilerParams(vmem_limit_bytes=LIMIT),
        cost_estimate=pl.CostEstimate(flops=1 << 20, bytes_accessed=1 << 20, transcendentals=0),
    )(*after, *args)


def moved_rows(moves):
    row = lax.broadcasted_iota(jnp.int32, (16, 256), 0)
    flags = jnp.zeros((16, 256), jnp.int32)
    for y in range(16):
        flags = jnp.where(row == y, moves[y], flags)
    return flags == 1


def place():
    return lax.axis_index("gx"), lax.axis_index("gy")


def send_faces(fields, sends):
    x1, od, y1, yo = sends
    gx, gy = place()
    even_x, even_y = lax.rem(gx, 2) == 0, lax.rem(gy, 2) == 0
    toward = jnp.where(even_x, 12, 0)
    for f, field in enumerate(fields):
        x1[f] = field[pl.ds(toward, 4)]
        od[f] = field[pl.ds(12 - toward, 4)]
        for half in range(2):
            block = field[8 * half : 8 * half + 8]
            low, high = block[:, 0:4, :], block[:, 12:16, :]
            rows = slice(4 * half, 4 * half + 4)
            y1[f, :, rows, :] = jnp.where(even_y, high, low)
            yo[f, :, rows, :] = jnp.where(even_y, low, high)


def interior_kernel(s, r, s_lap, r_lap, ext_s, ext_r, depth_s, depth_r):
    i = lax.broadcasted_iota(jnp.int32, (256, 256), 0)
    j = lax.broadcasted_iota(jnp.int32, (256, 256), 1)
    apart = jnp.abs(i - j)
    matrix = jnp.where(apart == 0, F32(3.0 * STENCIL[0]), F32(0.0))
    for k in range(1, 5):
        matrix = jnp.where(apart == k, F32(STENCIL[k]), matrix)
    for field, out, ext, depth in ((s, s_lap, ext_s, depth_s), (r, r_lap, ext_r, depth_r)):
        ext[4:20, 8:24, :] = field[...]
        ext[0:4, 8:24, :] = jnp.zeros((4, 16, 256), F32)
        ext[20:24, 8:24, :] = jnp.zeros((4, 16, 256), F32)
        ext[4:20, 0:8, :] = jnp.zeros((16, 8, 256), F32)
        ext[4:20, 24:32, :] = jnp.zeros((16, 8, 256), F32)
        depth[...] = jnp.dot(
            field[...].reshape(256, 256), matrix, precision=HIGHEST, preferred_element_type=F32
        ).reshape(16, 16, 256)
        for x in range(0, 16, 2):
            lap = depth[x : x + 2]
            here, there = slice(4 + x, 6 + x), slice(8, 24)
            for k in range(1, 5):
                pair = ext[4 + x + k : 6 + x + k, there, :] + ext[4 + x - k : 6 + x - k, there, :]
                pair = pair + (ext[here, 8 + k : 24 + k, :] + ext[here, 8 - k : 24 - k, :])
                lap = lap + F32(STENCIL[k]) * pair
            out[x : x + 2] = lap


def face_terms(halos, f):
    x1, od, y1, yo = halos
    gx, gy = place()
    even_x, even_y = lax.rem(gx, 2) == 0, lax.rem(gy, 2) == 0
    zero = F32(0.0)
    a, b = x1[f], od[f]
    low = jnp.where(gx > 0, jnp.where(even_x, b, a), zero)
    high = jnp.where(gx < 31, jnp.where(even_x, a, b), zero)
    planes = [None] * 16
    for p in range(4):
        planes[p] = sum(F32(STENCIL[k]) * low[4 + p - k] for k in range(p + 1, 5))
        planes[12 + p] = sum(F32(STENCIL[k]) * high[p + k - 4] for k in range(4 - p, 5))
    a, b = y1[f], yo[f]
    low = jnp.where(gy > 0, jnp.where(even_y, b, a), zero)
    high = jnp.where(gy < 7, jnp.where(even_y, a, b), zero)
    sub = lax.broadcasted_iota(jnp.int32, (8, 8, 256), 1)
    row = lax.rem(sub, 4)
    low_sum, high_sum = F32(STENCIL[4]) * low, F32(STENCIL[4]) * high
    for k in range(1, 4):
        c = F32(STENCIL[k])
        low_sum = low_sum + jnp.where(row < k, c * pltpu.roll(low, 4 + k, axis=1), zero)
        high_sum = high_sum + jnp.where(row >= 4 - k, c * pltpu.roll(high, 4 - k, axis=1), zero)
    first = sub < 4
    lows = (jnp.where(first, low_sum, zero), jnp.where(first, pltpu.roll(low_sum, 4, axis=1), zero))
    highs = (jnp.where(first, zero, pltpu.roll(high_sum, 4, axis=1)), jnp.where(first, zero, high_sum))
    return planes, lows, highs


def move_kernel(after, moves, s, r, s_in, r_in, s_out, r_out, *sends):
    arrives = place()[0] < 31
    moved = moved_rows(moves)
    for own, come, out in ((s, s_in, s_out), (r, r_in, r_out)):
        for x in range(0, 16, 2):
            out[x : x + 2] = jnp.where(
                moved[None], jnp.where(arrives, come[x : x + 2], F32(0.0)), own[x : x + 2]
            )
    send_faces((s_out, r_out), sends)


def own_kernel(s, r, s_out, r_out):
    s_out[...] = s[...]
    r_out[...] = r[...]


def pack_kernel(after, a, b, c, out):
    out[0] = a[...]
    out[1] = b[...]
    out[2] = c[...]


def update_kernel(step, *refs):
    refs = list(refs)
    take = lambda n: [refs.pop(0) for _ in range(n)]
    last = step == STEPS - 1
    if last:
        take(1)
    s, r, s_lap, r_lap = take(4)
    halos = take(4)
    if step == 0:
        moves, s_prev, r_prev, vel_own, vel_end, come = take(6)
    else:
        s_prev, r_prev, vel, picture = take(4)
    if last:
        moves, image, image_come = take(3)
    else:
        held, got = take(2)
    s_out, r_out, picture_out = take(3)
    if last:
        s_before, r_before = take(2)
    else:
        sends = take(4)
        low, high = take(2)
    if step == 0:
        (vel,) = take(1)

    if step == 0 or last:
        moved = moved_rows(moves)
        arrives = place()[0] < 31
    if last:
        s_before[...] = s[...]
        r_before[...] = r[...]
    if step == 0:
        for x in range(16):
            new = jnp.where(arrives, come[2, x], vel_end[x])
            vel[x] = jnp.where(moved, new, vel_own[x])
    for f, (field, lap, prev, out) in enumerate(
        ((s, s_lap, s_prev, s_out), (r, r_lap, r_prev, r_out))
    ):
        planes, lows, highs = face_terms(halos, f)
        for x in range(16):
            if step == 0:
                old = jnp.where(moved, jnp.where(arrives, come[f, x], F32(0.0)), prev[x])
            else:
                old = prev[x]
            ends = jnp.concatenate([lows[x // 8][x % 8], highs[x // 8][x % 8]], axis=0)
            full = lap[x] + ends
            if planes[x] is not None:
                full = full + planes[x]
            out[x] = 2.0 * field[x] - old + vel[x] * full
    for x in range(16):
        product = s_out[x] * r_out[x]
        if step > 0:
            product = picture[x] + product
        if last:
            product = product + jnp.where(
                moved, jnp.where(arrives, image_come[x], F32(0.0)), image[x]
            )
        picture_out[x] = product
    if not last:
        send_faces((s_out, r_out), sends)
        keep(8 >> step, held, got, low, high)


def distance():
    gx = lax.axis_index("gx")
    return jnp.minimum(gx, 31 - gx)


def keep(reach, held, got, low, high):
    half = 4 * reach
    holds = lax.rem(distance(), 2 * reach) == 0
    low[...] = jnp.where(holds, held[:half], got[:half])
    high[...] = jnp.where(holds, held[half:], got[half:])


def scatter_kernel(after, moves, owner, image, end, low, high):
    upper = lax.axis_index("gx") >= 16
    z = lax.broadcasted_iota(jnp.int32, (8, 256), 1)
    target = jnp.zeros((8, 256), jnp.int32)
    for slab in range(32):
        target = jnp.where(z // 8 == slab, owner[slab], target)
    target = jnp.where(upper, 31 - target, target) * 8 + lax.rem(z, 8)
    rows = lax.broadcasted_iota(jnp.int32, (128, 256), 0)
    pick = jnp.where(rows == target[0:1, :], F32(1.0), F32(0.0))
    tile = jnp.where(upper, end[...], image[...])
    leaving = jnp.where(moved_rows(moves)[None], tile, F32(0.0)).reshape(256, 256)
    slabs = lax.dot_general(
        pick, leaving, (((1,), (1,)), ((), ())), precision=HIGHEST, preferred_element_type=F32
    )
    low[...] = slabs[:64]
    high[...] = slabs[64:]


def gather_kernel(owner, held, got, base, out, token):
    gx = lax.axis_index("gx")
    mine = jnp.int32(0)
    for slab in range(32):
        mine = jnp.where(owner[slab] == gx, slab, mine)
    depth = lax.broadcasted_iota(jnp.int32, (8, 256), 0)
    z = lax.broadcasted_iota(jnp.int32, (8, 256), 1)
    spread = jnp.where(z == 8 * mine + depth, F32(1.0), F32(0.0))
    slab = jnp.where(lax.rem(distance(), 2) == 0, held[...], got[...])
    out[...] = base[...] + lax.dot_general(
        slab, spread, (((0,), (0,)), ((), ())), precision=HIGHEST, preferred_element_type=F32
    ).reshape(16, 16, 256)
    token[...] = jnp.zeros((8, 128), F32)


def body(
    courant,
    vel_entering,
    image,
    src_prev,
    src_cur,
    rcv_prev,
    rcv_cur,
    global_image,
    shift_map,
    image_owner,
):
    n, m = 32, 8
    west = [(i, (i - 1) % n) for i in range(n)]
    pair_x = [(i, i ^ 1) for i in range(n)]
    odd_x = [(i, (i + (1 if i % 2 else -1)) % n) for i in range(n)]
    pair_y = [(i, i ^ 1) for i in range(m)]
    odd_y = [(i, (i + (1 if i % 2 else -1)) % m) for i in range(m)]

    def swap(x1, od, y1, yo):
        x1 = lax.ppermute(x1, "gx", pair_x)
        od = lax.ppermute(od, "gx", odd_x)
        yo = lax.ppermute(yo, "gy", odd_y)
        y1 = lax.ppermute(y1, "gy", pair_y)
        return x1, od, y1, yo

    owner = image_owner.reshape(32)
    tile = sds(16, 16, 256)
    faces = [sds(2, 4, 16, 256), sds(2, 4, 16, 256), sds(2, 8, 8, 256), sds(2, 8, 8, 256)]
    scratch = [pltpu.VMEM((24, 32, 256), F32)] * 2 + [pltpu.VMEM((16, 16, 256), F32)] * 2

    s_come = lax.ppermute(src_cur, "gx", west)
    s_own, r_own = call(own_kernel, [tile, tile], [], src_cur, rcv_cur)
    r_come = lax.ppermute(r_own, "gx", west)
    end = lax.ppermute(image, "gx", [(0, n - 1)])
    s, r, *sends = call(
        move_kernel,
        [tile, tile] + faces,
        [],
        shift_map,
        s_own,
        r_own,
        s_come,
        r_come,
        after=(end,),
    )
    (packed,) = call(pack_kernel, [sds(3, 16, 16, 256)], [], src_prev, rcv_prev, courant, after=(s,))
    come = lax.ppermute(packed, "gx", west)
    image_come = lax.ppermute(image, "gx", west)

    for step in range(STEPS):
        last = step == STEPS - 1
        halos = swap(*sends)
        if step == 0:
            low, high = call(
                scatter_kernel,
                [sds(64, 256)] * 2,
                [],
                shift_map,
                owner,
                image,
                end,
                after=(halos[0],),
            )
        got = lax.ppermute(high, "gx", [(i, i ^ (8 >> step)) for i in range(n)])
        s_lap, r_lap = call(interior_kernel, [tile, tile], scratch, s, r)
        ins = [s, r, s_lap, r_lap, *halos]
        outs, after = [tile] * 3, ()
        if step == 0:
            ins += [shift_map, src_prev, rcv_prev, courant, vel_entering, come]
        else:
            ins += [s_old, r_old, velocity, picture]
        if last:
            global_out, token = call(
                gather_kernel, [tile, sds(8, 128)], [], owner, low, got, global_image
            )
            ins += [shift_map, image, image_come]
            outs, after = outs + [tile] * 2, (token,)
        else:
            ins += [low, got]
            outs = outs + faces + [sds(32 >> step, 256)] * 2
        if step == 0:
            outs = outs + [tile]
        new = call(functools.partial(update_kernel, step), outs, [], *ins, after=after)
        if last:
            s_new, r_new, picture, s, r = new
            return (global_out, picture, s, s_new, r, r_new)
        s_old, r_old = s, r
        s, r, picture, *sends = new
        if step == 0:
            velocity = sends.pop()
        *sends, low, high = sends


def solution(mesh):
    tiled = P("gx", "gy", None)
    in_specs = (
        tiled,
        P(None, "gy", None),
        tiled,
        tiled,
        tiled,
        tiled,
        tiled,
        tiled,
        P("gy"),
        P("gy", None),
    )
    return jax.shard_map(
        body, mesh=mesh, in_specs=in_specs, out_specs=(tiled,) * 6, check_vma=False
    )
```

time: 94.3 us -> 85 us (0.901)
  waiting for transfers between devices: 33 us -> 17.8 us
  starting transfers between devices: 41.5 us -> 50.9 us
  Pallas kernels: 14.2 us -> 12.2 us
  other arithmetic: 1.76 us -> 0 us
    ppermute x4, waiting for transfers between devices: 19.2 us -> 9.67 us  [swap(): od = lax.ppermute(od, 'gx', odd_x)]
    ppermute x1, waiting for transfers between devices: 4.44 us -> 0.01 us  [body(): s_come = lax.ppermute(src_cur, 'gx', west)]
    ppermute x4, starting transfers between devices: 8.47 us -> 12.5 us  [swap(): yo = lax.ppermute(yo, 'gy', odd_y)]
    ppermute x4, starting transfers between devices: 2.19 us -> 4.42 us  [swap(): od = lax.ppermute(od, 'gx', odd_x)]
    pallas_call x7 -> x13, Pallas kernels: 14.2 us -> 12.2 us  [call(): pl.pallas_call(kernel, out_shape=outs, in_specs=specs, out_specs=[pl.Bloc...]
    ppermute x7, starting transfers between devices: 13 us -> 14.4 us  [the longest x1 8.19 us: body(): r_come = lax.ppermute(r_own, 'gx', west)]
    ppermute x1, starting transfers between devices: 1.98 us -> 3.32 us  [body(): s_come = lax.ppermute(src_cur, 'gx', west)]
    ppermute x4, waiting for transfers between devices: 6.25 us -> 5.12 us  [swap(): y1 = lax.ppermute(y1, 'gy', pair_y)]
  transfers between devices with their start and end apart: 25 -> 25, of which waited for: 8 -> 7; matrix products, arithmetic and copies ran while one was open for 1% -> 0% of each run, Pallas kernels for 12% -> 10%
where the time goes in v2:
time: 85 us; the launch traced here: 84 us
  starting transfers between devices  50.9 us (60%)
  waiting for transfers between devices  17.8 us (21%)
  Pallas kernels  12.2 us (14%)
  local copies, waits for them, and re-layouts  2.29 us (3%)
    ppermute x4, starting transfers between devices, swap(): yo = lax.ppermute(yo, 'gy', odd_y)  12.5 us
    pallas_call x13, Pallas kernels, call(): pl.pallas_call(kernel, out_shape=outs, in_specs=specs, out_specs=[pl.Bloc...  12.2 us
    ppermute x4, starting transfers between devices, swap(): x1 = lax.ppermute(x1, 'gx', pair_x)  11.2 us
    ppermute x4, waiting for transfers between devices, swap(): od = lax.ppermute(od, 'gx', odd_x)  9.67 us
    ppermute x1, starting transfers between devices, body(): r_come = lax.ppermute(r_own, 'gx', west)  8.19 us
    ppermute x4, waiting for transfers between devices, swap(): y1 = lax.ppermute(y1, 'gy', pair_y)  5.12 us
    ppermute x4, starting transfers between devices, swap(): od = lax.ppermute(od, 'gx', odd_x)  4.42 us
    ppermute x1, starting transfers between devices, body(): come = lax.ppermute(packed, 'gx', west)  4.01 us
  transfers between devices with their start and end apart: 25, of which 7 were waited for; matrix products, arithmetic and copies ran while one was open for 0% of the time, Pallas kernels for 10%

profile of v2, /device:TPU:1, one launch (start us, length us, event | category | flops | bytes accessed | tf_op | source)
XLA Modules:
  0.0 84.0 jit_solution(17388081288211881740)
XLA Ops:
  0.6 3.3 %collective-permute-start.1 = (f32[16,16,256]{2,1,0:T(8,128)}, f32[16,16,256]{2,1,0:T(8,128)S(1)}, u32[]{:S(2)}, u32[]{:S(2)}) collective-permute-start(f32[16,16,256]{2,1,0:T(8,128)} %s.1), channel_id=1, source_target_pairs={{0,248},{8,0},{16,8},{24,16},{32,24},{40,32},{48,40},{56,48},{64,5... | collective-permute-start | bytes 786440 | tf_op jit(solution)/shard_map/ppermute | solution.py:280
  4.0 0.7 collective-permute-start
  4.6 0.9 %copy-done.4 = f32[16,16,256]{2,1,0:T(8,128)S(1)} copy-done((f32[16,16,256]{2,1,0:T(8,128)S(1)}, f32[16,16,256]{2,1,0:T(8,128)}, u32[]{:S(2)}) %copy-start.4) | copy-done | bytes 262168
  5.6 0.9 %copy-done.5 = f32[16,16,256]{2,1,0:T(8,128)S(1)} copy-done((f32[16,16,256]{2,1,0:T(8,128)S(1)}, f32[16,16,256]{2,1,0:T(8,128)}, u32[]{:S(2)}) %copy-start.5) | copy-done | bytes 262168
  6.6 0.0 copy-start.8
  6.6 8.2 %collective-permute-start.2 = (f32[16,16,256]{2,1,0:T(8,128)S(1)}, f32[16,16,256]{2,1,0:T(8,128)S(1)}, u32[]{:S(2)}, u32[]{:S(2)}) collective-permute-start(f32[16,16,256]{2,1,0:T(8,128)S(1)} %get-tuple-element.60.r), channel_id=1, source_target_pairs={{0,248},{8,0},{16,8},{24,16},{32,24},{40,32},{48,40},{56,48},{64,5... | collective-permute-start | bytes 786440 | tf_op jit(solution)/shard_map/ppermute | solution.py:282
  14.8 0.0 collective-permute-done.1.s_in
  14.8 0.0 collective-permute-done.after.end
  14.8 1.2 %collective-permute-done.2.r_in = f32[16,16,256]{2,1,0:T(8,128)S(1)} collective-permute-done((f32[16,16,256]{2,1,0:T(8,128)S(1)}, f32[16,16,256]{2,1,0:T(8,128)S(1)}, u32[]{:S(2)}, u32[]{:S(2)}) %collective-permute-start.2) | collective-permute-done | bytes 262176 | tf_op jit(solution)/shard_map/ppermute | solution.py:282
  15.9 0.7 shard_map.146
  16.7 0.2 copy-done
  16.9 0.1 copy-done.1
  17.0 0.1 copy-done.2
  17.0 0.1 shard_map.148
  17.1 4.0 %collective-permute-start.7 = (f32[3,16,16,256]{3,2,1,0:T(8,128)S(1)}, f32[3,16,16,256]{3,2,1,0:T(8,128)S(1)}, u32[]{:S(2)}, u32[]{:S(2)}) collective-permute-start(f32[3,16,16,256]{3,2,1,0:T(8,128)S(1)} %shard_map.148), channel_id=1, source_target_pairs={{0,248},{8,0},{16,8},{24,16},{32,24},{40,32},{48,40},{56,48},{64,5... | collective-permute-start | bytes 2359304 | tf_op jit(solution)/shard_map/ppermute | solution.py:296
  21.1 5.5 %collective-permute-start.3 = (f32[2,4,16,256]{3,2,1,0:T(8,128)S(1)}, f32[2,4,16,256]{3,2,1,0:T(8,128)S(1)}, u32[]{:S(2)}, u32[]{:S(2)}) collective-permute-start(f32[2,4,16,256]{3,2,1,0:T(8,128)S(1)} %get-tuple-element.65), channel_id=1, source_target_pairs={{0,8},{8,0},{16,24},{24,16},{32,40},{40,32},{48,56},{56,48},{64,72... | collective-permute-start | bytes 393224 | tf_op jit(solution)/shard_map/ppermute | solution.py:269
  26.6 0.0 collective-permute-start.4
  26.6 0.4 collective-permute-start.5
  27.0 3.3 %collective-permute-start.6 = (f32[2,8,8,256]{3,2,1,0:T(8,128)S(1)}, f32[2,8,8,256]{3,2,1,0:T(8,128)S(1)}, u32[]{:S(2)}, u32[]{:S(2)}) collective-permute-start(f32[2,8,8,256]{3,2,1,0:T(8,128)S(1)} %get-tuple-element.68), channel_id=1, source_target_pairs={{0,7},{1,2},{2,1},{3,4},{4,3},{5,6},{6,5},{7,0},{8,15},{9,10},{10,... | collective-permute-start | bytes 393224 | tf_op jit(solution)/shard_map/ppermute | solution.py:271
  30.3 0.0 collective-permute-done.3.after.refs_4_
  30.3 0.9 %shard_map.149 = (f32[64,256]{1,0:T(8,128)S(1)}, f32[64,256]{1,0:T(8,128)S(1)}) custom-call(f32[2,4,16,256]{3,2,1,0:T(8,128)S(1)} %collective-permute-done.3.after.refs_4_, s32[16]{0:T(128)S(1)} %copy-done.8, s32[32]{0:T(128)S(1)} %bitcast.1, f32[16,16,256]{2,1,0:T(8,128)S(1)} %copy-done.3, f32[16,16,256]{2,1,0:T(8,128)S(1)} %collective-permute-done.after.end), custom_call_target="tpu_custom_call" | custom-call | flops 1048576 | bytes 1048576 | tf_op jit(solution)/shard_map/pallas_call | solution.py:26
  31.2 0.1 collective-permute-start.8
  31.3 0.0 copy-start.7
  31.4 1.2 %shard_map.147 = (f32[16,16,256]{2,1,0:T(8,128)S(1)}, f32[16,16,256]{2,1,0:T(8,128)S(1)}) custom-call(f32[16,16,256]{2,1,0:T(8,128)S(1)} %get-tuple-element.61.s.after.refs_0_.refs_8_, f32[16,16,256]{2,1,0:T(8,128)S(1)} %get-tuple-element.62.r.refs_1_.refs_9_), custom_call_target="tpu_custom_call" | custom-call | flops 1048576 | bytes 1048576 | tf_op jit(solution)/shard_map/pallas_call | solution.py:26
  32.6 4.5 %collective-permute-done.4.refs_5_ = f32[2,4,16,256]{3,2,1,0:T(8,128)S(1)} collective-permute-done((f32[2,4,16,256]{3,2,1,0:T(8,128)S(1)}, f32[2,4,16,256]{3,2,1,0:T(8,128)S(1)}, u32[]{:S(2)}, u32[]{:S(2)}) %collective-permute-start.4) | collective-permute-done | bytes 131104 | tf_op jit(solution)/shard_map/ppermute | solution.py:270
  37.1 0.0 collective-permute-done.5.refs_6_
  37.1 0.0 collective-permute-done.6.refs_7_
  37.1 0.0 collective-permute-done.8.refs_15_
  37.1 0.0 collective-permute-done.7.refs_13_
  37.1 1.1 %shard_map.150 = (f32[16,16,256]{2,1,0:T(8,128)S(1)}, f32[16,16,256]{2,1,0:T(8,128)S(1)}, f32[16,16,256]{2,1,0:T(8,128)S(1)}, f32[2,4,16,256]{3,2,1,0:T(8,128)S(...) custom-call(f32[16,16,256]{2,1,0:T(8,128)S(1)} %get-tuple-element.61, ...), custom_call_target="tpu_custom_call" | custom-call | flops 1048576 | bytes 1048576 | tf_op jit(solution)/shard_map/pallas_call | solution.py:26
  38.3 2.0 %collective-permute-start.9 = (f32[2,4,16,256]{3,2,1,0:T(8,128)S(1)}, f32[2,4,16,256]{3,2,1,0:T(8,128)S(1)}, u32[]{:S(2)}, u32[]{:S(2)}) collective-permute-start(f32[2,4,16,256]{3,2,1,0:T(8,128)S(1)} %get-tuple-element.75), channel_id=1, source_target_pairs={{0,8},{8,0},{16,24},{24,16},{32,40},{40,32},{48,56},{56,48},{64,72... | collective-permute-start | bytes 393224 | tf_op jit(solution)/shard_map/ppermute | solution.py:269
  40.2 1.4 %collective-permute-start.10 = (f32[2,4,16,256]{3,2,1,0:T(8,128)S(1)}, f32[2,4,16,256]{3,2,1,0:T(8,128)S(1)}, u32[]{:S(2)}, u32[]{:S(2)}) collective-permute-start(f32[2,4,16,256]{3,2,1,0:T(8,128)S(1)} %get-tuple-element.76), channel_id=1, source_target_pairs={{0,248},{8,16},{16,8},{24,32},{32,24},{40,48},{48,40},{56,64},{64,... | collective-permute-start | bytes 393224 | tf_op jit(solution)/shard_map/ppermute | solution.py:270
  41.6 0.0 collective-permute-start.11
  41.6 3.5 %collective-permute-start.12 = (f32[2,8,8,256]{3,2,1,0:T(8,128)S(1)}, f32[2,8,8,256]{3,2,1,0:T(8,128)S(1)}, u32[]{:S(2)}, u32[]{:S(2)}) collective-permute-start(f32[2,8,8,256]{3,2,1,0:T(8,128)S(1)} %get-tuple-element.78), channel_id=1, source_target_pairs={{0,7},{1,2},{2,1},{3,4},{4,3},{5,6},{6,5},{7,0},{8,15},{9,10},{10,... | collective-permute-start | bytes 393224 | tf_op jit(solution)/shard_map/ppermute | solution.py:271
  45.1 0.0 collective-permute-start.13
  45.1 1.2 %shard_map.151 = (f32[16,16,256]{2,1,0:T(8,128)S(1)}, f32[16,16,256]{2,1,0:T(8,128)S(1)}) custom-call(f32[16,16,256]{2,1,0:T(8,128)S(1)} %get-tuple-element.71.s.refs_0_.refs_8_, f32[16,16,256]{2,1,0:T(8,128)S(1)} %get-tuple-element.72.r.refs_1_.refs_9_), custom_call_target="tpu_custom_call" | custom-call | flops 1048576 | bytes 1048576 | tf_op jit(solution)/shard_map/pallas_call | solution.py:26
  46.3 1.8 %collective-permute-done.13.refs_13_ = f32[32,256]{1,0:T(8,128)S(1)} collective-permute-done((f32[32,256]{1,0:T(8,128)S(1)}, f32[32,256]{1,0:T(8,128)S(1)}, u32[]{:S(2)}, u32[]{:S(2)}) %collective-permute-start.13) | collective-permute-done | bytes 32800 | tf_op jit(solution)/shard_map/ppermute | solution.py:313
  48.1 0.0 collective-permute-done.9.refs_4_
  48.1 3.4 %collective-permute-done.10.refs_5_ = f32[2,4,16,256]{3,2,1,0:T(8,128)S(1)} collective-permute-done((f32[2,4,16,256]{3,2,1,0:T(8,128)S(1)}, f32[2,4,16,256]{3,2,1,0:T(8,128)S(1)}, u32[]{:S(2)}, u32[]{:S(2)}) %collective-permute-start.10) | collective-permute-done | bytes 131104 | tf_op jit(solution)/shard_map/ppermute | solution.py:270
  51.6 0.0 collective-permute-done.11.refs_6_
  51.6 0.0 collective-permute-done.12.refs_7_
  51.6 0.5 shard_map.152
  52.1 0.3 collective-permute-start.18
  52.4 3.7 %collective-permute-start.14 = (f32[2,4,16,256]{3,2,1,0:T(8,128)S(1)}, f32[2,4,16,256]{3,2,1,0:T(8,128)S(1)}, u32[]{:S(2)}, u32[]{:S(2)}) collective-permute-start(f32[2,4,16,256]{3,2,1,0:T(8,128)S(1)} %get-tuple-element.87), channel_id=1, source_target_pairs={{0,8},{8,0},{16,24},{24,16},{32,40},{40,32},{48,56},{56,48},{64,72... | collective-permute-start | bytes 393224 | tf_op jit(solution)/shard_map/ppermute | solution.py:269
  56.0 3.0 %collective-permute-start.15 = (f32[2,4,16,256]{3,2,1,0:T(8,128)S(1)}, f32[2,4,16,256]{3,2,1,0:T(8,128)S(1)}, u32[]{:S(2)}, u32[]{:S(2)}) collective-permute-start(f32[2,4,16,256]{3,2,1,0:T(8,128)S(1)} %get-tuple-element.88), channel_id=1, source_target_pairs={{0,248},{8,16},{16,8},{24,32},{32,24},{40,48},{48,40},{56,64},{64,... | collective-permute-start | bytes 393224 | tf_op jit(solution)/shard_map/ppermute | solution.py:270
  59.1 2.9 %collective-permute-start.17 = (f32[2,8,8,256]{3,2,1,0:T(8,128)S(1)}, f32[2,8,8,256]{3,2,1,0:T(8,128)S(1)}, u32[]{:S(2)}, u32[]{:S(2)}) collective-permute-start(f32[2,8,8,256]{3,2,1,0:T(8,128)S(1)} %get-tuple-element.90), channel_id=1, source_target_pairs={{0,7},{1,2},{2,1},{3,4},{4,3},{5,6},{6,5},{7,0},{8,15},{9,10},{10,... | collective-permute-start | bytes 393224 | tf_op jit(solution)/shard_map/ppermute | solution.py:271
  61.9 0.0 collective-permute-done.18.refs_13_
  62.0 2.8 %collective-permute-start.24 = (f32[16,16,256]{2,1,0:T(8,128)S(1)}, f32[16,16,256]{2,1,0:T(8,128)S(1)}, u32[]{:S(2)}, u32[]{:S(2)}) collective-permute-start(f32[16,16,256]{2,1,0:T(8,128)S(1)} %copy-done.3), channel_id=1, source_target_pairs={{0,248},{8,0},{16,8},{24,16},{32,24},{40,32},{48,40},{56,48},{64,5... | collective-permute-start | bytes 786440 | tf_op jit(solution)/shard_map/ppermute | solution.py:297
  64.7 1.2 %shard_map.153 = (f32[16,16,256]{2,1,0:T(8,128)S(1)}, f32[16,16,256]{2,1,0:T(8,128)S(1)}) custom-call(f32[16,16,256]{2,1,0:T(8,128)S(1)} %get-tuple-element.83.s.refs_0_.refs_9_, f32[16,16,256]{2,1,0:T(8,128)S(1)} %get-tuple-element.84.r.refs_1_.refs_10_), custom_call_target="tpu_custom_call" | custom-call | flops 1048576 | bytes 1048576 | tf_op jit(solution)/shard_map/pallas_call | solution.py:26
  65.9 0.0 collective-permute-done.14.refs_4_
  65.9 1.7 %collective-permute-done.15.refs_5_ = f32[2,4,16,256]{3,2,1,0:T(8,128)S(1)} collective-permute-done((f32[2,4,16,256]{3,2,1,0:T(8,128)S(1)}, f32[2,4,16,256]{3,2,1,0:T(8,128)S(1)}, u32[]{:S(2)}, u32[]{:S(2)}) %collective-permute-start.15) | collective-permute-done | bytes 131104 | tf_op jit(solution)/shard_map/ppermute | solution.py:270
  67.7 2.8 %collective-permute-done.16.refs_6_ = f32[2,8,8,256]{3,2,1,0:T(8,128)S(1)} collective-permute-done((f32[2,8,8,256]{3,2,1,0:T(8,128)S(1)}, f32[2,8,8,256]{3,2,1,0:T(8,128)S(1)}, u32[]{:S(2)}, u32[]{:S(2)}) %collective-permute-start.16) | collective-permute-done | bytes 131104 | tf_op jit(solution)/shard_map/ppermute | solution.py:272
  70.5 0.5 shard_map.154
  71.0 1.2 %collective-permute-start.19 = (f32[8,256]{1,0:T(8,128)S(1)}, f32[8,256]{1,0:T(8,128)S(1)}, u32[]{:S(2)}, u32[]{:S(2)}) collective-permute-start(f32[8,256]{1,0:T(8,128)S(1)} %get-tuple-element.95), channel_id=1, source_target_pairs={{0,8},{8,0},{16,24},{24,16},{32,40},{40,32},{48,56},{56,48},{64,72... | collective-permute-start | bytes 24584 | tf_op jit(solution)/shard_map/ppermute | solution.py:313
  72.1 0.1 collective-permute-start.20
  72.2 1.9 %collective-permute-start.22 = (f32[2,8,8,256]{3,2,1,0:T(8,128)S(1)}, f32[2,8,8,256]{3,2,1,0:T(8,128)S(1)}, u32[]{:S(2)}, u32[]{:S(2)}) collective-permute-start(f32[2,8,8,256]{3,2,1,0:T(8,128)S(1)} %get-tuple-element.104), channel_id=1, source_target_pairs={{0,1},{1,0},{2,3},{3,2},{4,5},{5,4},{6,7},{7,6},{8,9},{9,8},{10,11... | collective-permute-start | bytes 393224 | tf_op jit(solution)/shard_map/ppermute | solution.py:272
  74.1 0.0 collective-permute-done.19.got
  74.1 2.9 %collective-permute-start.23 = (f32[2,8,8,256]{3,2,1,0:T(8,128)S(1)}, f32[2,8,8,256]{3,2,1,0:T(8,128)S(1)}, u32[]{:S(2)}, u32[]{:S(2)}) collective-permute-start(f32[2,8,8,256]{3,2,1,0:T(8,128)S(1)} %get-tuple-element.105), channel_id=1, source_target_pairs={{0,7},{1,2},{2,1},{3,4},{4,3},{5,6},{6,5},{7,0},{8,15},{9,10},{10,... | collective-permute-start | bytes 393224 | tf_op jit(solution)/shard_map/ppermute | solution.py:271
  77.0 1.2 %shard_map.156 = (f32[16,16,256]{2,1,0:T(8,128)S(1)}, f32[16,16,256]{2,1,0:T(8,128)S(1)}) custom-call(f32[16,16,256]{2,1,0:T(8,128)S(1)} %get-tuple-element.98.s.refs_1_, f32[16,16,256]{2,1,0:T(8,128)S(1)} %get-tuple-element.99.r.refs_2_), custom_call_target="tpu_custom_call" | custom-call | flops 1048576 | bytes 1048576 | tf_op jit(solution)/shard_map/pallas_call | solution.py:26
  78.2 1.7 %shard_map.155 = (f32[16,16,256]{2,1,0:T(8,128)}, f32[8,128]{1,0:T(8,128)S(1)}) custom-call(s32[32]{0:T(128)S(1)} %bitcast.2, f32[8,256]{1,0:T(8,128)S(1)} %get-tuple-element.94.held, f32[8,256]{1,0:T(8,128)S(1)} %collective-permute-done.19.got, f32[16,16,256]{2,1,0:T(8,128)S(1)} %copy-done.6), custom_call_target="tpu_custom_call" | custom-call | flops 1048576 | bytes 1048576 | tf_op jit(solution)/shard_map/pallas_call | solution.py:26
  79.9 0.0 collective-permute-done.24.refs_15_
  79.9 2.3 %collective-permute-done.22.refs_7_ = f32[2,8,8,256]{3,2,1,0:T(8,128)S(1)} collective-permute-done((f32[2,8,8,256]{3,2,1,0:T(8,128)S(1)}, f32[2,8,8,256]{3,2,1,0:T(8,128)S(1)}, u32[]{:S(2)}, u32[]{:S(2)}) %collective-permute-start.22) | collective-permute-done | bytes 131104 | tf_op jit(solution)/shard_map/ppermute | solution.py:272
  82.2 0.0 collective-permute-done.23.refs_8_
  82.2 1.8 %shard_map.157 = (f32[16,16,256]{2,1,0:T(8,128)}, f32[16,16,256]{2,1,0:T(8,128)}, f32[16,16,256]{2,1,0:T(8,128)}, f32[16,16,256]{2,1,0:T(8,128)}, f32[16,16,256]{2,1,0:T(8,128)}) custom-call(f32[8,128]{1,0:T(8,128)S(1)} %get-tuple-element.97.refs_0_, f32[16,16,256]{2,1,0:T(8,128)S(1)} %get-tuple-element.98.s.refs_1_, ...), custom_call_target="tpu_custom_call" | custom-call | flops 1048576 | bytes 1048576 | tf_op jit(solution)/shard_map/pallas_call | solution.py:26
  (19 shorter events, 0.1 us)
Async XLA Ops:
  0.6 14.1 %collective-permute-start.1 = (f32[16,16,256]{2,1,0:T(8,128)}, f32[16,16,256]{2,1,0:T(8,128)S(1)}, u32[]{:S(2)}, u32[]{:S(2)}) collective-permute-start(f32[16,16,256]{2,1,0:T(8,128)} %s.1), channel_id=1, source_target_pairs={{0,248},{8,0},{16,8},{24,16},{32,24},{40,32},{48,40},{56,48},{64,5... | collective-permute-start | bytes 786440 | tf_op jit(solution)/shard_map/ppermute | solution.py:280
  4.0 10.8 %collective-permute-start = (f32[16,16,256]{2,1,0:T(8,128)}, f32[16,16,256]{2,1,0:T(8,128)S(1)}, u32[]{:S(2)}, u32[]{:S(2)}) collective-permute-start(f32[16,16,256]{2,1,0:T(8,128)} %refs_14_.1), channel_id=1, source_target_pairs={{0,248},{1,249},{2,250},{3,251},{4,252},{5,253},{6,254},{7,255}} | collective-permute-start | bytes 786440 | tf_op jit(solution)/shard_map/ppermute | solution.py:283
  4.6 1.0 %copy-start.4 = (f32[16,16,256]{2,1,0:T(8,128)S(1)}, f32[16,16,256]{2,1,0:T(8,128)}, u32[]{:S(2)}) copy-start(f32[16,16,256]{2,1,0:T(8,128)} %r.1) | copy-start | bytes 786436
  5.6 0.9 %copy-start.5 = (f32[16,16,256]{2,1,0:T(8,128)S(1)}, f32[16,16,256]{2,1,0:T(8,128)}, u32[]{:S(2)}) copy-start(f32[16,16,256]{2,1,0:T(8,128)} %s.1) | copy-start | bytes 786436
  6.6 9.4 %copy-start.8 = (s32[16]{0:T(128)S(1)}, s32[16]{0:T(128)}, u32[]{:S(2)}) copy-start(s32[16]{0:T(128)} %refs_13_.1) | copy-start | bytes 196
  6.6 9.3 %collective-permute-start.2 = (f32[16,16,256]{2,1,0:T(8,128)S(1)}, f32[16,16,256]{2,1,0:T(8,128)S(1)}, u32[]{:S(2)}, u32[]{:S(2)}) collective-permute-start(f32[16,16,256]{2,1,0:T(8,128)S(1)} %get-tuple-element.60.r), channel_id=1, source_target_pairs={{0,248},{8,0},{16,8},{24,16},{32,24},{40,32},{48,40},{56,48},{64,5... | collective-permute-start | bytes 786440 | tf_op jit(solution)/shard_map/ppermute | solution.py:282
  15.9 1.0 %copy-start = (f32[16,16,256]{2,1,0:T(8,128)S(1)}, f32[16,16,256]{2,1,0:T(8,128)}, u32[]{:S(2)}) copy-start(f32[16,16,256]{2,1,0:T(8,128)} %refs_9_.1) | copy-start | bytes 786436
  15.9 1.0 %copy-start.1 = (f32[16,16,256]{2,1,0:T(8,128)S(1)}, f32[16,16,256]{2,1,0:T(8,128)}, u32[]{:S(2)}) copy-start(f32[16,16,256]{2,1,0:T(8,128)} %refs_10_.1) | copy-start | bytes 786436
  15.9 1.1 %copy-start.2 = (f32[16,16,256]{2,1,0:T(8,128)S(1)}, f32[16,16,256]{2,1,0:T(8,128)}, u32[]{:S(2)}) copy-start(f32[16,16,256]{2,1,0:T(8,128)} %refs_11_.1) | copy-start | bytes 786436
  17.0 13.3 %copy-start.3 = (f32[16,16,256]{2,1,0:T(8,128)S(1)}, f32[16,16,256]{2,1,0:T(8,128)}, u32[]{:S(2)}) copy-start(f32[16,16,256]{2,1,0:T(8,128)} %refs_14_.1) | copy-start | bytes 786436
  17.1 20.0 %collective-permute-start.7 = (f32[3,16,16,256]{3,2,1,0:T(8,128)S(1)}, f32[3,16,16,256]{3,2,1,0:T(8,128)S(1)}, u32[]{:S(2)}, u32[]{:S(2)}) collective-permute-start(f32[3,16,16,256]{3,2,1,0:T(8,128)S(1)} %shard_map.148), channel_id=1, source_target_pairs={{0,248},{8,0},{16,8},{24,16},{32,24},{40,32},{48,40},{56,48},{64,5... | collective-permute-start | bytes 2359304 | tf_op jit(solution)/shard_map/ppermute | solution.py:296
  21.1 9.2 %collective-permute-start.3 = (f32[2,4,16,256]{3,2,1,0:T(8,128)S(1)}, f32[2,4,16,256]{3,2,1,0:T(8,128)S(1)}, u32[]{:S(2)}, u32[]{:S(2)}) collective-permute-start(f32[2,4,16,256]{3,2,1,0:T(8,128)S(1)} %get-tuple-element.65), channel_id=1, source_target_pairs={{0,8},{8,0},{16,24},{24,16},{32,40},{40,32},{48,56},{56,48},{64,72... | collective-permute-start | bytes 393224 | tf_op jit(solution)/shard_map/ppermute | solution.py:269
  26.6 10.5 %collective-permute-start.4 = (f32[2,4,16,256]{3,2,1,0:T(8,128)S(1)}, f32[2,4,16,256]{3,2,1,0:T(8,128)S(1)}, u32[]{:S(2)}, u32[]{:S(2)}) collective-permute-start(f32[2,4,16,256]{3,2,1,0:T(8,128)S(1)} %get-tuple-element.66), channel_id=1, source_target_pairs={{0,248},{8,16},{16,8},{24,32},{32,24},{40,48},{48,40},{56,64},{64,... | collective-permute-start | bytes 393224 | tf_op jit(solution)/shard_map/ppermute | solution.py:270
  26.6 10.5 %collective-permute-start.5 = (f32[2,8,8,256]{3,2,1,0:T(8,128)S(1)}, f32[2,8,8,256]{3,2,1,0:T(8,128)S(1)}, u32[]{:S(2)}, u32[]{:S(2)}) collective-permute-start(f32[2,8,8,256]{3,2,1,0:T(8,128)S(1)} %get-tuple-element.67), channel_id=1, source_target_pairs={{0,1},{1,0},{2,3},{3,2},{4,5},{5,4},{6,7},{7,6},{8,9},{9,8},{10,11... | collective-permute-start | bytes 393224 | tf_op jit(solution)/shard_map/ppermute | solution.py:272
  27.0 3.3 %copy-start.9 = (s32[1,32]{1,0:T(1,128)S(1)}, s32[1,32]{1,0:T(1,128)}, u32[]{:S(2)}) copy-start(s32[1,32]{1,0:T(1,128)} %param.19) | copy-start | bytes 388
  27.0 10.1 %collective-permute-start.6 = (f32[2,8,8,256]{3,2,1,0:T(8,128)S(1)}, f32[2,8,8,256]{3,2,1,0:T(8,128)S(1)}, u32[]{:S(2)}, u32[]{:S(2)}) collective-permute-start(f32[2,8,8,256]{3,2,1,0:T(8,128)S(1)} %get-tuple-element.68), channel_id=1, source_target_pairs={{0,7},{1,2},{2,1},{3,4},{4,3},{5,6},{6,5},{7,0},{8,15},{9,10},{10,... | collective-permute-start | bytes 393224 | tf_op jit(solution)/shard_map/ppermute | solution.py:271
  31.2 5.9 %collective-permute-start.8 = (f32[64,256]{1,0:T(8,128)S(1)}, f32[64,256]{1,0:T(8,128)S(1)}, u32[]{:S(2)}, u32[]{:S(2)}) collective-permute-start(f32[64,256]{1,0:T(8,128)S(1)} %get-tuple-element.70), channel_id=1, source_target_pairs={{0,64},{8,72},{16,80},{24,88},{32,96},{40,104},{48,112},{56,120},{... | collective-permute-start | bytes 196616 | tf_op jit(solution)/shard_map/ppermute | solution.py:313
  31.3 5.8 %copy-start.7 = (f32[16,16,256]{2,1,0:T(8,128)S(1)}, f32[16,16,256]{2,1,0:T(8,128)}, u32[]{:S(2)}) copy-start(f32[16,16,256]{2,1,0:T(8,128)} %refs_12_.1) | copy-start | bytes 786436
  38.3 9.9 %collective-permute-start.9 = (f32[2,4,16,256]{3,2,1,0:T(8,128)S(1)}, f32[2,4,16,256]{3,2,1,0:T(8,128)S(1)}, u32[]{:S(2)}, u32[]{:S(2)}) collective-permute-start(f32[2,4,16,256]{3,2,1,0:T(8,128)S(1)} %get-tuple-element.75), channel_id=1, source_target_pairs={{0,8},{8,0},{16,24},{24,16},{32,40},{40,32},{48,56},{56,48},{64,72... | collective-permute-start | bytes 393224 | tf_op jit(solution)/shard_map/ppermute | solution.py:269
  40.2 11.4 %collective-permute-start.10 = (f32[2,4,16,256]{3,2,1,0:T(8,128)S(1)}, f32[2,4,16,256]{3,2,1,0:T(8,128)S(1)}, u32[]{:S(2)}, u32[]{:S(2)}) collective-permute-start(f32[2,4,16,256]{3,2,1,0:T(8,128)S(1)} %get-tuple-element.76), channel_id=1, source_target_pairs={{0,248},{8,16},{16,8},{24,32},{32,24},{40,48},{48,40},{56,64},{64,... | collective-permute-start | bytes 393224 | tf_op jit(solution)/shard_map/ppermute | solution.py:270
  41.6 10.0 %collective-permute-start.11 = (f32[2,8,8,256]{3,2,1,0:T(8,128)S(1)}, f32[2,8,8,256]{3,2,1,0:T(8,128)S(1)}, u32[]{:S(2)}, u32[]{:S(2)}) collective-permute-start(f32[2,8,8,256]{3,2,1,0:T(8,128)S(1)} %get-tuple-element.77), channel_id=1, source_target_pairs={{0,1},{1,0},{2,3},{3,2},{4,5},{5,4},{6,7},{7,6},{8,9},{9,8},{10,11... | collective-permute-start | bytes 393224 | tf_op jit(solution)/shard_map/ppermute | solution.py:272
  41.6 10.0 %collective-permute-start.12 = (f32[2,8,8,256]{3,2,1,0:T(8,128)S(1)}, f32[2,8,8,256]{3,2,1,0:T(8,128)S(1)}, u32[]{:S(2)}, u32[]{:S(2)}) collective-permute-start(f32[2,8,8,256]{3,2,1,0:T(8,128)S(1)} %get-tuple-element.78), channel_id=1, source_target_pairs={{0,7},{1,2},{2,1},{3,4},{4,3},{5,6},{6,5},{7,0},{8,15},{9,10},{10,... | collective-permute-start | bytes 393224 | tf_op jit(solution)/shard_map/ppermute | solution.py:271
  45.1 3.1 %collective-permute-start.13 = (f32[32,256]{1,0:T(8,128)S(1)}, f32[32,256]{1,0:T(8,128)S(1)}, u32[]{:S(2)}, u32[]{:S(2)}) collective-permute-start(f32[32,256]{1,0:T(8,128)S(1)} %get-tuple-element.82), channel_id=1, source_target_pairs={{0,32},{8,40},{16,48},{24,56},{32,0},{40,8},{48,16},{56,24},{64,96... | collective-permute-start | bytes 98312 | tf_op jit(solution)/shard_map/ppermute | solution.py:313
  52.1 9.9 %collective-permute-start.18 = (f32[16,256]{1,0:T(8,128)S(1)}, f32[16,256]{1,0:T(8,128)S(1)}, u32[]{:S(2)}, u32[]{:S(2)}) collective-permute-start(f32[16,256]{1,0:T(8,128)S(1)} %get-tuple-element.93), channel_id=1, source_target_pairs={{0,16},{8,24},{16,0},{24,8},{32,48},{40,56},{48,32},{56,40},{64,80... | collective-permute-start | bytes 49160 | tf_op jit(solution)/shard_map/ppermute | solution.py:313
  52.4 13.6 %collective-permute-start.14 = (f32[2,4,16,256]{3,2,1,0:T(8,128)S(1)}, f32[2,4,16,256]{3,2,1,0:T(8,128)S(1)}, u32[]{:S(2)}, u32[]{:S(2)}) collective-permute-start(f32[2,4,16,256]{3,2,1,0:T(8,128)S(1)} %get-tuple-element.87), channel_id=1, source_target_pairs={{0,8},{8,0},{16,24},{24,16},{32,40},{40,32},{48,56},{56,48},{64,72... | collective-permute-start | bytes 393224 | tf_op jit(solution)/shard_map/ppermute | solution.py:269
  56.0 11.6 %collective-permute-start.15 = (f32[2,4,16,256]{3,2,1,0:T(8,128)S(1)}, f32[2,4,16,256]{3,2,1,0:T(8,128)S(1)}, u32[]{:S(2)}, u32[]{:S(2)}) collective-permute-start(f32[2,4,16,256]{3,2,1,0:T(8,128)S(1)} %get-tuple-element.88), channel_id=1, source_target_pairs={{0,248},{8,16},{16,8},{24,32},{32,24},{40,48},{48,40},{56,64},{64,... | collective-permute-start | bytes 393224 | tf_op jit(solution)/shard_map/ppermute | solution.py:270
  59.1 11.4 %collective-permute-start.16 = (f32[2,8,8,256]{3,2,1,0:T(8,128)S(1)}, f32[2,8,8,256]{3,2,1,0:T(8,128)S(1)}, u32[]{:S(2)}, u32[]{:S(2)}) collective-permute-start(f32[2,8,8,256]{3,2,1,0:T(8,128)S(1)} %get-tuple-element.89), channel_id=1, source_target_pairs={{0,1},{1,0},{2,3},{3,2},{4,5},{5,4},{6,7},{7,6},{8,9},{9,8},{10,11... | collective-permute-start | bytes 393224 | tf_op jit(solution)/shard_map/ppermute | solution.py:272
  59.1 11.4 %collective-permute-start.17 = (f32[2,8,8,256]{3,2,1,0:T(8,128)S(1)}, f32[2,8,8,256]{3,2,1,0:T(8,128)S(1)}, u32[]{:S(2)}, u32[]{:S(2)}) collective-permute-start(f32[2,8,8,256]{3,2,1,0:T(8,128)S(1)} %get-tuple-element.90), channel_id=1, source_target_pairs={{0,7},{1,2},{2,1},{3,4},{4,3},{5,6},{6,5},{7,0},{8,15},{9,10},{10,... | collective-permute-start | bytes 393224 | tf_op jit(solution)/shard_map/ppermute | solution.py:271
  62.0 18.0 %collective-permute-start.24 = (f32[16,16,256]{2,1,0:T(8,128)S(1)}, f32[16,16,256]{2,1,0:T(8,128)S(1)}, u32[]{:S(2)}, u32[]{:S(2)}) collective-permute-start(f32[16,16,256]{2,1,0:T(8,128)S(1)} %copy-done.3), channel_id=1, source_target_pairs={{0,248},{8,0},{16,8},{24,16},{32,24},{40,32},{48,40},{56,48},{64,5... | collective-permute-start | bytes 786440 | tf_op jit(solution)/shard_map/ppermute | solution.py:297
  71.0 3.1 %collective-permute-start.19 = (f32[8,256]{1,0:T(8,128)S(1)}, f32[8,256]{1,0:T(8,128)S(1)}, u32[]{:S(2)}, u32[]{:S(2)}) collective-permute-start(f32[8,256]{1,0:T(8,128)S(1)} %get-tuple-element.95), channel_id=1, source_target_pairs={{0,8},{8,0},{16,24},{24,16},{32,40},{40,32},{48,56},{56,48},{64,72... | collective-permute-start | bytes 24584 | tf_op jit(solution)/shard_map/ppermute | solution.py:313
  72.1 7.8 %collective-permute-start.20 = (f32[2,4,16,256]{3,2,1,0:T(8,128)S(1)}, f32[2,4,16,256]{3,2,1,0:T(8,128)S(1)}, u32[]{:S(2)}, u32[]{:S(2)}) collective-permute-start(f32[2,4,16,256]{3,2,1,0:T(8,128)S(1)} %get-tuple-element.102), channel_id=1, source_target_pairs={{0,8},{8,0},{16,24},{24,16},{32,40},{40,32},{48,56},{56,48},{64,72... | collective-permute-start | bytes 393224 | tf_op jit(solution)/shard_map/ppermute | solution.py:269
  72.2 7.7 %collective-permute-start.21 = (f32[2,4,16,256]{3,2,1,0:T(8,128)S(1)}, f32[2,4,16,256]{3,2,1,0:T(8,128)S(1)}, u32[]{:S(2)}, u32[]{:S(2)}) collective-permute-start(f32[2,4,16,256]{3,2,1,0:T(8,128)S(1)} %get-tuple-element.103), channel_id=1, source_target_pairs={{0,248},{8,16},{16,8},{24,32},{32,24},{40,48},{48,40},{56,64},{64,... | collective-permute-start | bytes 393224 | tf_op jit(solution)/shard_map/ppermute | solution.py:270
  72.2 10.0 %collective-permute-start.22 = (f32[2,8,8,256]{3,2,1,0:T(8,128)S(1)}, f32[2,8,8,256]{3,2,1,0:T(8,128)S(1)}, u32[]{:S(2)}, u32[]{:S(2)}) collective-permute-start(f32[2,8,8,256]{3,2,1,0:T(8,128)S(1)} %get-tuple-element.104), channel_id=1, source_target_pairs={{0,1},{1,0},{2,3},{3,2},{4,5},{5,4},{6,7},{7,6},{8,9},{9,8},{10,11... | collective-permute-start | bytes 393224 | tf_op jit(solution)/shard_map/ppermute | solution.py:272
  74.1 8.1 %collective-permute-start.23 = (f32[2,8,8,256]{3,2,1,0:T(8,128)S(1)}, f32[2,8,8,256]{3,2,1,0:T(8,128)S(1)}, u32[]{:S(2)}, u32[]{:S(2)}) collective-permute-start(f32[2,8,8,256]{3,2,1,0:T(8,128)S(1)} %get-tuple-element.105), channel_id=1, source_target_pairs={{0,7},{1,2},{2,1},{3,4},{4,3},{5,6},{6,5},{7,0},{8,15},{9,10},{10,... | collective-permute-start | bytes 393224 | tf_op jit(solution)/shard_map/ppermute | solution.py:271
  77.0 1.2 %copy-start.6 = (f32[16,16,256]{2,1,0:T(8,128)S(1)}, f32[16,16,256]{2,1,0:T(8,128)}, u32[]{:S(2)}) copy-start(f32[16,16,256]{2,1,0:T(8,128)} %base.1) | copy-start | bytes 786436

commit v3 on v2

--- a/solution.py
+++ b/solution.py
@@ -18,7 +18,7 @@
     return jax.ShapeDtypeStruct(shape, F32)
 
 
-def call(kernel, outs, scratch, *args, after=()):
+def call(kernel, outs, scratch, *args, after=(), cost=1 << 20):
     specs = [pl.BlockSpec(memory_space=pl.ANY)] * len(after)
     for a in args:
         space = pltpu.SMEM if a.dtype == jnp.int32 else pltpu.VMEM
@@ -30,16 +30,8 @@
         out_specs=[pl.BlockSpec(memory_space=pltpu.VMEM)] * len(outs),
         scratch_shapes=scratch,
         compiler_params=pltpu.CompilerParams(vmem_limit_bytes=LIMIT),
-        cost_estimate=pl.CostEstimate(flops=1 << 20, bytes_accessed=1 << 20, transcendentals=0),
+        cost_estimate=pl.CostEstimate(flops=cost, bytes_accessed=cost, transcendentals=0),
     )(*after, *args)
-
-
-def moved_rows(moves):
-    row = lax.broadcasted_iota(jnp.int32, (16, 256), 0)
-    flags = jnp.zeros((16, 256), jnp.int32)
-    for y in range(16):
-        flags = jnp.where(row == y, moves[y], flags)
-    return flags == 1
 
 
 def place():
@@ -116,9 +108,9 @@
     return planes, lows, highs
 
 
-def move_kernel(after, moves, s, r, s_in, r_in, s_out, r_out, *sends):
+def move_kernel(moves, s, r, s_in, r_in, s_out, r_out, *sends):
     arrives = place()[0] < 31
-    moved = moved_rows(moves)
+    moved = (moves[...] == 1.0)
     for own, come, out in ((s, s_in, s_out), (r, r_in, r_out)):
         for x in range(0, 16, 2):
             out[x : x + 2] = jnp.where(
@@ -127,15 +119,22 @@
     send_faces((s_out, r_out), sends)
 
 
-def own_kernel(s, r, s_out, r_out):
+def own_kernel(moves, s, r, s_out, r_out, mask):
     s_out[...] = s[...]
     r_out[...] = r[...]
-
-
-def pack_kernel(after, a, b, c, out):
-    out[0] = a[...]
-    out[1] = b[...]
-    out[2] = c[...]
+    row = lax.broadcasted_iota(jnp.int32, (16, 256), 0)
+    flags = jnp.zeros((16, 256), jnp.int32)
+    for y in range(16):
+        flags = jnp.where(row == y, moves[y], flags)
+    mask[...] = jnp.where(flags == 1, F32(1.0), F32(0.0))
+
+
+def first_kernel(vel, image, out):
+    out[...] = jnp.where(place()[0] == 0, image[...], vel[...])
+
+
+def copy_kernel(after, a, out):
+    out[...] = a[...]
 
 
 def update_kernel(step, *refs):
@@ -147,39 +146,38 @@
     s, r, s_lap, r_lap = take(4)
     halos = take(4)
     if step == 0:
-        moves, s_prev, r_prev, vel_own, vel_end, come = take(6)
+        moves, s_prev, r_prev, vel_own, vel_end, s_come, r_come, vel_come = take(8)
     else:
         s_prev, r_prev, vel, picture = take(4)
     if last:
         moves, image, image_come = take(3)
-    else:
-        held, got = take(2)
     s_out, r_out, picture_out = take(3)
     if last:
         s_before, r_before = take(2)
     else:
         sends = take(4)
-        low, high = take(2)
     if step == 0:
         (vel,) = take(1)
 
     if step == 0 or last:
-        moved = moved_rows(moves)
+        moved = (moves[...] == 1.0)
         arrives = place()[0] < 31
     if last:
         s_before[...] = s[...]
         r_before[...] = r[...]
     if step == 0:
         for x in range(16):
-            new = jnp.where(arrives, come[2, x], vel_end[x])
+            new = jnp.where(arrives, vel_come[x], vel_end[x])
             vel[x] = jnp.where(moved, new, vel_own[x])
-    for f, (field, lap, prev, out) in enumerate(
-        ((s, s_lap, s_prev, s_out), (r, r_lap, r_prev, r_out))
+    if step > 0:
+        s_come = r_come = None
+    for f, (field, lap, prev, come, out) in enumerate(
+        ((s, s_lap, s_prev, s_come, s_out), (r, r_lap, r_prev, r_come, r_out))
     ):
         planes, lows, highs = face_terms(halos, f)
         for x in range(16):
             if step == 0:
-                old = jnp.where(moved, jnp.where(arrives, come[f, x], F32(0.0)), prev[x])
+                old = jnp.where(moved, jnp.where(arrives, come[x], F32(0.0)), prev[x])
             else:
                 old = prev[x]
             ends = jnp.concatenate([lows[x // 8][x % 8], highs[x // 8][x % 8]], axis=0)
@@ -198,7 +196,6 @@
         picture_out[x] = product
     if not last:
         send_faces((s_out, r_out), sends)
-        keep(8 >> step, held, got, low, high)
 
 
 def distance():
@@ -206,14 +203,14 @@
     return jnp.minimum(gx, 31 - gx)
 
 
-def keep(reach, held, got, low, high):
+def keep_kernel(reach, after, held, got, low, high):
     half = 4 * reach
     holds = lax.rem(distance(), 2 * reach) == 0
     low[...] = jnp.where(holds, held[:half], got[:half])
     high[...] = jnp.where(holds, held[half:], got[half:])
 
 
-def scatter_kernel(after, moves, owner, image, end, low, high):
+def scatter_kernel(after, moves, owner, image, come, low, high):
     upper = lax.axis_index("gx") >= 16
     z = lax.broadcasted_iota(jnp.int32, (8, 256), 1)
     target = jnp.zeros((8, 256), jnp.int32)
@@ -222,8 +219,8 @@
     target = jnp.where(upper, 31 - target, target) * 8 + lax.rem(z, 8)
     rows = lax.broadcasted_iota(jnp.int32, (128, 256), 0)
     pick = jnp.where(rows == target[0:1, :], F32(1.0), F32(0.0))
-    tile = jnp.where(upper, end[...], image[...])
-    leaving = jnp.where(moved_rows(moves)[None], tile, F32(0.0)).reshape(256, 256)
+    tile = jnp.where(upper, come[...], image[...])
+    leaving = jnp.where((moves[...] == 1.0)[None], tile, F32(0.0)).reshape(256, 256)
     slabs = lax.dot_general(
         pick, leaving, (((1,), (1,)), ((), ())), precision=HIGHEST, preferred_element_type=F32
     )
@@ -278,23 +275,17 @@
     scratch = [pltpu.VMEM((24, 32, 256), F32)] * 2 + [pltpu.VMEM((16, 16, 256), F32)] * 2
 
     s_come = lax.ppermute(src_cur, "gx", west)
-    s_own, r_own = call(own_kernel, [tile, tile], [], src_cur, rcv_cur)
-    r_come = lax.ppermute(r_own, "gx", west)
-    end = lax.ppermute(image, "gx", [(0, n - 1)])
+    r_come = lax.ppermute(rcv_cur, "gx", west)
+    sp_come = lax.ppermute(src_prev, "gx", west)
+    rp_come = lax.ppermute(rcv_prev, "gx", west)
+    (vel_send,) = call(first_kernel, [tile], [], courant, image)
+    vel_come = lax.ppermute(vel_send, "gx", west)
+    s_own, r_own, mask = call(
+        own_kernel, [tile] * 2 + [sds(16, 256)], [], shift_map, src_cur, rcv_cur
+    )
     s, r, *sends = call(
-        move_kernel,
-        [tile, tile] + faces,
-        [],
-        shift_map,
-        s_own,
-        r_own,
-        s_come,
-        r_come,
-        after=(end,),
-    )
-    (packed,) = call(pack_kernel, [sds(3, 16, 16, 256)], [], src_prev, rcv_prev, courant, after=(s,))
-    come = lax.ppermute(packed, "gx", west)
-    image_come = lax.ppermute(image, "gx", west)
+        move_kernel, [tile, tile] + faces, [], mask, s_own, r_own, s_come, r_come
+    )
 
     for step in range(STEPS):
         last = step == STEPS - 1
@@ -304,29 +295,41 @@
                 scatter_kernel,
                 [sds(64, 256)] * 2,
                 [],
-                shift_map,
+                mask,
                 owner,
                 image,
-                end,
+                vel_come,
                 after=(halos[0],),
             )
+        else:
+            low, high = call(
+                functools.partial(keep_kernel, 16 >> step),
+                [sds(64 >> step, 256)] * 2,
+                [],
+                low,
+                got,
+                after=(halos[0],),
+            )
         got = lax.ppermute(high, "gx", [(i, i ^ (8 >> step)) for i in range(n)])
+        if step == 1:
+            (image_send,) = call(copy_kernel, [tile], [], image, after=(halos[1],))
+            image_come = lax.ppermute(image_send, "gx", west)
         s_lap, r_lap = call(interior_kernel, [tile, tile], scratch, s, r)
         ins = [s, r, s_lap, r_lap, *halos]
         outs, after = [tile] * 3, ()
         if step == 0:
-            ins += [shift_map, src_prev, rcv_prev, courant, vel_entering, come]
+            ins += [mask, src_prev, rcv_prev, courant, vel_entering]
+            ins += [sp_come, rp_come, vel_come]
         else:
             ins += [s_old, r_old, velocity, picture]
         if last:
             global_out, token = call(
                 gather_kernel, [tile, sds(8, 128)], [], owner, low, got, global_image
             )
-            ins += [shift_map, image, image_come]
+            ins += [mask, image, image_come]
             outs, after = outs + [tile] * 2, (token,)
         else:
-            ins += [low, got]
-            outs = outs + faces + [sds(32 >> step, 256)] * 2
+            outs = outs + faces
         if step == 0:
             outs = outs + [tile]
         new = call(functools.partial(update_kernel, step), outs, [], *ins, after=after)
@@ -337,7 +340,6 @@
         s, r, picture, *sends = new
         if step == 0:
             velocity = sends.pop()
-        *sends, low, high = sends
 
 
 def solution(mesh):

time: 85 us -> 78.2 us (0.920)
  starting transfers between devices: 50.9 us -> 42.4 us
  waiting for transfers between devices: 17.8 us -> 20.8 us
  Pallas kernels: 12.2 us -> 11 us
    ppermute x4 -> x5, waiting for transfers between devices: 1.16 us -> 7.92 us  [the longest x1 4.6 us: body(): rp_come = lax.ppermute(rcv_prev, 'gx', west)]
    ppermute x4, waiting for transfers between devices: 9.67 us -> 4.51 us  [swap(): od = lax.ppermute(od, 'gx', odd_x)]
    ppermute x4 -> x5, starting transfers between devices: 15.6 us -> 11 us  [the longest x1 6.19 us: body(): r_come = lax.ppermute(rcv_cur, 'gx', west)]
    ppermute x4, starting transfers between devices: 12.5 us -> 9.29 us  [swap(): yo = lax.ppermute(yo, 'gy', odd_y)]
    ppermute x4, waiting for transfers between devices: 1.82 us -> 4.83 us  [body(): got = lax.ppermute(high, 'gx', [(i, i ^ 8 >> step) for i in range(n)])]
    ppermute x4, starting transfers between devices: 11.2 us -> 9.16 us  [swap(): x1 = lax.ppermute(x1, 'gx', pair_x)]
    ppermute x4, starting transfers between devices: 1.54 us -> 3.31 us  [body(): got = lax.ppermute(high, 'gx', [(i, i ^ 8 >> step) for i in range(n)])]
    ppermute x4, waiting for transfers between devices: 5.12 us -> 3.5 us  [swap(): y1 = lax.ppermute(y1, 'gy', pair_y)]
  transfers between devices with their start and end apart: 25 -> 26, of which waited for: 7 -> 7; matrix products, arithmetic and copies ran while one was open for 0% -> 0% of each run, Pallas kernels for 10% -> 12%
where the time goes in v3:
time: 78.2 us; the launch traced here: 77.8 us
  starting transfers between devices  42.4 us (54%)
  waiting for transfers between devices  20.8 us (27%)
  Pallas kernels  11 us (14%)
  local copies, waits for them, and re-layouts  2.75 us (4%)
  between operations  0.88 us (1%)
    pallas_call x17, Pallas kernels, call(): pl.pallas_call(kernel, out_shape=outs, in_specs=specs, out_specs=[pl.Bloc...  11 us
    ppermute x4, starting transfers between devices, swap(): yo = lax.ppermute(yo, 'gy', odd_y)  9.29 us
    ppermute x4, starting transfers between devices, swap(): x1 = lax.ppermute(x1, 'gx', pair_x)  9.16 us
    ppermute x1, starting transfers between devices, body(): r_come = lax.ppermute(rcv_cur, 'gx', west)  6.19 us
    ppermute x4, waiting for transfers between devices, body(): got = lax.ppermute(high, 'gx', [(i, i ^ 8 >> step) for i in range(n)])  4.83 us
    ppermute x1, waiting for transfers between devices, body(): rp_come = lax.ppermute(rcv_prev, 'gx', west)  4.6 us
    ppermute x4, starting transfers between devices, swap(): od = lax.ppermute(od, 'gx', odd_x)  4.59 us
    ppermute x4, waiting for transfers between devices, swap(): od = lax.ppermute(od, 'gx', odd_x)  4.51 us
  transfers between devices with their start and end apart: 26, of which 7 were waited for; matrix products, arithmetic and copies ran while one was open for 0% of the time, Pallas kernels for 12%

profile of v3, /device:TPU:1, one launch (start us, length us, event | category | flops | bytes accessed | tf_op | source)
XLA Modules:
  0.0 77.8 jit_solution(10183274964589941853)
XLA Ops:
  0.6 3.3 %collective-permute-start = (f32[16,16,256]{2,1,0:T(8,128)}, f32[16,16,256]{2,1,0:T(8,128)S(1)}, u32[]{:S(2)}, u32[]{:S(2)}) collective-permute-start(f32[16,16,256]{2,1,0:T(8,128)} %s.1), channel_id=1, source_target_pairs={{0,248},{8,0},{16,8},{24,16},{32,24},{40,32},{48,40},{56,48},{64,5... | collective-permute-start | bytes 786440 | tf_op jit(solution)/shard_map/ppermute | solution.py:277
  4.0 6.2 %collective-permute-start.1 = (f32[16,16,256]{2,1,0:T(8,128)}, f32[16,16,256]{2,1,0:T(8,128)S(1)}, u32[]{:S(2)}, u32[]{:S(2)}) collective-permute-start(f32[16,16,256]{2,1,0:T(8,128)} %r.1), channel_id=1, source_target_pairs={{0,248},{8,0},{16,8},{24,16},{32,24},{40,32},{48,40},{56,48},{64,5... | collective-permute-start | bytes 786440 | tf_op jit(solution)/shard_map/ppermute | solution.py:278
  10.1 0.9 %copy-done = f32[16,16,256]{2,1,0:T(8,128)S(1)} copy-done((f32[16,16,256]{2,1,0:T(8,128)S(1)}, f32[16,16,256]{2,1,0:T(8,128)}, u32[]{:S(2)}) %copy-start) | copy-done | bytes 262168
  11.1 0.9 %copy-done.2 = f32[16,16,256]{2,1,0:T(8,128)S(1)} copy-done((f32[16,16,256]{2,1,0:T(8,128)S(1)}, f32[16,16,256]{2,1,0:T(8,128)}, u32[]{:S(2)}) %copy-start.2) | copy-done | bytes 262168
  12.1 0.8 collective-permute-start.8
  12.8 0.2 copy-done.7
  13.0 0.7 collective-permute-start.6
  13.7 0.1 collective-permute-start.7
  13.8 0.7 copy-done.11
  14.4 0.6 shard_map.145
  15.0 0.0 collective-permute-done.s_in
  15.0 0.0 collective-permute-done.1.r_in
  15.0 0.0 copy-start.9
  15.0 0.2 shard_map.146
  15.2 2.7 %collective-permute-start.2 = (f32[2,4,16,256]{3,2,1,0:T(8,128)S(1)}, f32[2,4,16,256]{3,2,1,0:T(8,128)S(1)}, u32[]{:S(2)}, u32[]{:S(2)}) collective-permute-start(f32[2,4,16,256]{3,2,1,0:T(8,128)S(1)} %get-tuple-element.67), channel_id=1, source_target_pairs={{0,8},{8,0},{16,24},{24,16},{32,40},{40,32},{48,56},{56,48},{64,72... | collective-permute-start | bytes 393224 | tf_op jit(solution)/shard_map/ppermute | solution.py:266
  17.9 0.7 collective-permute-start.3
  18.6 0.9 %collective-permute-done.8.refs_15_.come = f32[16,16,256]{2,1,0:T(8,128)S(1)} collective-permute-done((f32[16,16,256]{2,1,0:T(8,128)S(1)}, f32[16,16,256]{2,1,0:T(8,128)S(1)}, u32[]{:S(2)}, u32[]{:S(2)}) %collective-permute-start.8) | collective-permute-done | bytes 262176 | tf_op jit(solution)/shard_map/ppermute | solution.py:282
  19.5 0.4 collective-permute-start.4
  19.9 2.4 %collective-permute-done.6.refs_13_ = f32[16,16,256]{2,1,0:T(8,128)S(1)} collective-permute-done((f32[16,16,256]{2,1,0:T(8,128)S(1)}, f32[16,16,256]{2,1,0:T(8,128)S(1)}, u32[]{:S(2)}, u32[]{:S(2)}) %collective-permute-start.6) | collective-permute-done | bytes 262176 | tf_op jit(solution)/shard_map/ppermute | solution.py:279
  22.3 2.6 %collective-permute-start.5 = (f32[2,8,8,256]{3,2,1,0:T(8,128)S(1)}, f32[2,8,8,256]{3,2,1,0:T(8,128)S(1)}, u32[]{:S(2)}, u32[]{:S(2)}) collective-permute-start(f32[2,8,8,256]{3,2,1,0:T(8,128)S(1)} %get-tuple-element.70), channel_id=1, source_target_pairs={{0,7},{1,2},{2,1},{3,4},{4,3},{5,6},{6,5},{7,0},{8,15},{9,10},{10,... | collective-permute-start | bytes 393224 | tf_op jit(solution)/shard_map/ppermute | solution.py:268
  24.9 1.2 %shard_map.147 = (f32[16,16,256]{2,1,0:T(8,128)S(1)}, f32[16,16,256]{2,1,0:T(8,128)S(1)}) custom-call(f32[16,16,256]{2,1,0:T(8,128)S(1)} %get-tuple-element.63.s.refs_0_.refs_8_, f32[16,16,256]{2,1,0:T(8,128)S(1)} %get-tuple-element.64.r.refs_1_.refs_9_), custom_call_target="tpu_custom_call" | custom-call | flops 1048576 | bytes 1048576 | tf_op jit(solution)/shard_map/pallas_call | solution.py:26
  26.1 4.6 %collective-permute-done.7.refs_14_ = f32[16,16,256]{2,1,0:T(8,128)S(1)} collective-permute-done((f32[16,16,256]{2,1,0:T(8,128)}, f32[16,16,256]{2,1,0:T(8,128)S(1)}, u32[]{:S(2)}, u32[]{:S(2)}) %collective-permute-start.7) | collective-permute-done | bytes 262176 | tf_op jit(solution)/shard_map/ppermute | solution.py:280
  30.7 0.0 collective-permute-done.2.refs_4_.after
  30.7 1.4 %collective-permute-done.3.refs_5_ = f32[2,4,16,256]{3,2,1,0:T(8,128)S(1)} collective-permute-done((f32[2,4,16,256]{3,2,1,0:T(8,128)S(1)}, f32[2,4,16,256]{3,2,1,0:T(8,128)S(1)}, u32[]{:S(2)}, u32[]{:S(2)}) %collective-permute-start.3) | collective-permute-done | bytes 131104 | tf_op jit(solution)/shard_map/ppermute | solution.py:267
  32.1 0.0 collective-permute-done.4.refs_6_
  32.1 0.0 collective-permute-done.5.refs_7_
  32.1 0.0 copy-start.1
  32.1 0.5 shard_map.149
  32.7 0.1 collective-permute-start.9
  32.8 3.1 %collective-permute-start.10 = (f32[2,4,16,256]{3,2,1,0:T(8,128)S(1)}, f32[2,4,16,256]{3,2,1,0:T(8,128)S(1)}, u32[]{:S(2)}, u32[]{:S(2)}) collective-permute-start(f32[2,4,16,256]{3,2,1,0:T(8,128)S(1)} %get-tuple-element.76), channel_id=1, source_target_pairs={{0,248},{8,16},{16,8},{24,32},{32,24},{40,48},{48,40},{56,64},{64,... | collective-permute-start | bytes 393224 | tf_op jit(solution)/shard_map/ppermute | solution.py:267
  35.8 0.0 collective-permute-start.11
  35.8 3.7 %collective-permute-start.12 = (f32[2,8,8,256]{3,2,1,0:T(8,128)S(1)}, f32[2,8,8,256]{3,2,1,0:T(8,128)S(1)}, u32[]{:S(2)}, u32[]{:S(2)}) collective-permute-start(f32[2,8,8,256]{3,2,1,0:T(8,128)S(1)} %get-tuple-element.78), channel_id=1, source_target_pairs={{0,7},{1,2},{2,1},{3,4},{4,3},{5,6},{6,5},{7,0},{8,15},{9,10},{10,... | collective-permute-start | bytes 393224 | tf_op jit(solution)/shard_map/ppermute | solution.py:268
  39.5 0.9 %shard_map.154 = (f32[64,256]{1,0:T(8,128)S(1)}, f32[64,256]{1,0:T(8,128)S(1)}) custom-call(f32[2,4,16,256]{3,2,1,0:T(8,128)S(1)} %collective-permute-done.2.refs_4_.after, f32[16,256]{1,0:T(8,128)S(1)} %get-tuple-element.60.moves.refs_8_.refs_13_, s32[32]{0:T(128)S(1)} %bitcast.1, f32[16,16,256]{2,1,0:T(8,128)S(1)} %copy-done.1, ...), custom_call_target="tpu_custom_call" | custom-call | flops 1048576 | bytes 1048576 | tf_op jit(solution)/shard_map/pallas_call | solution.py:26
  40.4 0.1 collective-permute-start.18
  40.5 4.8 %collective-permute-done.18.got = f32[64,256]{1,0:T(8,128)S(1)} collective-permute-done((f32[64,256]{1,0:T(8,128)S(1)}, f32[64,256]{1,0:T(8,128)S(1)}, u32[]{:S(2)}, u32[]{:S(2)}) %collective-permute-start.18) | collective-permute-done | bytes 65568 | tf_op jit(solution)/shard_map/ppermute | solution.py:313
  45.4 0.0 collective-permute-done.9.refs_4_.after
  45.4 0.3 collective-permute-start.19
  45.7 1.2 %shard_map.150 = (f32[16,16,256]{2,1,0:T(8,128)S(1)}, f32[16,16,256]{2,1,0:T(8,128)S(1)}) custom-call(f32[16,16,256]{2,1,0:T(8,128)S(1)} %get-tuple-element.71.s.refs_0_.refs_8_, f32[16,16,256]{2,1,0:T(8,128)S(1)} %get-tuple-element.72.r.refs_1_.refs_9_), custom_call_target="tpu_custom_call" | custom-call | flops 1048576 | bytes 1048576 | tf_op jit(solution)/shard_map/pallas_call | solution.py:26
  46.9 0.0 collective-permute-done.10.refs_5_.after
  46.9 0.0 collective-permute-done.12.refs_7_
  46.9 0.5 shard_map.151
  47.4 4.5 %collective-permute-start.13 = (f32[2,4,16,256]{3,2,1,0:T(8,128)S(1)}, f32[2,4,16,256]{3,2,1,0:T(8,128)S(1)}, u32[]{:S(2)}, u32[]{:S(2)}) collective-permute-start(f32[2,4,16,256]{3,2,1,0:T(8,128)S(1)} %get-tuple-element.85), channel_id=1, source_target_pairs={{0,8},{8,0},{16,24},{24,16},{32,40},{40,32},{48,56},{56,48},{64,72... | collective-permute-start | bytes 393224 | tf_op jit(solution)/shard_map/ppermute | solution.py:266
  51.9 0.0 collective-permute-start.14
  52.0 0.0 collective-permute-start.15
  52.0 1.7 %collective-permute-start.16 = (f32[2,8,8,256]{3,2,1,0:T(8,128)S(1)}, f32[2,8,8,256]{3,2,1,0:T(8,128)S(1)}, u32[]{:S(2)}, u32[]{:S(2)}) collective-permute-start(f32[2,8,8,256]{3,2,1,0:T(8,128)S(1)} %get-tuple-element.88), channel_id=1, source_target_pairs={{0,7},{1,2},{2,1},{3,4},{4,3},{5,6},{6,5},{7,0},{8,15},{9,10},{10,... | collective-permute-start | bytes 393224 | tf_op jit(solution)/shard_map/ppermute | solution.py:268
  53.7 0.0 collective-permute-done.19.got
  53.7 3.3 %collective-permute-start.25 = (f32[16,16,256]{2,1,0:T(8,128)S(1)}, f32[16,16,256]{2,1,0:T(8,128)S(1)}, u32[]{:S(2)}, u32[]{:S(2)}) collective-permute-start(f32[16,16,256]{2,1,0:T(8,128)S(1)} %shard_map.160), channel_id=1, source_target_pairs={{0,248},{8,0},{16,8},{24,16},{32,24},{40,32},{48,40},{56,48},{64,5... | collective-permute-start | bytes 786440 | tf_op jit(solution)/shard_map/ppermute | solution.py:316
  56.9 0.0 collective-permute-done.13.refs_4_.after
  56.9 1.3 %collective-permute-start.20 = (f32[16,256]{1,0:T(8,128)S(1)}, f32[16,256]{1,0:T(8,128)S(1)}, u32[]{:S(2)}, u32[]{:S(2)}) collective-permute-start(f32[16,256]{1,0:T(8,128)S(1)} %get-tuple-element.96), channel_id=1, source_target_pairs={{0,16},{8,24},{16,0},{24,8},{32,48},{40,56},{48,32},{56,40},{64,80... | collective-permute-start | bytes 49160 | tf_op jit(solution)/shard_map/ppermute | solution.py:313
  58.3 1.2 %shard_map.152 = (f32[16,16,256]{2,1,0:T(8,128)S(1)}, f32[16,16,256]{2,1,0:T(8,128)S(1)}) custom-call(f32[16,16,256]{2,1,0:T(8,128)S(1)} %get-tuple-element.81.s.refs_0_.refs_9_, f32[16,16,256]{2,1,0:T(8,128)S(1)} %get-tuple-element.82.r.refs_1_.refs_10_), custom_call_target="tpu_custom_call" | custom-call | flops 1048576 | bytes 1048576 | tf_op jit(solution)/shard_map/pallas_call | solution.py:26
  59.5 3.1 %collective-permute-done.14.refs_5_ = f32[2,4,16,256]{3,2,1,0:T(8,128)S(1)} collective-permute-done((f32[2,4,16,256]{3,2,1,0:T(8,128)S(1)}, f32[2,4,16,256]{3,2,1,0:T(8,128)S(1)}, u32[]{:S(2)}, u32[]{:S(2)}) %collective-permute-start.14) | collective-permute-done | bytes 131104 | tf_op jit(solution)/shard_map/ppermute | solution.py:267
  62.6 0.4 shard_map.153
  63.1 1.8 %collective-permute-start.17 = (f32[2,4,16,256]{3,2,1,0:T(8,128)S(1)}, f32[2,4,16,256]{3,2,1,0:T(8,128)S(1)}, u32[]{:S(2)}, u32[]{:S(2)}) collective-permute-start(f32[2,4,16,256]{3,2,1,0:T(8,128)S(1)} %get-tuple-element.90), channel_id=1, source_target_pairs={{0,8},{8,0},{16,24},{24,16},{32,40},{40,32},{48,56},{56,48},{64,72... | collective-permute-start | bytes 393224 | tf_op jit(solution)/shard_map/ppermute | solution.py:266
  64.9 0.9 %collective-permute-start.22 = (f32[2,4,16,256]{3,2,1,0:T(8,128)S(1)}, f32[2,4,16,256]{3,2,1,0:T(8,128)S(1)}, u32[]{:S(2)}, u32[]{:S(2)}) collective-permute-start(f32[2,4,16,256]{3,2,1,0:T(8,128)S(1)} %get-tuple-element.105), channel_id=1, source_target_pairs={{0,248},{8,16},{16,8},{24,32},{32,24},{40,48},{48,40},{56,64},{64,... | collective-permute-start | bytes 393224 | tf_op jit(solution)/shard_map/ppermute | solution.py:267
  65.8 1.3 %collective-permute-start.23 = (f32[2,8,8,256]{3,2,1,0:T(8,128)S(1)}, f32[2,8,8,256]{3,2,1,0:T(8,128)S(1)}, u32[]{:S(2)}, u32[]{:S(2)}) collective-permute-start(f32[2,8,8,256]{3,2,1,0:T(8,128)S(1)} %get-tuple-element.106), channel_id=1, source_target_pairs={{0,1},{1,0},{2,3},{3,2},{4,5},{5,4},{6,7},{7,6},{8,9},{9,8},{10,11... | collective-permute-start | bytes 393224 | tf_op jit(solution)/shard_map/ppermute | solution.py:269
  67.1 0.0 collective-permute-done.20.got
  67.1 1.4 %collective-permute-start.24 = (f32[2,8,8,256]{3,2,1,0:T(8,128)S(1)}, f32[2,8,8,256]{3,2,1,0:T(8,128)S(1)}, u32[]{:S(2)}, u32[]{:S(2)}) collective-permute-start(f32[2,8,8,256]{3,2,1,0:T(8,128)S(1)} %get-tuple-element.107), channel_id=1, source_target_pairs={{0,7},{1,2},{2,1},{3,4},{4,3},{5,6},{6,5},{7,0},{8,15},{9,10},{10,... | collective-permute-start | bytes 393224 | tf_op jit(solution)/shard_map/ppermute | solution.py:268
  68.5 0.0 collective-permute-done.17.after.refs_5_
  68.5 1.6 %collective-permute-start.21 = (f32[8,256]{1,0:T(8,128)S(1)}, f32[8,256]{1,0:T(8,128)S(1)}, u32[]{:S(2)}, u32[]{:S(2)}) collective-permute-start(f32[8,256]{1,0:T(8,128)S(1)} %get-tuple-element.98), channel_id=1, source_target_pairs={{0,8},{8,0},{16,24},{24,16},{32,40},{40,32},{48,56},{56,48},{64,72... | collective-permute-start | bytes 24584 | tf_op jit(solution)/shard_map/ppermute | solution.py:313
  70.1 1.2 %shard_map.159 = (f32[16,16,256]{2,1,0:T(8,128)S(1)}, f32[16,16,256]{2,1,0:T(8,128)S(1)}) custom-call(f32[16,16,256]{2,1,0:T(8,128)S(1)} %get-tuple-element.101.s.refs_1_, f32[16,16,256]{2,1,0:T(8,128)S(1)} %get-tuple-element.102.r.refs_2_), custom_call_target="tpu_custom_call" | custom-call | flops 1048576 | bytes 1048576 | tf_op jit(solution)/shard_map/pallas_call | solution.py:26
  71.3 1.7 %shard_map.158 = (f32[16,16,256]{2,1,0:T(8,128)}, f32[8,128]{1,0:T(8,128)S(1)}) custom-call(s32[32]{0:T(128)S(1)} %bitcast.2, f32[8,256]{1,0:T(8,128)S(1)} %get-tuple-element.97.held, f32[8,256]{1,0:T(8,128)S(1)} %collective-permute-done.21.got, f32[16,16,256]{2,1,0:T(8,128)S(1)} %copy-done.6), custom_call_target="tpu_custom_call" | custom-call | flops 1048576 | bytes 1048576 | tf_op jit(solution)/shard_map/pallas_call | solution.py:26
  73.0 3.5 %collective-permute-done.23.refs_7_ = f32[2,8,8,256]{3,2,1,0:T(8,128)S(1)} collective-permute-done((f32[2,8,8,256]{3,2,1,0:T(8,128)S(1)}, f32[2,8,8,256]{3,2,1,0:T(8,128)S(1)}, u32[]{:S(2)}, u32[]{:S(2)}) %collective-permute-start.23) | collective-permute-done | bytes 131104 | tf_op jit(solution)/shard_map/ppermute | solution.py:269
  76.5 0.0 collective-permute-done.24.refs_8_
  76.5 1.3 %shard_map.161 = (f32[16,16,256]{2,1,0:T(8,128)}, f32[16,16,256]{2,1,0:T(8,128)}, f32[16,16,256]{2,1,0:T(8,128)}, f32[16,16,256]{2,1,0:T(8,128)}, f32[16,16,256]{2,1,0:T(8,128)}) custom-call(f32[8,128]{1,0:T(8,128)S(1)} %get-tuple-element.100.refs_0_, f32[16,16,256]{2,1,0:T(8,128)S(1)} %get-tuple-element.101.s.refs_1_, ...), custom_call_target="tpu_custom_call" | custom-call | flops 1048576 | bytes 1048576 | tf_op jit(solution)/shard_map/pallas_call | solution.py:26
  (29 shorter events, 0.1 us)
Async XLA Ops:
  0.6 14.4 %collective-permute-start = (f32[16,16,256]{2,1,0:T(8,128)}, f32[16,16,256]{2,1,0:T(8,128)S(1)}, u32[]{:S(2)}, u32[]{:S(2)}) collective-permute-start(f32[16,16,256]{2,1,0:T(8,128)} %s.1), channel_id=1, source_target_pairs={{0,248},{8,0},{16,8},{24,16},{32,24},{40,32},{48,40},{56,48},{64,5... | collective-permute-start | bytes 786440 | tf_op jit(solution)/shard_map/ppermute | solution.py:277
  4.0 11.1 %collective-permute-start.1 = (f32[16,16,256]{2,1,0:T(8,128)}, f32[16,16,256]{2,1,0:T(8,128)S(1)}, u32[]{:S(2)}, u32[]{:S(2)}) collective-permute-start(f32[16,16,256]{2,1,0:T(8,128)} %r.1), channel_id=1, source_target_pairs={{0,248},{8,0},{16,8},{24,16},{32,24},{40,32},{48,40},{56,48},{64,5... | collective-permute-start | bytes 786440 | tf_op jit(solution)/shard_map/ppermute | solution.py:278
  10.1 0.9 %copy-start = (f32[16,16,256]{2,1,0:T(8,128)S(1)}, f32[16,16,256]{2,1,0:T(8,128)}, u32[]{:S(2)}) copy-start(f32[16,16,256]{2,1,0:T(8,128)} %refs_14_.1) | copy-start | bytes 786436
  11.1 0.9 %copy-start.2 = (f32[16,16,256]{2,1,0:T(8,128)S(1)}, f32[16,16,256]{2,1,0:T(8,128)}, u32[]{:S(2)}) copy-start(f32[16,16,256]{2,1,0:T(8,128)} %refs_11_.1) | copy-start | bytes 786436
  12.0 0.9 %copy-start.7 = (f32[16,16,256]{2,1,0:T(8,128)S(1)}, f32[16,16,256]{2,1,0:T(8,128)}, u32[]{:S(2)}) copy-start(f32[16,16,256]{2,1,0:T(8,128)} %refs_9_.1) | copy-start | bytes 786436
  12.0 1.7 %copy-start.4 = (f32[16,16,256]{2,1,0:T(8,128)S(1)}, f32[16,16,256]{2,1,0:T(8,128)}, u32[]{:S(2)}) copy-start(f32[16,16,256]{2,1,0:T(8,128)} %s.1) | copy-start | bytes 786436
  12.0 1.7 %copy-start.5 = (f32[16,16,256]{2,1,0:T(8,128)S(1)}, f32[16,16,256]{2,1,0:T(8,128)}, u32[]{:S(2)}) copy-start(f32[16,16,256]{2,1,0:T(8,128)} %r.1) | copy-start | bytes 786436
  12.1 7.4 %collective-permute-start.8 = (f32[16,16,256]{2,1,0:T(8,128)S(1)}, f32[16,16,256]{2,1,0:T(8,128)S(1)}, u32[]{:S(2)}, u32[]{:S(2)}) collective-permute-start(f32[16,16,256]{2,1,0:T(8,128)S(1)} %shard_map.148), channel_id=1, source_target_pairs={{0,248},{8,0},{16,8},{24,16},{32,24},{40,32},{48,40},{56,48},{64,5... | collective-permute-start | bytes 786440 | tf_op jit(solution)/shard_map/ppermute | solution.py:282
  13.0 9.3 %collective-permute-start.6 = (f32[16,16,256]{2,1,0:T(8,128)S(1)}, f32[16,16,256]{2,1,0:T(8,128)S(1)}, u32[]{:S(2)}, u32[]{:S(2)}) collective-permute-start(f32[16,16,256]{2,1,0:T(8,128)S(1)} %copy-done.7), channel_id=1, source_target_pairs={{0,248},{8,0},{16,8},{24,16},{32,24},{40,32},{48,40},{56,48},{64,5... | collective-permute-start | bytes 786440 | tf_op jit(solution)/shard_map/ppermute | solution.py:279
  13.7 17.0 %collective-permute-start.7 = (f32[16,16,256]{2,1,0:T(8,128)}, f32[16,16,256]{2,1,0:T(8,128)S(1)}, u32[]{:S(2)}, u32[]{:S(2)}) collective-permute-start(f32[16,16,256]{2,1,0:T(8,128)} %refs_10_.1), channel_id=1, source_target_pairs={{0,248},{8,0},{16,8},{24,16},{32,24},{40,32},{48,40},{56,48},{64,5... | collective-permute-start | bytes 786440 | tf_op jit(solution)/shard_map/ppermute | solution.py:280
  13.8 0.7 copy-start.11
  15.0 17.1 %copy-start.9 = (f32[16,16,256]{2,1,0:T(8,128)S(1)}, f32[16,16,256]{2,1,0:T(8,128)}, u32[]{:S(2)}) copy-start(f32[16,16,256]{2,1,0:T(8,128)} %refs_12_.1) | copy-start | bytes 786436
  15.2 15.5 %collective-permute-start.2 = (f32[2,4,16,256]{3,2,1,0:T(8,128)S(1)}, f32[2,4,16,256]{3,2,1,0:T(8,128)S(1)}, u32[]{:S(2)}, u32[]{:S(2)}) collective-permute-start(f32[2,4,16,256]{3,2,1,0:T(8,128)S(1)} %get-tuple-element.67), channel_id=1, source_target_pairs={{0,8},{8,0},{16,24},{24,16},{32,40},{40,32},{48,56},{56,48},{64,72... | collective-permute-start | bytes 393224 | tf_op jit(solution)/shard_map/ppermute | solution.py:266
  17.9 14.2 %collective-permute-start.3 = (f32[2,4,16,256]{3,2,1,0:T(8,128)S(1)}, f32[2,4,16,256]{3,2,1,0:T(8,128)S(1)}, u32[]{:S(2)}, u32[]{:S(2)}) collective-permute-start(f32[2,4,16,256]{3,2,1,0:T(8,128)S(1)} %get-tuple-element.68), channel_id=1, source_target_pairs={{0,248},{8,16},{16,8},{24,32},{32,24},{40,48},{48,40},{56,64},{64,... | collective-permute-start | bytes 393224 | tf_op jit(solution)/shard_map/ppermute | solution.py:267
  19.5 12.6 %collective-permute-start.4 = (f32[2,8,8,256]{3,2,1,0:T(8,128)S(1)}, f32[2,8,8,256]{3,2,1,0:T(8,128)S(1)}, u32[]{:S(2)}, u32[]{:S(2)}) collective-permute-start(f32[2,8,8,256]{3,2,1,0:T(8,128)S(1)} %get-tuple-element.69), channel_id=1, source_target_pairs={{0,1},{1,0},{2,3},{3,2},{4,5},{5,4},{6,7},{7,6},{8,9},{9,8},{10,11... | collective-permute-start | bytes 393224 | tf_op jit(solution)/shard_map/ppermute | solution.py:269
  22.3 9.8 %collective-permute-start.5 = (f32[2,8,8,256]{3,2,1,0:T(8,128)S(1)}, f32[2,8,8,256]{3,2,1,0:T(8,128)S(1)}, u32[]{:S(2)}, u32[]{:S(2)}) collective-permute-start(f32[2,8,8,256]{3,2,1,0:T(8,128)S(1)} %get-tuple-element.70), channel_id=1, source_target_pairs={{0,7},{1,2},{2,1},{3,4},{4,3},{5,6},{6,5},{7,0},{8,15},{9,10},{10,... | collective-permute-start | bytes 393224 | tf_op jit(solution)/shard_map/ppermute | solution.py:268
  24.9 7.3 %copy-start.3 = (f32[16,16,256]{2,1,0:T(8,128)S(1)}, f32[16,16,256]{2,1,0:T(8,128)}, u32[]{:S(2)}) copy-start(f32[16,16,256]{2,1,0:T(8,128)} %refs_11_.1) | copy-start | bytes 786436
  24.9 7.3 %copy-start.8 = (f32[16,16,256]{2,1,0:T(8,128)S(1)}, f32[16,16,256]{2,1,0:T(8,128)}, u32[]{:S(2)}) copy-start(f32[16,16,256]{2,1,0:T(8,128)} %refs_10_.1) | copy-start | bytes 786436
  32.1 7.4 %copy-start.1 = (f32[16,16,256]{2,1,0:T(8,128)S(1)}, f32[16,16,256]{2,1,0:T(8,128)}, u32[]{:S(2)}) copy-start(f32[16,16,256]{2,1,0:T(8,128)} %refs_14_.1) | copy-start | bytes 786436
  32.7 12.7 %collective-permute-start.9 = (f32[2,4,16,256]{3,2,1,0:T(8,128)S(1)}, f32[2,4,16,256]{3,2,1,0:T(8,128)S(1)}, u32[]{:S(2)}, u32[]{:S(2)}) collective-permute-start(f32[2,4,16,256]{3,2,1,0:T(8,128)S(1)} %get-tuple-element.75), channel_id=1, source_target_pairs={{0,8},{8,0},{16,24},{24,16},{32,40},{40,32},{48,56},{56,48},{64,72... | collective-permute-start | bytes 393224 | tf_op jit(solution)/shard_map/ppermute | solution.py:266
  32.8 14.1 %collective-permute-start.10 = (f32[2,4,16,256]{3,2,1,0:T(8,128)S(1)}, f32[2,4,16,256]{3,2,1,0:T(8,128)S(1)}, u32[]{:S(2)}, u32[]{:S(2)}) collective-permute-start(f32[2,4,16,256]{3,2,1,0:T(8,128)S(1)} %get-tuple-element.76), channel_id=1, source_target_pairs={{0,248},{8,16},{16,8},{24,32},{32,24},{40,48},{48,40},{56,64},{64,... | collective-permute-start | bytes 393224 | tf_op jit(solution)/shard_map/ppermute | solution.py:267
  35.8 11.1 %collective-permute-start.11 = (f32[2,8,8,256]{3,2,1,0:T(8,128)S(1)}, f32[2,8,8,256]{3,2,1,0:T(8,128)S(1)}, u32[]{:S(2)}, u32[]{:S(2)}) collective-permute-start(f32[2,8,8,256]{3,2,1,0:T(8,128)S(1)} %get-tuple-element.77), channel_id=1, source_target_pairs={{0,1},{1,0},{2,3},{3,2},{4,5},{5,4},{6,7},{7,6},{8,9},{9,8},{10,11... | collective-permute-start | bytes 393224 | tf_op jit(solution)/shard_map/ppermute | solution.py:269
  35.8 3.7 %copy-start.10 = (s32[1,32]{1,0:T(1,128)S(1)}, s32[1,32]{1,0:T(1,128)}, u32[]{:S(2)}) copy-start(s32[1,32]{1,0:T(1,128)} %param.19) | copy-start | bytes 388
  35.8 11.1 %collective-permute-start.12 = (f32[2,8,8,256]{3,2,1,0:T(8,128)S(1)}, f32[2,8,8,256]{3,2,1,0:T(8,128)S(1)}, u32[]{:S(2)}, u32[]{:S(2)}) collective-permute-start(f32[2,8,8,256]{3,2,1,0:T(8,128)S(1)} %get-tuple-element.78), channel_id=1, source_target_pairs={{0,7},{1,2},{2,1},{3,4},{4,3},{5,6},{6,5},{7,0},{8,15},{9,10},{10,... | collective-permute-start | bytes 393224 | tf_op jit(solution)/shard_map/ppermute | solution.py:268
  40.4 4.9 %collective-permute-start.18 = (f32[64,256]{1,0:T(8,128)S(1)}, f32[64,256]{1,0:T(8,128)S(1)}, u32[]{:S(2)}, u32[]{:S(2)}) collective-permute-start(f32[64,256]{1,0:T(8,128)S(1)} %get-tuple-element.92), channel_id=1, source_target_pairs={{0,64},{8,72},{16,80},{24,88},{32,96},{40,104},{48,112},{56,120},{... | collective-permute-start | bytes 196616 | tf_op jit(solution)/shard_map/ppermute | solution.py:313
  45.4 8.3 %collective-permute-start.19 = (f32[32,256]{1,0:T(8,128)S(1)}, f32[32,256]{1,0:T(8,128)S(1)}, u32[]{:S(2)}, u32[]{:S(2)}) collective-permute-start(f32[32,256]{1,0:T(8,128)S(1)} %get-tuple-element.94), channel_id=1, source_target_pairs={{0,32},{8,40},{16,48},{24,56},{32,0},{40,8},{48,16},{56,24},{64,96... | collective-permute-start | bytes 98312 | tf_op jit(solution)/shard_map/ppermute | solution.py:313
  47.4 9.5 %collective-permute-start.13 = (f32[2,4,16,256]{3,2,1,0:T(8,128)S(1)}, f32[2,4,16,256]{3,2,1,0:T(8,128)S(1)}, u32[]{:S(2)}, u32[]{:S(2)}) collective-permute-start(f32[2,4,16,256]{3,2,1,0:T(8,128)S(1)} %get-tuple-element.85), channel_id=1, source_target_pairs={{0,8},{8,0},{16,24},{24,16},{32,40},{40,32},{48,56},{56,48},{64,72... | collective-permute-start | bytes 393224 | tf_op jit(solution)/shard_map/ppermute | solution.py:266
  51.9 10.7 %collective-permute-start.14 = (f32[2,4,16,256]{3,2,1,0:T(8,128)S(1)}, f32[2,4,16,256]{3,2,1,0:T(8,128)S(1)}, u32[]{:S(2)}, u32[]{:S(2)}) collective-permute-start(f32[2,4,16,256]{3,2,1,0:T(8,128)S(1)} %get-tuple-element.86), channel_id=1, source_target_pairs={{0,248},{8,16},{16,8},{24,32},{32,24},{40,48},{48,40},{56,64},{64,... | collective-permute-start | bytes 393224 | tf_op jit(solution)/shard_map/ppermute | solution.py:267
  52.0 10.7 %collective-permute-start.15 = (f32[2,8,8,256]{3,2,1,0:T(8,128)S(1)}, f32[2,8,8,256]{3,2,1,0:T(8,128)S(1)}, u32[]{:S(2)}, u32[]{:S(2)}) collective-permute-start(f32[2,8,8,256]{3,2,1,0:T(8,128)S(1)} %get-tuple-element.87), channel_id=1, source_target_pairs={{0,1},{1,0},{2,3},{3,2},{4,5},{5,4},{6,7},{7,6},{8,9},{9,8},{10,11... | collective-permute-start | bytes 393224 | tf_op jit(solution)/shard_map/ppermute | solution.py:269
  52.0 10.7 %collective-permute-start.16 = (f32[2,8,8,256]{3,2,1,0:T(8,128)S(1)}, f32[2,8,8,256]{3,2,1,0:T(8,128)S(1)}, u32[]{:S(2)}, u32[]{:S(2)}) collective-permute-start(f32[2,8,8,256]{3,2,1,0:T(8,128)S(1)} %get-tuple-element.88), channel_id=1, source_target_pairs={{0,7},{1,2},{2,1},{3,4},{4,3},{5,6},{6,5},{7,0},{8,15},{9,10},{10,... | collective-permute-start | bytes 393224 | tf_op jit(solution)/shard_map/ppermute | solution.py:268
  53.7 19.3 %collective-permute-start.25 = (f32[16,16,256]{2,1,0:T(8,128)S(1)}, f32[16,16,256]{2,1,0:T(8,128)S(1)}, u32[]{:S(2)}, u32[]{:S(2)}) collective-permute-start(f32[16,16,256]{2,1,0:T(8,128)S(1)} %shard_map.160), channel_id=1, source_target_pairs={{0,248},{8,0},{16,8},{24,16},{32,24},{40,32},{48,40},{56,48},{64,5... | collective-permute-start | bytes 786440 | tf_op jit(solution)/shard_map/ppermute | solution.py:316
  56.9 10.2 %collective-permute-start.20 = (f32[16,256]{1,0:T(8,128)S(1)}, f32[16,256]{1,0:T(8,128)S(1)}, u32[]{:S(2)}, u32[]{:S(2)}) collective-permute-start(f32[16,256]{1,0:T(8,128)S(1)} %get-tuple-element.96), channel_id=1, source_target_pairs={{0,16},{8,24},{16,0},{24,8},{32,48},{40,56},{48,32},{56,40},{64,80... | collective-permute-start | bytes 49160 | tf_op jit(solution)/shard_map/ppermute | solution.py:313
  63.1 5.4 %collective-permute-start.17 = (f32[2,4,16,256]{3,2,1,0:T(8,128)S(1)}, f32[2,4,16,256]{3,2,1,0:T(8,128)S(1)}, u32[]{:S(2)}, u32[]{:S(2)}) collective-permute-start(f32[2,4,16,256]{3,2,1,0:T(8,128)S(1)} %get-tuple-element.90), channel_id=1, source_target_pairs={{0,8},{8,0},{16,24},{24,16},{32,40},{40,32},{48,56},{56,48},{64,72... | collective-permute-start | bytes 393224 | tf_op jit(solution)/shard_map/ppermute | solution.py:266
  64.9 8.1 %collective-permute-start.22 = (f32[2,4,16,256]{3,2,1,0:T(8,128)S(1)}, f32[2,4,16,256]{3,2,1,0:T(8,128)S(1)}, u32[]{:S(2)}, u32[]{:S(2)}) collective-permute-start(f32[2,4,16,256]{3,2,1,0:T(8,128)S(1)} %get-tuple-element.105), channel_id=1, source_target_pairs={{0,248},{8,16},{16,8},{24,32},{32,24},{40,48},{48,40},{56,64},{64,... | collective-permute-start | bytes 393224 | tf_op jit(solution)/shard_map/ppermute | solution.py:267
  65.8 10.7 %collective-permute-start.23 = (f32[2,8,8,256]{3,2,1,0:T(8,128)S(1)}, f32[2,8,8,256]{3,2,1,0:T(8,128)S(1)}, u32[]{:S(2)}, u32[]{:S(2)}) collective-permute-start(f32[2,8,8,256]{3,2,1,0:T(8,128)S(1)} %get-tuple-element.106), channel_id=1, source_target_pairs={{0,1},{1,0},{2,3},{3,2},{4,5},{5,4},{6,7},{7,6},{8,9},{9,8},{10,11... | collective-permute-start | bytes 393224 | tf_op jit(solution)/shard_map/ppermute | solution.py:269
  67.1 9.4 %collective-permute-start.24 = (f32[2,8,8,256]{3,2,1,0:T(8,128)S(1)}, f32[2,8,8,256]{3,2,1,0:T(8,128)S(1)}, u32[]{:S(2)}, u32[]{:S(2)}) collective-permute-start(f32[2,8,8,256]{3,2,1,0:T(8,128)S(1)} %get-tuple-element.107), channel_id=1, source_target_pairs={{0,7},{1,2},{2,1},{3,4},{4,3},{5,6},{6,5},{7,0},{8,15},{9,10},{10,... | collective-permute-start | bytes 393224 | tf_op jit(solution)/shard_map/ppermute | solution.py:268
  68.5 2.8 %collective-permute-start.21 = (f32[8,256]{1,0:T(8,128)S(1)}, f32[8,256]{1,0:T(8,128)S(1)}, u32[]{:S(2)}, u32[]{:S(2)}) collective-permute-start(f32[8,256]{1,0:T(8,128)S(1)} %get-tuple-element.98), channel_id=1, source_target_pairs={{0,8},{8,0},{16,24},{24,16},{32,40},{40,32},{48,56},{56,48},{64,72... | collective-permute-start | bytes 24584 | tf_op jit(solution)/shard_map/ppermute | solution.py:313
  70.1 1.2 %copy-start.6 = (f32[16,16,256]{2,1,0:T(8,128)S(1)}, f32[16,16,256]{2,1,0:T(8,128)}, u32[]{:S(2)}) copy-start(f32[16,16,256]{2,1,0:T(8,128)} %base.1) | copy-start | bytes 786436

commit v4 on v3

--- a/solution.py
+++ b/solution.py
@@ -12,6 +12,7 @@
 F32 = jnp.float32
 HIGHEST = lax.Precision.HIGHEST
 LIMIT = 12 * 1024 * 1024
+WAITS = (1, 0, 0, 1)
 
 
 def sds(*shape):
@@ -141,8 +142,7 @@
     refs = list(refs)
     take = lambda n: [refs.pop(0) for _ in range(n)]
     last = step == STEPS - 1
-    if last:
-        take(1)
+    take(WAITS[step])
     s, r, s_lap, r_lap = take(4)
     halos = take(4)
     if step == 0:
@@ -316,7 +316,7 @@
             image_come = lax.ppermute(image_send, "gx", west)
         s_lap, r_lap = call(interior_kernel, [tile, tile], scratch, s, r)
         ins = [s, r, s_lap, r_lap, *halos]
-        outs, after = [tile] * 3, ()
+        outs = [tile] * 3
         if step == 0:
             ins += [mask, src_prev, rcv_prev, courant, vel_entering]
             ins += [sp_come, rp_come, vel_come]
@@ -327,11 +327,16 @@
                 gather_kernel, [tile, sds(8, 128)], [], owner, low, got, global_image
             )
             ins += [mask, image, image_come]
-            outs, after = outs + [tile] * 2, (token,)
+            outs = outs + [tile] * 2
         else:
             outs = outs + faces
         if step == 0:
             outs = outs + [tile]
+        after = ()
+        if step == 0:
+            after = (got,)
+        if step == 3:
+            after = (token,)
         new = call(functools.partial(update_kernel, step), outs, [], *ins, after=after)
         if last:
             s_new, r_new, picture, s, r = new

time: 78.2 us -> 74.3 us (0.950)
  waiting for transfers between devices: 20.8 us -> 14.3 us
  starting transfers between devices: 42.4 us -> 45.2 us
    ppermute x4, waiting for transfers between devices: 4.83 us -> 0.01 us  [body(): got = lax.ppermute(high, 'gx', [(i, i ^ 8 >> step) for i in range(n)])]
    ppermute x4, starting transfers between devices: 9.29 us -> 12.6 us  [swap(): yo = lax.ppermute(yo, 'gy', odd_y)]
    ppermute x1, waiting for transfers between devices: 2.41 us -> 0.01 us  [body(): sp_come = lax.ppermute(src_prev, 'gx', west)]
    ppermute x4, waiting for transfers between devices: 4.51 us -> 6.47 us  [swap(): od = lax.ppermute(od, 'gx', odd_x)]
    ppermute x4, waiting for transfers between devices: 3.5 us -> 1.63 us  [swap(): y1 = lax.ppermute(y1, 'gy', pair_y)]
    ppermute x4, starting transfers between devices: 9.16 us -> 7.47 us  [swap(): x1 = lax.ppermute(x1, 'gx', pair_x)]
    ppermute x4, starting transfers between devices: 3.31 us -> 4.85 us  [body(): got = lax.ppermute(high, 'gx', [(i, i ^ 8 >> step) for i in range(n)])]
    ppermute x4, starting transfers between devices: 4.59 us -> 3.1 us  [swap(): od = lax.ppermute(od, 'gx', odd_x)]
  transfers between devices with their start and end apart: 26 -> 26, of which waited for: 7 -> 6; matrix products, arithmetic and copies ran while one was open for 0% -> 0% of each run, Pallas kernels for 12% -> 12%
where the time goes in v4:
time: 74.3 us; the launch traced here: 74.1 us
  starting transfers between devices  45.2 us (61%)
  waiting for transfers between devices  14.3 us (19%)
  Pallas kernels  11 us (15%)
  local copies, waits for them, and re-layouts  2.75 us (4%)
  between operations  0.89 us (1%)
    ppermute x4, starting transfers between devices, swap(): yo = lax.ppermute(yo, 'gy', odd_y)  12.6 us
    pallas_call x17, Pallas kernels, call(): pl.pallas_call(kernel, out_shape=outs, in_specs=specs, out_specs=[pl.Bloc...  11 us
    ppermute x4, starting transfers between devices, swap(): x1 = lax.ppermute(x1, 'gx', pair_x)  7.47 us
    ppermute x4, waiting for transfers between devices, swap(): od = lax.ppermute(od, 'gx', odd_x)  6.47 us
    ppermute x1, starting transfers between devices, body(): r_come = lax.ppermute(rcv_cur, 'gx', west)  6.19 us
    ppermute x1, waiting for transfers between devices, body(): rp_come = lax.ppermute(rcv_prev, 'gx', west)  5.25 us
    ppermute x4, starting transfers between devices, body(): got = lax.ppermute(high, 'gx', [(i, i ^ 8 >> step) for i in range(n)])  4.85 us
    ppermute x1, starting transfers between devices, body(): image_come = lax.ppermute(image_send, 'gx', west)  4.59 us
  transfers between devices with their start and end apart: 26, of which 6 were waited for; matrix products, arithmetic and copies ran while one was open for 0% of the time, Pallas kernels for 12%

profile of v4, /device:TPU:1, one launch (start us, length us, event | category | flops | bytes accessed | tf_op | source)
XLA Modules:
  0.0 74.1 jit_solution(10545157020521786395)
XLA Ops:
  0.6 3.3 %collective-permute-start = (f32[16,16,256]{2,1,0:T(8,128)}, f32[16,16,256]{2,1,0:T(8,128)S(1)}, u32[]{:S(2)}, u32[]{:S(2)}) collective-permute-start(f32[16,16,256]{2,1,0:T(8,128)} %s.1), channel_id=1, source_target_pairs={{0,248},{8,0},{16,8},{24,16},{32,24},{40,32},{48,40},{56,48},{64,5... | collective-permute-start | bytes 786440 | tf_op jit(solution)/shard_map/ppermute | solution.py:277
  4.0 6.2 %collective-permute-start.1 = (f32[16,16,256]{2,1,0:T(8,128)}, f32[16,16,256]{2,1,0:T(8,128)S(1)}, u32[]{:S(2)}, u32[]{:S(2)}) collective-permute-start(f32[16,16,256]{2,1,0:T(8,128)} %r.1), channel_id=1, source_target_pairs={{0,248},{8,0},{16,8},{24,16},{32,24},{40,32},{48,40},{56,48},{64,5... | collective-permute-start | bytes 786440 | tf_op jit(solution)/shard_map/ppermute | solution.py:278
  10.1 0.9 %copy-done = f32[16,16,256]{2,1,0:T(8,128)S(1)} copy-done((f32[16,16,256]{2,1,0:T(8,128)S(1)}, f32[16,16,256]{2,1,0:T(8,128)}, u32[]{:S(2)}) %copy-start) | copy-done | bytes 262168
  11.1 0.9 %copy-done.2 = f32[16,16,256]{2,1,0:T(8,128)S(1)} copy-done((f32[16,16,256]{2,1,0:T(8,128)S(1)}, f32[16,16,256]{2,1,0:T(8,128)}, u32[]{:S(2)}) %copy-start.2) | copy-done | bytes 262168
  12.1 0.8 %collective-permute-start.3 = (f32[16,16,256]{2,1,0:T(8,128)S(1)}, f32[16,16,256]{2,1,0:T(8,128)S(1)}, u32[]{:S(2)}, u32[]{:S(2)}) collective-permute-start(f32[16,16,256]{2,1,0:T(8,128)S(1)} %shard_map.147), channel_id=1, source_target_pairs={{0,248},{8,0},{16,8},{24,16},{32,24},{40,32},{48,40},{56,48},{64,5... | collective-permute-start | bytes 786440 | tf_op jit(solution)/shard_map/ppermute | solution.py:282
  12.8 0.2 copy-done.7
  13.0 0.7 collective-permute-start.8
  13.7 0.1 collective-permute-start.9
  13.8 0.7 copy-done.11
  14.4 0.6 shard_map.145
  15.0 0.0 collective-permute-done.s_in
  15.0 0.0 collective-permute-done.1.r_in
  15.0 0.0 copy-start.1
  15.0 0.2 shard_map.146
  15.2 2.7 %collective-permute-start.2 = (f32[2,4,16,256]{3,2,1,0:T(8,128)S(1)}, f32[2,4,16,256]{3,2,1,0:T(8,128)S(1)}, u32[]{:S(2)}, u32[]{:S(2)}) collective-permute-start(f32[2,4,16,256]{3,2,1,0:T(8,128)S(1)} %get-tuple-element.63), channel_id=1, source_target_pairs={{0,8},{8,0},{16,24},{24,16},{32,40},{40,32},{48,56},{56,48},{64,72... | collective-permute-start | bytes 393224 | tf_op jit(solution)/shard_map/ppermute | solution.py:266
  17.9 0.7 collective-permute-start.5
  18.6 0.9 %collective-permute-done.3.come.refs_16_ = f32[16,16,256]{2,1,0:T(8,128)S(1)} collective-permute-done((f32[16,16,256]{2,1,0:T(8,128)S(1)}, f32[16,16,256]{2,1,0:T(8,128)S(1)}, u32[]{:S(2)}, u32[]{:S(2)}) %collective-permute-start.3) | collective-permute-done | bytes 262176 | tf_op jit(solution)/shard_map/ppermute | solution.py:282
  19.5 0.4 collective-permute-start.6
  19.9 0.0 collective-permute-done.2.after.refs_5_
  19.9 3.3 %collective-permute-start.7 = (f32[2,8,8,256]{3,2,1,0:T(8,128)S(1)}, f32[2,8,8,256]{3,2,1,0:T(8,128)S(1)}, u32[]{:S(2)}, u32[]{:S(2)}) collective-permute-start(f32[2,8,8,256]{3,2,1,0:T(8,128)S(1)} %get-tuple-element.71), channel_id=1, source_target_pairs={{0,7},{1,2},{2,1},{3,4},{4,3},{5,6},{6,5},{7,0},{8,15},{9,10},{10,... | collective-permute-start | bytes 393224 | tf_op jit(solution)/shard_map/ppermute | solution.py:268
  23.1 0.9 %shard_map.148 = (f32[64,256]{1,0:T(8,128)S(1)}, f32[64,256]{1,0:T(8,128)S(1)}) custom-call(f32[2,4,16,256]{3,2,1,0:T(8,128)S(1)} %collective-permute-done.2.after.refs_5_, f32[16,256]{1,0:T(8,128)S(1)} %get-tuple-element.60.moves.refs_9_.refs_13_, s32[32]{0:T(128)S(1)} %bitcast.1, f32[16,16,256]{2,1,0:T(8,128)S(1)} %copy-done.1, ...), custom_call_target="tpu_custom_call" | custom-call | flops 1048576 | bytes 1048576 | tf_op jit(solution)/shard_map/pallas_call | solution.py:27
  24.1 0.0 collective-permute-done.8.refs_14_
  24.1 0.1 collective-permute-start.4
  24.2 0.0 copy-start.3
  24.2 0.0 copy-start.8
  24.2 1.2 %shard_map.149 = (f32[16,16,256]{2,1,0:T(8,128)S(1)}, f32[16,16,256]{2,1,0:T(8,128)S(1)}) custom-call(f32[16,16,256]{2,1,0:T(8,128)S(1)} %get-tuple-element.65.s.refs_1_.refs_8_, f32[16,16,256]{2,1,0:T(8,128)S(1)} %get-tuple-element.66.r.refs_2_.refs_9_), custom_call_target="tpu_custom_call" | custom-call | flops 1048576 | bytes 1048576 | tf_op jit(solution)/shard_map/pallas_call | solution.py:27
  25.5 5.2 %collective-permute-done.9.refs_15_ = f32[16,16,256]{2,1,0:T(8,128)S(1)} collective-permute-done((f32[16,16,256]{2,1,0:T(8,128)}, f32[16,16,256]{2,1,0:T(8,128)S(1)}, u32[]{:S(2)}, u32[]{:S(2)}) %collective-permute-start.9) | collective-permute-done | bytes 262176 | tf_op jit(solution)/shard_map/ppermute | solution.py:280
  30.7 1.4 %collective-permute-done.5.refs_6_ = f32[2,4,16,256]{3,2,1,0:T(8,128)S(1)} collective-permute-done((f32[2,4,16,256]{3,2,1,0:T(8,128)S(1)}, f32[2,4,16,256]{3,2,1,0:T(8,128)S(1)}, u32[]{:S(2)}, u32[]{:S(2)}) %collective-permute-start.5) | collective-permute-done | bytes 131104 | tf_op jit(solution)/shard_map/ppermute | solution.py:267
  32.1 0.0 collective-permute-done.6.refs_7_
  32.1 0.0 collective-permute-done.7.refs_8_
  32.1 0.5 shard_map.150
  32.7 1.3 %collective-permute-start.10 = (f32[2,4,16,256]{3,2,1,0:T(8,128)S(1)}, f32[2,4,16,256]{3,2,1,0:T(8,128)S(1)}, u32[]{:S(2)}, u32[]{:S(2)}) collective-permute-start(f32[2,4,16,256]{3,2,1,0:T(8,128)S(1)} %get-tuple-element.76), channel_id=1, source_target_pairs={{0,8},{8,0},{16,24},{24,16},{32,40},{40,32},{48,56},{56,48},{64,72... | collective-permute-start | bytes 393224 | tf_op jit(solution)/shard_map/ppermute | solution.py:266
  34.0 1.8 %collective-permute-start.11 = (f32[2,4,16,256]{3,2,1,0:T(8,128)S(1)}, f32[2,4,16,256]{3,2,1,0:T(8,128)S(1)}, u32[]{:S(2)}, u32[]{:S(2)}) collective-permute-start(f32[2,4,16,256]{3,2,1,0:T(8,128)S(1)} %get-tuple-element.77), channel_id=1, source_target_pairs={{0,248},{8,16},{16,8},{24,32},{32,24},{40,48},{48,40},{56,64},{64,... | collective-permute-start | bytes 393224 | tf_op jit(solution)/shard_map/ppermute | solution.py:267
  35.8 3.7 %collective-permute-start.13 = (f32[2,8,8,256]{3,2,1,0:T(8,128)S(1)}, f32[2,8,8,256]{3,2,1,0:T(8,128)S(1)}, u32[]{:S(2)}, u32[]{:S(2)}) collective-permute-start(f32[2,8,8,256]{3,2,1,0:T(8,128)S(1)} %get-tuple-element.79), channel_id=1, source_target_pairs={{0,7},{1,2},{2,1},{3,4},{4,3},{5,6},{6,5},{7,0},{8,15},{9,10},{10,... | collective-permute-start | bytes 393224 | tf_op jit(solution)/shard_map/ppermute | solution.py:268
  39.5 0.3 collective-permute-start.19
  39.8 1.2 %shard_map.151 = (f32[16,16,256]{2,1,0:T(8,128)S(1)}, f32[16,16,256]{2,1,0:T(8,128)S(1)}) custom-call(f32[16,16,256]{2,1,0:T(8,128)S(1)} %get-tuple-element.72.s.refs_0_.refs_8_, f32[16,16,256]{2,1,0:T(8,128)S(1)} %get-tuple-element.73.r.refs_1_.refs_9_), custom_call_target="tpu_custom_call" | custom-call | flops 1048576 | bytes 1048576 | tf_op jit(solution)/shard_map/pallas_call | solution.py:27
  41.0 4.2 %collective-permute-done.11.refs_5_.after = f32[2,4,16,256]{3,2,1,0:T(8,128)S(1)} collective-permute-done((f32[2,4,16,256]{3,2,1,0:T(8,128)S(1)}, f32[2,4,16,256]{3,2,1,0:T(8,128)S(1)}, u32[]{:S(2)}, u32[]{:S(2)}) %collective-permute-start.11) | collective-permute-done | bytes 131104 | tf_op jit(solution)/shard_map/ppermute | solution.py:267
  45.3 0.0 collective-permute-done.12.refs_6_
  45.3 0.0 collective-permute-done.13.refs_7_
  45.3 0.4 shard_map.152
  45.7 1.9 %collective-permute-start.14 = (f32[2,4,16,256]{3,2,1,0:T(8,128)S(1)}, f32[2,4,16,256]{3,2,1,0:T(8,128)S(1)}, u32[]{:S(2)}, u32[]{:S(2)}) collective-permute-start(f32[2,4,16,256]{3,2,1,0:T(8,128)S(1)} %get-tuple-element.86), channel_id=1, source_target_pairs={{0,8},{8,0},{16,24},{24,16},{32,40},{40,32},{48,56},{56,48},{64,72... | collective-permute-start | bytes 393224 | tf_op jit(solution)/shard_map/ppermute | solution.py:266
  47.6 0.3 collective-permute-start.15
  47.9 0.5 collective-permute-start.16
  48.4 3.1 %collective-permute-start.17 = (f32[2,8,8,256]{3,2,1,0:T(8,128)S(1)}, f32[2,8,8,256]{3,2,1,0:T(8,128)S(1)}, u32[]{:S(2)}, u32[]{:S(2)}) collective-permute-start(f32[2,8,8,256]{3,2,1,0:T(8,128)S(1)} %get-tuple-element.89), channel_id=1, source_target_pairs={{0,7},{1,2},{2,1},{3,4},{4,3},{5,6},{6,5},{7,0},{8,15},{9,10},{10,... | collective-permute-start | bytes 393224 | tf_op jit(solution)/shard_map/ppermute | solution.py:268
  51.6 0.0 collective-permute-done.19.got
  51.6 4.6 %collective-permute-start.25 = (f32[16,16,256]{2,1,0:T(8,128)S(1)}, f32[16,16,256]{2,1,0:T(8,128)S(1)}, u32[]{:S(2)}, u32[]{:S(2)}) collective-permute-start(f32[16,16,256]{2,1,0:T(8,128)S(1)} %shard_map.160), channel_id=1, source_target_pairs={{0,248},{8,0},{16,8},{24,16},{32,24},{40,32},{48,40},{56,48},{64,5... | collective-permute-start | bytes 786440 | tf_op jit(solution)/shard_map/ppermute | solution.py:316
  56.2 0.1 collective-permute-start.20
  56.3 1.2 %shard_map.153 = (f32[16,16,256]{2,1,0:T(8,128)S(1)}, f32[16,16,256]{2,1,0:T(8,128)S(1)}) custom-call(f32[16,16,256]{2,1,0:T(8,128)S(1)} %get-tuple-element.82.s.refs_0_.refs_9_, f32[16,16,256]{2,1,0:T(8,128)S(1)} %get-tuple-element.83.r.refs_1_.refs_10_), custom_call_target="tpu_custom_call" | custom-call | flops 1048576 | bytes 1048576 | tf_op jit(solution)/shard_map/pallas_call | solution.py:27
  57.5 0.8 %collective-permute-done.15.refs_5_ = f32[2,4,16,256]{3,2,1,0:T(8,128)S(1)} collective-permute-done((f32[2,4,16,256]{3,2,1,0:T(8,128)S(1)}, f32[2,4,16,256]{3,2,1,0:T(8,128)S(1)}, u32[]{:S(2)}, u32[]{:S(2)}) %collective-permute-start.15) | collective-permute-done | bytes 131104 | tf_op jit(solution)/shard_map/ppermute | solution.py:267
  58.4 1.6 %collective-permute-done.16.refs_6_ = f32[2,8,8,256]{3,2,1,0:T(8,128)S(1)} collective-permute-done((f32[2,8,8,256]{3,2,1,0:T(8,128)S(1)}, f32[2,8,8,256]{3,2,1,0:T(8,128)S(1)}, u32[]{:S(2)}, u32[]{:S(2)}) %collective-permute-start.16) | collective-permute-done | bytes 131104 | tf_op jit(solution)/shard_map/ppermute | solution.py:269
  60.0 0.0 collective-permute-done.17.refs_7_
  60.0 0.4 shard_map.154
  60.4 1.6 %collective-permute-start.18 = (f32[2,4,16,256]{3,2,1,0:T(8,128)S(1)}, f32[2,4,16,256]{3,2,1,0:T(8,128)S(1)}, u32[]{:S(2)}, u32[]{:S(2)}) collective-permute-start(f32[2,4,16,256]{3,2,1,0:T(8,128)S(1)} %get-tuple-element.91), channel_id=1, source_target_pairs={{0,8},{8,0},{16,24},{24,16},{32,40},{40,32},{48,56},{56,48},{64,72... | collective-permute-start | bytes 393224 | tf_op jit(solution)/shard_map/ppermute | solution.py:266
  62.0 0.3 collective-permute-start.22
  62.3 0.6 collective-permute-start.23
  63.0 0.0 collective-permute-done.20.got
  63.0 2.5 %collective-permute-start.24 = (f32[2,8,8,256]{3,2,1,0:T(8,128)S(1)}, f32[2,8,8,256]{3,2,1,0:T(8,128)S(1)}, u32[]{:S(2)}, u32[]{:S(2)}) collective-permute-start(f32[2,8,8,256]{3,2,1,0:T(8,128)S(1)} %get-tuple-element.107), channel_id=1, source_target_pairs={{0,7},{1,2},{2,1},{3,4},{4,3},{5,6},{6,5},{7,0},{8,15},{9,10},{10,... | collective-permute-start | bytes 393224 | tf_op jit(solution)/shard_map/ppermute | solution.py:268
  65.5 0.0 collective-permute-done.18.after.refs_5_
  65.5 4.4 %collective-permute-start.21 = (f32[8,256]{1,0:T(8,128)S(1)}, f32[8,256]{1,0:T(8,128)S(1)}, u32[]{:S(2)}, u32[]{:S(2)}) collective-permute-start(f32[8,256]{1,0:T(8,128)S(1)} %get-tuple-element.98), channel_id=1, source_target_pairs={{0,8},{8,0},{16,24},{24,16},{32,40},{40,32},{48,56},{56,48},{64,72... | collective-permute-start | bytes 24584 | tf_op jit(solution)/shard_map/ppermute | solution.py:313
  69.9 1.2 %shard_map.159 = (f32[16,16,256]{2,1,0:T(8,128)S(1)}, f32[16,16,256]{2,1,0:T(8,128)S(1)}) custom-call(f32[16,16,256]{2,1,0:T(8,128)S(1)} %get-tuple-element.101.s.refs_1_, f32[16,16,256]{2,1,0:T(8,128)S(1)} %get-tuple-element.102.r.refs_2_), custom_call_target="tpu_custom_call" | custom-call | flops 1048576 | bytes 1048576 | tf_op jit(solution)/shard_map/pallas_call | solution.py:27
  71.1 1.7 %shard_map.158 = (f32[16,16,256]{2,1,0:T(8,128)}, f32[8,128]{1,0:T(8,128)S(1)}) custom-call(s32[32]{0:T(128)S(1)} %bitcast.2, f32[8,256]{1,0:T(8,128)S(1)} %get-tuple-element.97.held, f32[8,256]{1,0:T(8,128)S(1)} %collective-permute-done.21.got, f32[16,16,256]{2,1,0:T(8,128)S(1)} %copy-done.6), custom_call_target="tpu_custom_call" | custom-call | flops 1048576 | bytes 1048576 | tf_op jit(solution)/shard_map/pallas_call | solution.py:27
  72.8 0.0 collective-permute-done.25.refs_15_
  72.8 0.0 collective-permute-done.24.refs_8_
  72.8 1.3 %shard_map.161 = (f32[16,16,256]{2,1,0:T(8,128)}, f32[16,16,256]{2,1,0:T(8,128)}, f32[16,16,256]{2,1,0:T(8,128)}, f32[16,16,256]{2,1,0:T(8,128)}, f32[16,16,256]{2,1,0:T(8,128)}) custom-call(f32[8,128]{1,0:T(8,128)S(1)} %get-tuple-element.100.refs_0_, f32[16,16,256]{2,1,0:T(8,128)S(1)} %get-tuple-element.101.s.refs_1_, ...), custom_call_target="tpu_custom_call" | custom-call | flops 1048576 | bytes 1048576 | tf_op jit(solution)/shard_map/pallas_call | solution.py:27
  (29 shorter events, 0.1 us)
Async XLA Ops:
  0.6 14.4 %collective-permute-start = (f32[16,16,256]{2,1,0:T(8,128)}, f32[16,16,256]{2,1,0:T(8,128)S(1)}, u32[]{:S(2)}, u32[]{:S(2)}) collective-permute-start(f32[16,16,256]{2,1,0:T(8,128)} %s.1), channel_id=1, source_target_pairs={{0,248},{8,0},{16,8},{24,16},{32,24},{40,32},{48,40},{56,48},{64,5... | collective-permute-start | bytes 786440 | tf_op jit(solution)/shard_map/ppermute | solution.py:277
  4.0 11.1 %collective-permute-start.1 = (f32[16,16,256]{2,1,0:T(8,128)}, f32[16,16,256]{2,1,0:T(8,128)S(1)}, u32[]{:S(2)}, u32[]{:S(2)}) collective-permute-start(f32[16,16,256]{2,1,0:T(8,128)} %r.1), channel_id=1, source_target_pairs={{0,248},{8,0},{16,8},{24,16},{32,24},{40,32},{48,40},{56,48},{64,5... | collective-permute-start | bytes 786440 | tf_op jit(solution)/shard_map/ppermute | solution.py:278
  10.1 0.9 %copy-start = (f32[16,16,256]{2,1,0:T(8,128)S(1)}, f32[16,16,256]{2,1,0:T(8,128)}, u32[]{:S(2)}) copy-start(f32[16,16,256]{2,1,0:T(8,128)} %refs_14_.1) | copy-start | bytes 786436
  11.1 0.9 %copy-start.2 = (f32[16,16,256]{2,1,0:T(8,128)S(1)}, f32[16,16,256]{2,1,0:T(8,128)}, u32[]{:S(2)}) copy-start(f32[16,16,256]{2,1,0:T(8,128)} %refs_12_.1) | copy-start | bytes 786436
  12.0 0.9 %copy-start.7 = (f32[16,16,256]{2,1,0:T(8,128)S(1)}, f32[16,16,256]{2,1,0:T(8,128)}, u32[]{:S(2)}) copy-start(f32[16,16,256]{2,1,0:T(8,128)} %refs_10_.1) | copy-start | bytes 786436
  12.0 1.7 %copy-start.4 = (f32[16,16,256]{2,1,0:T(8,128)S(1)}, f32[16,16,256]{2,1,0:T(8,128)}, u32[]{:S(2)}) copy-start(f32[16,16,256]{2,1,0:T(8,128)} %s.1) | copy-start | bytes 786436
  12.0 1.7 %copy-start.5 = (f32[16,16,256]{2,1,0:T(8,128)S(1)}, f32[16,16,256]{2,1,0:T(8,128)}, u32[]{:S(2)}) copy-start(f32[16,16,256]{2,1,0:T(8,128)} %r.1) | copy-start | bytes 786436
  12.1 7.4 %collective-permute-start.3 = (f32[16,16,256]{2,1,0:T(8,128)S(1)}, f32[16,16,256]{2,1,0:T(8,128)S(1)}, u32[]{:S(2)}, u32[]{:S(2)}) collective-permute-start(f32[16,16,256]{2,1,0:T(8,128)S(1)} %shard_map.147), channel_id=1, source_target_pairs={{0,248},{8,0},{16,8},{24,16},{32,24},{40,32},{48,40},{56,48},{64,5... | collective-permute-start | bytes 786440 | tf_op jit(solution)/shard_map/ppermute | solution.py:282
  13.0 11.1 %collective-permute-start.8 = (f32[16,16,256]{2,1,0:T(8,128)S(1)}, f32[16,16,256]{2,1,0:T(8,128)S(1)}, u32[]{:S(2)}, u32[]{:S(2)}) collective-permute-start(f32[16,16,256]{2,1,0:T(8,128)S(1)} %copy-done.7), channel_id=1, source_target_pairs={{0,248},{8,0},{16,8},{24,16},{32,24},{40,32},{48,40},{56,48},{64,5... | collective-permute-start | bytes 786440 | tf_op jit(solution)/shard_map/ppermute | solution.py:279
  13.7 17.0 %collective-permute-start.9 = (f32[16,16,256]{2,1,0:T(8,128)}, f32[16,16,256]{2,1,0:T(8,128)S(1)}, u32[]{:S(2)}, u32[]{:S(2)}) collective-permute-start(f32[16,16,256]{2,1,0:T(8,128)} %refs_11_.1), channel_id=1, source_target_pairs={{0,248},{8,0},{16,8},{24,16},{32,24},{40,32},{48,40},{56,48},{64,5... | collective-permute-start | bytes 786440 | tf_op jit(solution)/shard_map/ppermute | solution.py:280
  13.8 0.7 copy-start.11
  15.0 8.1 %copy-start.1 = (f32[16,16,256]{2,1,0:T(8,128)S(1)}, f32[16,16,256]{2,1,0:T(8,128)}, u32[]{:S(2)}) copy-start(f32[16,16,256]{2,1,0:T(8,128)} %refs_14_.1) | copy-start | bytes 786436
  15.2 4.6 %collective-permute-start.2 = (f32[2,4,16,256]{3,2,1,0:T(8,128)S(1)}, f32[2,4,16,256]{3,2,1,0:T(8,128)S(1)}, u32[]{:S(2)}, u32[]{:S(2)}) collective-permute-start(f32[2,4,16,256]{3,2,1,0:T(8,128)S(1)} %get-tuple-element.63), channel_id=1, source_target_pairs={{0,8},{8,0},{16,24},{24,16},{32,40},{40,32},{48,56},{56,48},{64,72... | collective-permute-start | bytes 393224 | tf_op jit(solution)/shard_map/ppermute | solution.py:266
  17.9 14.2 %collective-permute-start.5 = (f32[2,4,16,256]{3,2,1,0:T(8,128)S(1)}, f32[2,4,16,256]{3,2,1,0:T(8,128)S(1)}, u32[]{:S(2)}, u32[]{:S(2)}) collective-permute-start(f32[2,4,16,256]{3,2,1,0:T(8,128)S(1)} %get-tuple-element.69), channel_id=1, source_target_pairs={{0,248},{8,16},{16,8},{24,32},{32,24},{40,48},{48,40},{56,64},{64,... | collective-permute-start | bytes 393224 | tf_op jit(solution)/shard_map/ppermute | solution.py:267
  19.5 12.6 %collective-permute-start.6 = (f32[2,8,8,256]{3,2,1,0:T(8,128)S(1)}, f32[2,8,8,256]{3,2,1,0:T(8,128)S(1)}, u32[]{:S(2)}, u32[]{:S(2)}) collective-permute-start(f32[2,8,8,256]{3,2,1,0:T(8,128)S(1)} %get-tuple-element.70), channel_id=1, source_target_pairs={{0,1},{1,0},{2,3},{3,2},{4,5},{5,4},{6,7},{7,6},{8,9},{9,8},{10,11... | collective-permute-start | bytes 393224 | tf_op jit(solution)/shard_map/ppermute | solution.py:269
  19.9 3.3 %copy-start.10 = (s32[1,32]{1,0:T(1,128)S(1)}, s32[1,32]{1,0:T(1,128)}, u32[]{:S(2)}) copy-start(s32[1,32]{1,0:T(1,128)} %param.19) | copy-start | bytes 388
  19.9 12.2 %collective-permute-start.7 = (f32[2,8,8,256]{3,2,1,0:T(8,128)S(1)}, f32[2,8,8,256]{3,2,1,0:T(8,128)S(1)}, u32[]{:S(2)}, u32[]{:S(2)}) collective-permute-start(f32[2,8,8,256]{3,2,1,0:T(8,128)S(1)} %get-tuple-element.71), channel_id=1, source_target_pairs={{0,7},{1,2},{2,1},{3,4},{4,3},{5,6},{6,5},{7,0},{8,15},{9,10},{10,... | collective-permute-start | bytes 393224 | tf_op jit(solution)/shard_map/ppermute | solution.py:268
  23.1 9.0 %copy-start.9 = (f32[16,16,256]{2,1,0:T(8,128)S(1)}, f32[16,16,256]{2,1,0:T(8,128)}, u32[]{:S(2)}) copy-start(f32[16,16,256]{2,1,0:T(8,128)} %refs_13_.1) | copy-start | bytes 786436
  24.1 8.0 %collective-permute-start.4 = (f32[64,256]{1,0:T(8,128)S(1)}, f32[64,256]{1,0:T(8,128)S(1)}, u32[]{:S(2)}, u32[]{:S(2)}) collective-permute-start(f32[64,256]{1,0:T(8,128)S(1)} %get-tuple-element.64), channel_id=1, source_target_pairs={{0,64},{8,72},{16,80},{24,88},{32,96},{40,104},{48,112},{56,120},{... | collective-permute-start | bytes 196616 | tf_op jit(solution)/shard_map/ppermute | solution.py:313
  24.2 7.9 %copy-start.3 = (f32[16,16,256]{2,1,0:T(8,128)S(1)}, f32[16,16,256]{2,1,0:T(8,128)}, u32[]{:S(2)}) copy-start(f32[16,16,256]{2,1,0:T(8,128)} %refs_12_.1) | copy-start | bytes 786436
  24.2 7.9 %copy-start.8 = (f32[16,16,256]{2,1,0:T(8,128)S(1)}, f32[16,16,256]{2,1,0:T(8,128)}, u32[]{:S(2)}) copy-start(f32[16,16,256]{2,1,0:T(8,128)} %refs_11_.1) | copy-start | bytes 786436
  32.7 6.8 %collective-permute-start.10 = (f32[2,4,16,256]{3,2,1,0:T(8,128)S(1)}, f32[2,4,16,256]{3,2,1,0:T(8,128)S(1)}, u32[]{:S(2)}, u32[]{:S(2)}) collective-permute-start(f32[2,4,16,256]{3,2,1,0:T(8,128)S(1)} %get-tuple-element.76), channel_id=1, source_target_pairs={{0,8},{8,0},{16,24},{24,16},{32,40},{40,32},{48,56},{56,48},{64,72... | collective-permute-start | bytes 393224 | tf_op jit(solution)/shard_map/ppermute | solution.py:266
  34.0 11.3 %collective-permute-start.11 = (f32[2,4,16,256]{3,2,1,0:T(8,128)S(1)}, f32[2,4,16,256]{3,2,1,0:T(8,128)S(1)}, u32[]{:S(2)}, u32[]{:S(2)}) collective-permute-start(f32[2,4,16,256]{3,2,1,0:T(8,128)S(1)} %get-tuple-element.77), channel_id=1, source_target_pairs={{0,248},{8,16},{16,8},{24,32},{32,24},{40,48},{48,40},{56,64},{64,... | collective-permute-start | bytes 393224 | tf_op jit(solution)/shard_map/ppermute | solution.py:267
  35.8 9.4 %collective-permute-start.12 = (f32[2,8,8,256]{3,2,1,0:T(8,128)S(1)}, f32[2,8,8,256]{3,2,1,0:T(8,128)S(1)}, u32[]{:S(2)}, u32[]{:S(2)}) collective-permute-start(f32[2,8,8,256]{3,2,1,0:T(8,128)S(1)} %get-tuple-element.78), channel_id=1, source_target_pairs={{0,1},{1,0},{2,3},{3,2},{4,5},{5,4},{6,7},{7,6},{8,9},{9,8},{10,11... | collective-permute-start | bytes 393224 | tf_op jit(solution)/shard_map/ppermute | solution.py:269
  35.8 9.4 %collective-permute-start.13 = (f32[2,8,8,256]{3,2,1,0:T(8,128)S(1)}, f32[2,8,8,256]{3,2,1,0:T(8,128)S(1)}, u32[]{:S(2)}, u32[]{:S(2)}) collective-permute-start(f32[2,8,8,256]{3,2,1,0:T(8,128)S(1)} %get-tuple-element.79), channel_id=1, source_target_pairs={{0,7},{1,2},{2,1},{3,4},{4,3},{5,6},{6,5},{7,0},{8,15},{9,10},{10,... | collective-permute-start | bytes 393224 | tf_op jit(solution)/shard_map/ppermute | solution.py:268
  39.5 12.1 %collective-permute-start.19 = (f32[32,256]{1,0:T(8,128)S(1)}, f32[32,256]{1,0:T(8,128)S(1)}, u32[]{:S(2)}, u32[]{:S(2)}) collective-permute-start(f32[32,256]{1,0:T(8,128)S(1)} %get-tuple-element.94), channel_id=1, source_target_pairs={{0,32},{8,40},{16,48},{24,56},{32,0},{40,8},{48,16},{56,24},{64,96... | collective-permute-start | bytes 98312 | tf_op jit(solution)/shard_map/ppermute | solution.py:313
  45.7 10.5 %collective-permute-start.14 = (f32[2,4,16,256]{3,2,1,0:T(8,128)S(1)}, f32[2,4,16,256]{3,2,1,0:T(8,128)S(1)}, u32[]{:S(2)}, u32[]{:S(2)}) collective-permute-start(f32[2,4,16,256]{3,2,1,0:T(8,128)S(1)} %get-tuple-element.86), channel_id=1, source_target_pairs={{0,8},{8,0},{16,24},{24,16},{32,40},{40,32},{48,56},{56,48},{64,72... | collective-permute-start | bytes 393224 | tf_op jit(solution)/shard_map/ppermute | solution.py:266
  47.6 10.8 %collective-permute-start.15 = (f32[2,4,16,256]{3,2,1,0:T(8,128)S(1)}, f32[2,4,16,256]{3,2,1,0:T(8,128)S(1)}, u32[]{:S(2)}, u32[]{:S(2)}) collective-permute-start(f32[2,4,16,256]{3,2,1,0:T(8,128)S(1)} %get-tuple-element.87), channel_id=1, source_target_pairs={{0,248},{8,16},{16,8},{24,32},{32,24},{40,48},{48,40},{56,64},{64,... | collective-permute-start | bytes 393224 | tf_op jit(solution)/shard_map/ppermute | solution.py:267
  47.9 12.1 %collective-permute-start.16 = (f32[2,8,8,256]{3,2,1,0:T(8,128)S(1)}, f32[2,8,8,256]{3,2,1,0:T(8,128)S(1)}, u32[]{:S(2)}, u32[]{:S(2)}) collective-permute-start(f32[2,8,8,256]{3,2,1,0:T(8,128)S(1)} %get-tuple-element.88), channel_id=1, source_target_pairs={{0,1},{1,0},{2,3},{3,2},{4,5},{5,4},{6,7},{7,6},{8,9},{9,8},{10,11... | collective-permute-start | bytes 393224 | tf_op jit(solution)/shard_map/ppermute | solution.py:269
  48.4 11.5 %collective-permute-start.17 = (f32[2,8,8,256]{3,2,1,0:T(8,128)S(1)}, f32[2,8,8,256]{3,2,1,0:T(8,128)S(1)}, u32[]{:S(2)}, u32[]{:S(2)}) collective-permute-start(f32[2,8,8,256]{3,2,1,0:T(8,128)S(1)} %get-tuple-element.89), channel_id=1, source_target_pairs={{0,7},{1,2},{2,1},{3,4},{4,3},{5,6},{6,5},{7,0},{8,15},{9,10},{10,... | collective-permute-start | bytes 393224 | tf_op jit(solution)/shard_map/ppermute | solution.py:268
  51.6 21.2 %collective-permute-start.25 = (f32[16,16,256]{2,1,0:T(8,128)S(1)}, f32[16,16,256]{2,1,0:T(8,128)S(1)}, u32[]{:S(2)}, u32[]{:S(2)}) collective-permute-start(f32[16,16,256]{2,1,0:T(8,128)S(1)} %shard_map.160), channel_id=1, source_target_pairs={{0,248},{8,0},{16,8},{24,16},{32,24},{40,32},{48,40},{56,48},{64,5... | collective-permute-start | bytes 786440 | tf_op jit(solution)/shard_map/ppermute | solution.py:316
  56.2 6.8 %collective-permute-start.20 = (f32[16,256]{1,0:T(8,128)S(1)}, f32[16,256]{1,0:T(8,128)S(1)}, u32[]{:S(2)}, u32[]{:S(2)}) collective-permute-start(f32[16,256]{1,0:T(8,128)S(1)} %get-tuple-element.96), channel_id=1, source_target_pairs={{0,16},{8,24},{16,0},{24,8},{32,48},{40,56},{48,32},{56,40},{64,80... | collective-permute-start | bytes 49160 | tf_op jit(solution)/shard_map/ppermute | solution.py:313
  60.4 5.0 %collective-permute-start.18 = (f32[2,4,16,256]{3,2,1,0:T(8,128)S(1)}, f32[2,4,16,256]{3,2,1,0:T(8,128)S(1)}, u32[]{:S(2)}, u32[]{:S(2)}) collective-permute-start(f32[2,4,16,256]{3,2,1,0:T(8,128)S(1)} %get-tuple-element.91), channel_id=1, source_target_pairs={{0,8},{8,0},{16,24},{24,16},{32,40},{40,32},{48,56},{56,48},{64,72... | collective-permute-start | bytes 393224 | tf_op jit(solution)/shard_map/ppermute | solution.py:266
  62.0 10.8 %collective-permute-start.22 = (f32[2,4,16,256]{3,2,1,0:T(8,128)S(1)}, f32[2,4,16,256]{3,2,1,0:T(8,128)S(1)}, u32[]{:S(2)}, u32[]{:S(2)}) collective-permute-start(f32[2,4,16,256]{3,2,1,0:T(8,128)S(1)} %get-tuple-element.105), channel_id=1, source_target_pairs={{0,248},{8,16},{16,8},{24,32},{32,24},{40,48},{48,40},{56,64},{64,... | collective-permute-start | bytes 393224 | tf_op jit(solution)/shard_map/ppermute | solution.py:267
  62.3 10.5 %collective-permute-start.23 = (f32[2,8,8,256]{3,2,1,0:T(8,128)S(1)}, f32[2,8,8,256]{3,2,1,0:T(8,128)S(1)}, u32[]{:S(2)}, u32[]{:S(2)}) collective-permute-start(f32[2,8,8,256]{3,2,1,0:T(8,128)S(1)} %get-tuple-element.106), channel_id=1, source_target_pairs={{0,1},{1,0},{2,3},{3,2},{4,5},{5,4},{6,7},{7,6},{8,9},{9,8},{10,11... | collective-permute-start | bytes 393224 | tf_op jit(solution)/shard_map/ppermute | solution.py:269
  63.0 9.9 %collective-permute-start.24 = (f32[2,8,8,256]{3,2,1,0:T(8,128)S(1)}, f32[2,8,8,256]{3,2,1,0:T(8,128)S(1)}, u32[]{:S(2)}, u32[]{:S(2)}) collective-permute-start(f32[2,8,8,256]{3,2,1,0:T(8,128)S(1)} %get-tuple-element.107), channel_id=1, source_target_pairs={{0,7},{1,2},{2,1},{3,4},{4,3},{5,6},{6,5},{7,0},{8,15},{9,10},{10,... | collective-permute-start | bytes 393224 | tf_op jit(solution)/shard_map/ppermute | solution.py:268
  65.5 5.6 %collective-permute-start.21 = (f32[8,256]{1,0:T(8,128)S(1)}, f32[8,256]{1,0:T(8,128)S(1)}, u32[]{:S(2)}, u32[]{:S(2)}) collective-permute-start(f32[8,256]{1,0:T(8,128)S(1)} %get-tuple-element.98), channel_id=1, source_target_pairs={{0,8},{8,0},{16,24},{24,16},{32,40},{40,32},{48,56},{56,48},{64,72... | collective-permute-start | bytes 24584 | tf_op jit(solution)/shard_map/ppermute | solution.py:313
  69.9 1.2 %copy-start.6 = (f32[16,16,256]{2,1,0:T(8,128)S(1)}, f32[16,16,256]{2,1,0:T(8,128)}, u32[]{:S(2)}) copy-start(f32[16,16,256]{2,1,0:T(8,128)} %base.1) | copy-start | bytes 786436

commit v5 on v4

--- a/solution.py
+++ b/solution.py
@@ -308,13 +308,13 @@
                 [],
                 low,
                 got,
-                after=(halos[0],),
+                after=(halos[1] if step in (1, 2,) else halos[0],),
             )
         got = lax.ppermute(high, "gx", [(i, i ^ (8 >> step)) for i in range(n)])
-        if step == 1:
-            (image_send,) = call(copy_kernel, [tile], [], image, after=(halos[1],))
+        s_lap, r_lap = call(interior_kernel, [tile, tile], scratch, s, r)
+        if step == 2:
+            (image_send,) = call(copy_kernel, [tile], [], image, after=(s_lap,))
             image_come = lax.ppermute(image_send, "gx", west)
-        s_lap, r_lap = call(interior_kernel, [tile, tile], scratch, s, r)
         ins = [s, r, s_lap, r_lap, *halos]
         outs = [tile] * 3
         if step == 0:

time: 74.3 us -> 74.1 us (level)
    ppermute x4, starting transfers between devices: 3.1 us -> 7.9 us  [swap(): od = lax.ppermute(od, 'gx', odd_x)]
    ppermute x4, waiting for transfers between devices: 6.47 us -> 1.88 us  [swap(): od = lax.ppermute(od, 'gx', odd_x)]
    ppermute x1, starting transfers between devices: 4.59 us -> 0.64 us  [body(): image_come = lax.ppermute(image_send, 'gx', west)]
    ppermute x4, waiting for transfers between devices: 1.63 us -> 5.53 us  [swap(): y1 = lax.ppermute(y1, 'gy', pair_y)]
    ppermute x4, starting transfers between devices: 12.6 us -> 14 us  [swap(): yo = lax.ppermute(yo, 'gy', odd_y)]
    ppermute x4, starting transfers between devices: 1.58 us -> 0.52 us  [swap(): y1 = lax.ppermute(y1, 'gy', pair_y)]
    ppermute x4, starting transfers between devices: 7.47 us -> 6.7 us  [swap(): x1 = lax.ppermute(x1, 'gx', pair_x)]
where the time goes in v5:
time: 74.1 us; the launch traced here: 73.9 us
  starting transfers between devices  45.6 us (62%)
  waiting for transfers between devices  13.6 us (18%)
  Pallas kernels  11 us (15%)
  local copies, waits for them, and re-layouts  2.75 us (4%)
  between operations  0.89 us (1%)
    ppermute x4, starting transfers between devices, swap(): yo = lax.ppermute(yo, 'gy', odd_y)  14 us
    pallas_call x17, Pallas kernels, call(): pl.pallas_call(kernel, out_shape=outs, in_specs=specs, out_specs=[pl.Bloc...  11 us
    ppermute x4, starting transfers between devices, swap(): od = lax.ppermute(od, 'gx', odd_x)  7.9 us
    ppermute x4, starting transfers between devices, swap(): x1 = lax.ppermute(x1, 'gx', pair_x)  6.7 us
    ppermute x1, starting transfers between devices, body(): r_come = lax.ppermute(rcv_cur, 'gx', west)  6.19 us
    ppermute x4, waiting for transfers between devices, swap(): y1 = lax.ppermute(y1, 'gy', pair_y)  5.53 us
    ppermute x1, waiting for transfers between devices, body(): rp_come = lax.ppermute(rcv_prev, 'gx', west)  5.25 us
    ppermute x4, starting transfers between devices, body(): got = lax.ppermute(high, 'gx', [(i, i ^ 8 >> step) for i in range(n)])  4.9 us
  transfers between devices with their start and end apart: 26, of which 6 were waited for; matrix products, arithmetic and copies ran while one was open for 0% of the time, Pallas kernels for 12%

profile of v5, /device:TPU:1, one launch (start us, length us, event | category | flops | bytes accessed | tf_op | source)
XLA Modules:
  0.0 73.9 jit_solution(14558585777387189193)
XLA Ops:
  0.6 3.3 %collective-permute-start = (f32[16,16,256]{2,1,0:T(8,128)}, f32[16,16,256]{2,1,0:T(8,128)S(1)}, u32[]{:S(2)}, u32[]{:S(2)}) collective-permute-start(f32[16,16,256]{2,1,0:T(8,128)} %s.1), channel_id=1, source_target_pairs={{0,248},{8,0},{16,8},{24,16},{32,24},{40,32},{48,40},{56,48},{64,5... | collective-permute-start | bytes 786440 | tf_op jit(solution)/shard_map/ppermute | solution.py:277
  4.0 6.2 %collective-permute-start.1 = (f32[16,16,256]{2,1,0:T(8,128)}, f32[16,16,256]{2,1,0:T(8,128)S(1)}, u32[]{:S(2)}, u32[]{:S(2)}) collective-permute-start(f32[16,16,256]{2,1,0:T(8,128)} %r.1), channel_id=1, source_target_pairs={{0,248},{8,0},{16,8},{24,16},{32,24},{40,32},{48,40},{56,48},{64,5... | collective-permute-start | bytes 786440 | tf_op jit(solution)/shard_map/ppermute | solution.py:278
  10.1 0.9 %copy-done = f32[16,16,256]{2,1,0:T(8,128)S(1)} copy-done((f32[16,16,256]{2,1,0:T(8,128)S(1)}, f32[16,16,256]{2,1,0:T(8,128)}, u32[]{:S(2)}) %copy-start) | copy-done | bytes 262168
  11.1 0.9 %copy-done.2 = f32[16,16,256]{2,1,0:T(8,128)S(1)} copy-done((f32[16,16,256]{2,1,0:T(8,128)S(1)}, f32[16,16,256]{2,1,0:T(8,128)}, u32[]{:S(2)}) %copy-start.2) | copy-done | bytes 262168
  12.1 0.8 %collective-permute-start.3 = (f32[16,16,256]{2,1,0:T(8,128)S(1)}, f32[16,16,256]{2,1,0:T(8,128)S(1)}, u32[]{:S(2)}, u32[]{:S(2)}) collective-permute-start(f32[16,16,256]{2,1,0:T(8,128)S(1)} %shard_map.147), channel_id=1, source_target_pairs={{0,248},{8,0},{16,8},{24,16},{32,24},{40,32},{48,40},{56,48},{64,5... | collective-permute-start | bytes 786440 | tf_op jit(solution)/shard_map/ppermute | solution.py:282
  12.8 0.2 copy-done.7
  13.0 0.7 collective-permute-start.8
  13.7 0.1 collective-permute-start.9
  13.8 0.7 copy-done.11
  14.4 0.6 shard_map.145
  15.0 0.0 collective-permute-done.s_in
  15.0 0.0 collective-permute-done.1.r_in
  15.0 0.0 copy-start.1
  15.0 0.2 shard_map.146
  15.2 2.7 %collective-permute-start.2 = (f32[2,4,16,256]{3,2,1,0:T(8,128)S(1)}, f32[2,4,16,256]{3,2,1,0:T(8,128)S(1)}, u32[]{:S(2)}, u32[]{:S(2)}) collective-permute-start(f32[2,4,16,256]{3,2,1,0:T(8,128)S(1)} %get-tuple-element.63), channel_id=1, source_target_pairs={{0,8},{8,0},{16,24},{24,16},{32,40},{40,32},{48,56},{56,48},{64,72... | collective-permute-start | bytes 393224 | tf_op jit(solution)/shard_map/ppermute | solution.py:266
  17.9 0.7 collective-permute-start.5
  18.6 0.9 %collective-permute-done.3.come.refs_16_ = f32[16,16,256]{2,1,0:T(8,128)S(1)} collective-permute-done((f32[16,16,256]{2,1,0:T(8,128)S(1)}, f32[16,16,256]{2,1,0:T(8,128)S(1)}, u32[]{:S(2)}, u32[]{:S(2)}) %collective-permute-start.3) | collective-permute-done | bytes 262176 | tf_op jit(solution)/shard_map/ppermute | solution.py:282
  19.5 0.4 collective-permute-start.6
  19.9 0.0 collective-permute-done.2.after.refs_5_
  19.9 3.3 %collective-permute-start.7 = (f32[2,8,8,256]{3,2,1,0:T(8,128)S(1)}, f32[2,8,8,256]{3,2,1,0:T(8,128)S(1)}, u32[]{:S(2)}, u32[]{:S(2)}) collective-permute-start(f32[2,8,8,256]{3,2,1,0:T(8,128)S(1)} %get-tuple-element.71), channel_id=1, source_target_pairs={{0,7},{1,2},{2,1},{3,4},{4,3},{5,6},{6,5},{7,0},{8,15},{9,10},{10,... | collective-permute-start | bytes 393224 | tf_op jit(solution)/shard_map/ppermute | solution.py:268
  23.1 0.9 %shard_map.148 = (f32[64,256]{1,0:T(8,128)S(1)}, f32[64,256]{1,0:T(8,128)S(1)}) custom-call(f32[2,4,16,256]{3,2,1,0:T(8,128)S(1)} %collective-permute-done.2.after.refs_5_, f32[16,256]{1,0:T(8,128)S(1)} %get-tuple-element.60.moves.refs_9_.refs_13_, s32[32]{0:T(128)S(1)} %bitcast.1, f32[16,16,256]{2,1,0:T(8,128)S(1)} %copy-done.1, ...), custom_call_target="tpu_custom_call" | custom-call | flops 1048576 | bytes 1048576 | tf_op jit(solution)/shard_map/pallas_call | solution.py:27
  24.1 0.0 collective-permute-done.8.refs_14_
  24.1 0.1 collective-permute-start.4
  24.2 0.0 copy-start.3
  24.2 0.0 copy-start.8
  24.2 1.2 %shard_map.149 = (f32[16,16,256]{2,1,0:T(8,128)S(1)}, f32[16,16,256]{2,1,0:T(8,128)S(1)}) custom-call(f32[16,16,256]{2,1,0:T(8,128)S(1)} %get-tuple-element.65.s.refs_1_.refs_8_, f32[16,16,256]{2,1,0:T(8,128)S(1)} %get-tuple-element.66.r.refs_2_.refs_9_), custom_call_target="tpu_custom_call" | custom-call | flops 1048576 | bytes 1048576 | tf_op jit(solution)/shard_map/pallas_call | solution.py:27
  25.5 5.2 %collective-permute-done.9.refs_15_ = f32[16,16,256]{2,1,0:T(8,128)S(1)} collective-permute-done((f32[16,16,256]{2,1,0:T(8,128)}, f32[16,16,256]{2,1,0:T(8,128)S(1)}, u32[]{:S(2)}, u32[]{:S(2)}) %collective-permute-start.9) | collective-permute-done | bytes 262176 | tf_op jit(solution)/shard_map/ppermute | solution.py:280
  30.7 1.4 %collective-permute-done.5.refs_6_ = f32[2,4,16,256]{3,2,1,0:T(8,128)S(1)} collective-permute-done((f32[2,4,16,256]{3,2,1,0:T(8,128)S(1)}, f32[2,4,16,256]{3,2,1,0:T(8,128)S(1)}, u32[]{:S(2)}, u32[]{:S(2)}) %collective-permute-start.5) | collective-permute-done | bytes 131104 | tf_op jit(solution)/shard_map/ppermute | solution.py:267
  32.1 0.0 collective-permute-done.7.refs_8_
  32.1 0.0 collective-permute-done.4.refs_0_.got
  32.1 0.5 shard_map.150
  32.7 3.1 %collective-permute-start.11 = (f32[2,4,16,256]{3,2,1,0:T(8,128)S(1)}, f32[2,4,16,256]{3,2,1,0:T(8,128)S(1)}, u32[]{:S(2)}, u32[]{:S(2)}) collective-permute-start(f32[2,4,16,256]{3,2,1,0:T(8,128)S(1)} %get-tuple-element.77), channel_id=1, source_target_pairs={{0,248},{8,16},{16,8},{24,32},{32,24},{40,48},{48,40},{56,64},{64,... | collective-permute-start | bytes 393224 | tf_op jit(solution)/shard_map/ppermute | solution.py:267
  35.7 0.0 collective-permute-start.10
  35.7 0.0 collective-permute-start.12
  35.7 3.7 %collective-permute-start.13 = (f32[2,8,8,256]{3,2,1,0:T(8,128)S(1)}, f32[2,8,8,256]{3,2,1,0:T(8,128)S(1)}, u32[]{:S(2)}, u32[]{:S(2)}) collective-permute-start(f32[2,8,8,256]{3,2,1,0:T(8,128)S(1)} %get-tuple-element.79), channel_id=1, source_target_pairs={{0,7},{1,2},{2,1},{3,4},{4,3},{5,6},{6,5},{7,0},{8,15},{9,10},{10,... | collective-permute-start | bytes 393224 | tf_op jit(solution)/shard_map/ppermute | solution.py:268
  39.4 0.0 collective-permute-done.11.refs_5_.after
  39.4 2.2 %collective-permute-start.19 = (f32[32,256]{1,0:T(8,128)S(1)}, f32[32,256]{1,0:T(8,128)S(1)}, u32[]{:S(2)}, u32[]{:S(2)}) collective-permute-start(f32[32,256]{1,0:T(8,128)S(1)} %get-tuple-element.94), channel_id=1, source_target_pairs={{0,32},{8,40},{16,48},{24,56},{32,0},{40,8},{48,16},{56,24},{64,96... | collective-permute-start | bytes 98312 | tf_op jit(solution)/shard_map/ppermute | solution.py:313
  41.6 1.2 %shard_map.151 = (f32[16,16,256]{2,1,0:T(8,128)S(1)}, f32[16,16,256]{2,1,0:T(8,128)S(1)}) custom-call(f32[16,16,256]{2,1,0:T(8,128)S(1)} %get-tuple-element.72.s.refs_0_.refs_8_, f32[16,16,256]{2,1,0:T(8,128)S(1)} %get-tuple-element.73.r.refs_1_.refs_9_), custom_call_target="tpu_custom_call" | custom-call | flops 1048576 | bytes 1048576 | tf_op jit(solution)/shard_map/pallas_call | solution.py:27
  42.8 0.4 collective-permute-done.12.refs_6_
  43.3 0.4 shard_map.152
  43.7 4.1 %collective-permute-start.15 = (f32[2,4,16,256]{3,2,1,0:T(8,128)S(1)}, f32[2,4,16,256]{3,2,1,0:T(8,128)S(1)}, u32[]{:S(2)}, u32[]{:S(2)}) collective-permute-start(f32[2,4,16,256]{3,2,1,0:T(8,128)S(1)} %get-tuple-element.87), channel_id=1, source_target_pairs={{0,248},{8,16},{16,8},{24,32},{32,24},{40,48},{48,40},{56,64},{64,... | collective-permute-start | bytes 393224 | tf_op jit(solution)/shard_map/ppermute | solution.py:267
  47.8 3.0 %collective-permute-start.14 = (f32[2,4,16,256]{3,2,1,0:T(8,128)S(1)}, f32[2,4,16,256]{3,2,1,0:T(8,128)S(1)}, u32[]{:S(2)}, u32[]{:S(2)}) collective-permute-start(f32[2,4,16,256]{3,2,1,0:T(8,128)S(1)} %get-tuple-element.86), channel_id=1, source_target_pairs={{0,8},{8,0},{16,24},{24,16},{32,40},{40,32},{48,56},{56,48},{64,72... | collective-permute-start | bytes 393224 | tf_op jit(solution)/shard_map/ppermute | solution.py:266
  50.8 0.1 collective-permute-start.16
  50.9 3.5 %collective-permute-start.17 = (f32[2,8,8,256]{3,2,1,0:T(8,128)S(1)}, f32[2,8,8,256]{3,2,1,0:T(8,128)S(1)}, u32[]{:S(2)}, u32[]{:S(2)}) collective-permute-start(f32[2,8,8,256]{3,2,1,0:T(8,128)S(1)} %get-tuple-element.89), channel_id=1, source_target_pairs={{0,7},{1,2},{2,1},{3,4},{4,3},{5,6},{6,5},{7,0},{8,15},{9,10},{10,... | collective-permute-start | bytes 393224 | tf_op jit(solution)/shard_map/ppermute | solution.py:268
  54.4 1.2 %shard_map.153 = (f32[16,16,256]{2,1,0:T(8,128)S(1)}, f32[16,16,256]{2,1,0:T(8,128)S(1)}) custom-call(f32[16,16,256]{2,1,0:T(8,128)S(1)} %get-tuple-element.82.s.refs_0_.refs_9_, f32[16,16,256]{2,1,0:T(8,128)S(1)} %get-tuple-element.83.r.refs_1_.refs_10_), custom_call_target="tpu_custom_call" | custom-call | flops 1048576 | bytes 1048576 | tf_op jit(solution)/shard_map/pallas_call | solution.py:27
  55.6 0.0 collective-permute-done.19.got
  55.6 0.6 collective-permute-start.25
  56.3 0.1 collective-permute-start.20
  56.4 5.1 %collective-permute-done.16.refs_6_ = f32[2,8,8,256]{3,2,1,0:T(8,128)S(1)} collective-permute-done((f32[2,8,8,256]{3,2,1,0:T(8,128)S(1)}, f32[2,8,8,256]{3,2,1,0:T(8,128)S(1)}, u32[]{:S(2)}, u32[]{:S(2)}) %collective-permute-start.16) | collective-permute-done | bytes 131104 | tf_op jit(solution)/shard_map/ppermute | solution.py:269
  61.5 0.0 collective-permute-done.17.refs_7_
  61.5 0.4 shard_map.154
  62.0 1.0 %collective-permute-start.18 = (f32[2,4,16,256]{3,2,1,0:T(8,128)S(1)}, f32[2,4,16,256]{3,2,1,0:T(8,128)S(1)}, u32[]{:S(2)}, u32[]{:S(2)}) collective-permute-start(f32[2,4,16,256]{3,2,1,0:T(8,128)S(1)} %get-tuple-element.91), channel_id=1, source_target_pairs={{0,8},{8,0},{16,24},{24,16},{32,40},{40,32},{48,56},{56,48},{64,72... | collective-permute-start | bytes 393224 | tf_op jit(solution)/shard_map/ppermute | solution.py:266
  63.0 0.1 collective-permute-start.22
  63.1 0.0 collective-permute-start.23
  63.1 3.5 %collective-permute-start.24 = (f32[2,8,8,256]{3,2,1,0:T(8,128)S(1)}, f32[2,8,8,256]{3,2,1,0:T(8,128)S(1)}, u32[]{:S(2)}, u32[]{:S(2)}) collective-permute-start(f32[2,8,8,256]{3,2,1,0:T(8,128)S(1)} %get-tuple-element.107), channel_id=1, source_target_pairs={{0,7},{1,2},{2,1},{3,4},{4,3},{5,6},{6,5},{7,0},{8,15},{9,10},{10,... | collective-permute-start | bytes 393224 | tf_op jit(solution)/shard_map/ppermute | solution.py:268
  66.6 0.0 collective-permute-done.18.after.refs_5_
  66.6 2.5 %collective-permute-start.21 = (f32[8,256]{1,0:T(8,128)S(1)}, f32[8,256]{1,0:T(8,128)S(1)}, u32[]{:S(2)}, u32[]{:S(2)}) collective-permute-start(f32[8,256]{1,0:T(8,128)S(1)} %get-tuple-element.98), channel_id=1, source_target_pairs={{0,8},{8,0},{16,24},{24,16},{32,40},{40,32},{48,56},{56,48},{64,72... | collective-permute-start | bytes 24584 | tf_op jit(solution)/shard_map/ppermute | solution.py:313
  69.2 1.2 %shard_map.159 = (f32[16,16,256]{2,1,0:T(8,128)S(1)}, f32[16,16,256]{2,1,0:T(8,128)S(1)}) custom-call(f32[16,16,256]{2,1,0:T(8,128)S(1)} %get-tuple-element.101.s.refs_1_, f32[16,16,256]{2,1,0:T(8,128)S(1)} %get-tuple-element.102.r.refs_2_), custom_call_target="tpu_custom_call" | custom-call | flops 1048576 | bytes 1048576 | tf_op jit(solution)/shard_map/pallas_call | solution.py:27
  70.4 0.0 collective-permute-done.21.got
  70.4 1.7 %shard_map.158 = (f32[16,16,256]{2,1,0:T(8,128)}, f32[8,128]{1,0:T(8,128)S(1)}) custom-call(s32[32]{0:T(128)S(1)} %bitcast.2, f32[8,256]{1,0:T(8,128)S(1)} %get-tuple-element.97.held, f32[8,256]{1,0:T(8,128)S(1)} %collective-permute-done.21.got, f32[16,16,256]{2,1,0:T(8,128)S(1)} %copy-done.6), custom_call_target="tpu_custom_call" | custom-call | flops 1048576 | bytes 1048576 | tf_op jit(solution)/shard_map/pallas_call | solution.py:27
  72.1 0.5 collective-permute-done.22.refs_6_
  72.6 0.0 collective-permute-done.23.refs_7_
  72.6 0.0 collective-permute-done.24.refs_8_
  72.6 1.3 %shard_map.161 = (f32[16,16,256]{2,1,0:T(8,128)}, f32[16,16,256]{2,1,0:T(8,128)}, f32[16,16,256]{2,1,0:T(8,128)}, f32[16,16,256]{2,1,0:T(8,128)}, f32[16,16,256]{2,1,0:T(8,128)}) custom-call(f32[8,128]{1,0:T(8,128)S(1)} %get-tuple-element.100.refs_0_, f32[16,16,256]{2,1,0:T(8,128)S(1)} %get-tuple-element.101.s.refs_1_, ...), custom_call_target="tpu_custom_call" | custom-call | flops 1048576 | bytes 1048576 | tf_op jit(solution)/shard_map/pallas_call | solution.py:27
  (29 shorter events, 0.1 us)
Async XLA Ops:
  0.6 14.4 %collective-permute-start = (f32[16,16,256]{2,1,0:T(8,128)}, f32[16,16,256]{2,1,0:T(8,128)S(1)}, u32[]{:S(2)}, u32[]{:S(2)}) collective-permute-start(f32[16,16,256]{2,1,0:T(8,128)} %s.1), channel_id=1, source_target_pairs={{0,248},{8,0},{16,8},{24,16},{32,24},{40,32},{48,40},{56,48},{64,5... | collective-permute-start | bytes 786440 | tf_op jit(solution)/shard_map/ppermute | solution.py:277
  4.0 11.1 %collective-permute-start.1 = (f32[16,16,256]{2,1,0:T(8,128)}, f32[16,16,256]{2,1,0:T(8,128)S(1)}, u32[]{:S(2)}, u32[]{:S(2)}) collective-permute-start(f32[16,16,256]{2,1,0:T(8,128)} %r.1), channel_id=1, source_target_pairs={{0,248},{8,0},{16,8},{24,16},{32,24},{40,32},{48,40},{56,48},{64,5... | collective-permute-start | bytes 786440 | tf_op jit(solution)/shard_map/ppermute | solution.py:278
  10.1 0.9 %copy-start = (f32[16,16,256]{2,1,0:T(8,128)S(1)}, f32[16,16,256]{2,1,0:T(8,128)}, u32[]{:S(2)}) copy-start(f32[16,16,256]{2,1,0:T(8,128)} %refs_14_.1) | copy-start | bytes 786436
  11.1 0.9 %copy-start.2 = (f32[16,16,256]{2,1,0:T(8,128)S(1)}, f32[16,16,256]{2,1,0:T(8,128)}, u32[]{:S(2)}) copy-start(f32[16,16,256]{2,1,0:T(8,128)} %refs_12_.1) | copy-start | bytes 786436
  12.0 0.9 %copy-start.7 = (f32[16,16,256]{2,1,0:T(8,128)S(1)}, f32[16,16,256]{2,1,0:T(8,128)}, u32[]{:S(2)}) copy-start(f32[16,16,256]{2,1,0:T(8,128)} %refs_10_.1) | copy-start | bytes 786436
  12.0 1.7 %copy-start.4 = (f32[16,16,256]{2,1,0:T(8,128)S(1)}, f32[16,16,256]{2,1,0:T(8,128)}, u32[]{:S(2)}) copy-start(f32[16,16,256]{2,1,0:T(8,128)} %s.1) | copy-start | bytes 786436
  12.0 1.7 %copy-start.5 = (f32[16,16,256]{2,1,0:T(8,128)S(1)}, f32[16,16,256]{2,1,0:T(8,128)}, u32[]{:S(2)}) copy-start(f32[16,16,256]{2,1,0:T(8,128)} %r.1) | copy-start | bytes 786436
  12.1 7.4 %collective-permute-start.3 = (f32[16,16,256]{2,1,0:T(8,128)S(1)}, f32[16,16,256]{2,1,0:T(8,128)S(1)}, u32[]{:S(2)}, u32[]{:S(2)}) collective-permute-start(f32[16,16,256]{2,1,0:T(8,128)S(1)} %shard_map.147), channel_id=1, source_target_pairs={{0,248},{8,0},{16,8},{24,16},{32,24},{40,32},{48,40},{56,48},{64,5... | collective-permute-start | bytes 786440 | tf_op jit(solution)/shard_map/ppermute | solution.py:282
  13.0 11.1 %collective-permute-start.8 = (f32[16,16,256]{2,1,0:T(8,128)S(1)}, f32[16,16,256]{2,1,0:T(8,128)S(1)}, u32[]{:S(2)}, u32[]{:S(2)}) collective-permute-start(f32[16,16,256]{2,1,0:T(8,128)S(1)} %copy-done.7), channel_id=1, source_target_pairs={{0,248},{8,0},{16,8},{24,16},{32,24},{40,32},{48,40},{56,48},{64,5... | collective-permute-start | bytes 786440 | tf_op jit(solution)/shard_map/ppermute | solution.py:279
  13.7 17.0 %collective-permute-start.9 = (f32[16,16,256]{2,1,0:T(8,128)}, f32[16,16,256]{2,1,0:T(8,128)S(1)}, u32[]{:S(2)}, u32[]{:S(2)}) collective-permute-start(f32[16,16,256]{2,1,0:T(8,128)} %refs_11_.1), channel_id=1, source_target_pairs={{0,248},{8,0},{16,8},{24,16},{32,24},{40,32},{48,40},{56,48},{64,5... | collective-permute-start | bytes 786440 | tf_op jit(solution)/shard_map/ppermute | solution.py:280
  13.8 0.7 copy-start.11
  15.0 8.1 %copy-start.1 = (f32[16,16,256]{2,1,0:T(8,128)S(1)}, f32[16,16,256]{2,1,0:T(8,128)}, u32[]{:S(2)}) copy-start(f32[16,16,256]{2,1,0:T(8,128)} %refs_14_.1) | copy-start | bytes 786436
  15.2 4.6 %collective-permute-start.2 = (f32[2,4,16,256]{3,2,1,0:T(8,128)S(1)}, f32[2,4,16,256]{3,2,1,0:T(8,128)S(1)}, u32[]{:S(2)}, u32[]{:S(2)}) collective-permute-start(f32[2,4,16,256]{3,2,1,0:T(8,128)S(1)} %get-tuple-element.63), channel_id=1, source_target_pairs={{0,8},{8,0},{16,24},{24,16},{32,40},{40,32},{48,56},{56,48},{64,72... | collective-permute-start | bytes 393224 | tf_op jit(solution)/shard_map/ppermute | solution.py:266
  17.9 14.2 %collective-permute-start.5 = (f32[2,4,16,256]{3,2,1,0:T(8,128)S(1)}, f32[2,4,16,256]{3,2,1,0:T(8,128)S(1)}, u32[]{:S(2)}, u32[]{:S(2)}) collective-permute-start(f32[2,4,16,256]{3,2,1,0:T(8,128)S(1)} %get-tuple-element.69), channel_id=1, source_target_pairs={{0,248},{8,16},{16,8},{24,32},{32,24},{40,48},{48,40},{56,64},{64,... | collective-permute-start | bytes 393224 | tf_op jit(solution)/shard_map/ppermute | solution.py:267
  19.5 12.6 %collective-permute-start.6 = (f32[2,8,8,256]{3,2,1,0:T(8,128)S(1)}, f32[2,8,8,256]{3,2,1,0:T(8,128)S(1)}, u32[]{:S(2)}, u32[]{:S(2)}) collective-permute-start(f32[2,8,8,256]{3,2,1,0:T(8,128)S(1)} %get-tuple-element.70), channel_id=1, source_target_pairs={{0,1},{1,0},{2,3},{3,2},{4,5},{5,4},{6,7},{7,6},{8,9},{9,8},{10,11... | collective-permute-start | bytes 393224 | tf_op jit(solution)/shard_map/ppermute | solution.py:269
  19.9 3.3 %copy-start.10 = (s32[1,32]{1,0:T(1,128)S(1)}, s32[1,32]{1,0:T(1,128)}, u32[]{:S(2)}) copy-start(s32[1,32]{1,0:T(1,128)} %param.19) | copy-start | bytes 388
  19.9 12.2 %collective-permute-start.7 = (f32[2,8,8,256]{3,2,1,0:T(8,128)S(1)}, f32[2,8,8,256]{3,2,1,0:T(8,128)S(1)}, u32[]{:S(2)}, u32[]{:S(2)}) collective-permute-start(f32[2,8,8,256]{3,2,1,0:T(8,128)S(1)} %get-tuple-element.71), channel_id=1, source_target_pairs={{0,7},{1,2},{2,1},{3,4},{4,3},{5,6},{6,5},{7,0},{8,15},{9,10},{10,... | collective-permute-start | bytes 393224 | tf_op jit(solution)/shard_map/ppermute | solution.py:268
  23.1 9.0 %copy-start.9 = (f32[16,16,256]{2,1,0:T(8,128)S(1)}, f32[16,16,256]{2,1,0:T(8,128)}, u32[]{:S(2)}) copy-start(f32[16,16,256]{2,1,0:T(8,128)} %refs_13_.1) | copy-start | bytes 786436
  24.1 8.0 %collective-permute-start.4 = (f32[64,256]{1,0:T(8,128)S(1)}, f32[64,256]{1,0:T(8,128)S(1)}, u32[]{:S(2)}, u32[]{:S(2)}) collective-permute-start(f32[64,256]{1,0:T(8,128)S(1)} %get-tuple-element.64), channel_id=1, source_target_pairs={{0,64},{8,72},{16,80},{24,88},{32,96},{40,104},{48,112},{56,120},{... | collective-permute-start | bytes 196616 | tf_op jit(solution)/shard_map/ppermute | solution.py:313
  24.2 7.9 %copy-start.3 = (f32[16,16,256]{2,1,0:T(8,128)S(1)}, f32[16,16,256]{2,1,0:T(8,128)}, u32[]{:S(2)}) copy-start(f32[16,16,256]{2,1,0:T(8,128)} %refs_12_.1) | copy-start | bytes 786436
  24.2 7.9 %copy-start.8 = (f32[16,16,256]{2,1,0:T(8,128)S(1)}, f32[16,16,256]{2,1,0:T(8,128)}, u32[]{:S(2)}) copy-start(f32[16,16,256]{2,1,0:T(8,128)} %refs_11_.1) | copy-start | bytes 786436
  32.7 6.7 %collective-permute-start.11 = (f32[2,4,16,256]{3,2,1,0:T(8,128)S(1)}, f32[2,4,16,256]{3,2,1,0:T(8,128)S(1)}, u32[]{:S(2)}, u32[]{:S(2)}) collective-permute-start(f32[2,4,16,256]{3,2,1,0:T(8,128)S(1)} %get-tuple-element.77), channel_id=1, source_target_pairs={{0,248},{8,16},{16,8},{24,32},{32,24},{40,48},{48,40},{56,64},{64,... | collective-permute-start | bytes 393224 | tf_op jit(solution)/shard_map/ppermute | solution.py:267
  35.7 7.1 %collective-permute-start.10 = (f32[2,4,16,256]{3,2,1,0:T(8,128)S(1)}, f32[2,4,16,256]{3,2,1,0:T(8,128)S(1)}, u32[]{:S(2)}, u32[]{:S(2)}) collective-permute-start(f32[2,4,16,256]{3,2,1,0:T(8,128)S(1)} %get-tuple-element.76), channel_id=1, source_target_pairs={{0,8},{8,0},{16,24},{24,16},{32,40},{40,32},{48,56},{56,48},{64,72... | collective-permute-start | bytes 393224 | tf_op jit(solution)/shard_map/ppermute | solution.py:266
  35.7 7.5 %collective-permute-start.12 = (f32[2,8,8,256]{3,2,1,0:T(8,128)S(1)}, f32[2,8,8,256]{3,2,1,0:T(8,128)S(1)}, u32[]{:S(2)}, u32[]{:S(2)}) collective-permute-start(f32[2,8,8,256]{3,2,1,0:T(8,128)S(1)} %get-tuple-element.78), channel_id=1, source_target_pairs={{0,1},{1,0},{2,3},{3,2},{4,5},{5,4},{6,7},{7,6},{8,9},{9,8},{10,11... | collective-permute-start | bytes 393224 | tf_op jit(solution)/shard_map/ppermute | solution.py:269
  35.7 7.5 %collective-permute-start.13 = (f32[2,8,8,256]{3,2,1,0:T(8,128)S(1)}, f32[2,8,8,256]{3,2,1,0:T(8,128)S(1)}, u32[]{:S(2)}, u32[]{:S(2)}) collective-permute-start(f32[2,8,8,256]{3,2,1,0:T(8,128)S(1)} %get-tuple-element.79), channel_id=1, source_target_pairs={{0,7},{1,2},{2,1},{3,4},{4,3},{5,6},{6,5},{7,0},{8,15},{9,10},{10,... | collective-permute-start | bytes 393224 | tf_op jit(solution)/shard_map/ppermute | solution.py:268
  39.4 16.2 %collective-permute-start.19 = (f32[32,256]{1,0:T(8,128)S(1)}, f32[32,256]{1,0:T(8,128)S(1)}, u32[]{:S(2)}, u32[]{:S(2)}) collective-permute-start(f32[32,256]{1,0:T(8,128)S(1)} %get-tuple-element.94), channel_id=1, source_target_pairs={{0,32},{8,40},{16,48},{24,56},{32,0},{40,8},{48,16},{56,24},{64,96... | collective-permute-start | bytes 98312 | tf_op jit(solution)/shard_map/ppermute | solution.py:313
  43.7 12.6 %collective-permute-start.15 = (f32[2,4,16,256]{3,2,1,0:T(8,128)S(1)}, f32[2,4,16,256]{3,2,1,0:T(8,128)S(1)}, u32[]{:S(2)}, u32[]{:S(2)}) collective-permute-start(f32[2,4,16,256]{3,2,1,0:T(8,128)S(1)} %get-tuple-element.87), channel_id=1, source_target_pairs={{0,248},{8,16},{16,8},{24,32},{32,24},{40,48},{48,40},{56,64},{64,... | collective-permute-start | bytes 393224 | tf_op jit(solution)/shard_map/ppermute | solution.py:267
  47.8 8.6 %collective-permute-start.14 = (f32[2,4,16,256]{3,2,1,0:T(8,128)S(1)}, f32[2,4,16,256]{3,2,1,0:T(8,128)S(1)}, u32[]{:S(2)}, u32[]{:S(2)}) collective-permute-start(f32[2,4,16,256]{3,2,1,0:T(8,128)S(1)} %get-tuple-element.86), channel_id=1, source_target_pairs={{0,8},{8,0},{16,24},{24,16},{32,40},{40,32},{48,56},{56,48},{64,72... | collective-permute-start | bytes 393224 | tf_op jit(solution)/shard_map/ppermute | solution.py:266
  50.8 10.7 %collective-permute-start.16 = (f32[2,8,8,256]{3,2,1,0:T(8,128)S(1)}, f32[2,8,8,256]{3,2,1,0:T(8,128)S(1)}, u32[]{:S(2)}, u32[]{:S(2)}) collective-permute-start(f32[2,8,8,256]{3,2,1,0:T(8,128)S(1)} %get-tuple-element.88), channel_id=1, source_target_pairs={{0,1},{1,0},{2,3},{3,2},{4,5},{5,4},{6,7},{7,6},{8,9},{9,8},{10,11... | collective-permute-start | bytes 393224 | tf_op jit(solution)/shard_map/ppermute | solution.py:269
  50.9 10.6 %collective-permute-start.17 = (f32[2,8,8,256]{3,2,1,0:T(8,128)S(1)}, f32[2,8,8,256]{3,2,1,0:T(8,128)S(1)}, u32[]{:S(2)}, u32[]{:S(2)}) collective-permute-start(f32[2,8,8,256]{3,2,1,0:T(8,128)S(1)} %get-tuple-element.89), channel_id=1, source_target_pairs={{0,7},{1,2},{2,1},{3,4},{4,3},{5,6},{6,5},{7,0},{8,15},{9,10},{10,... | collective-permute-start | bytes 393224 | tf_op jit(solution)/shard_map/ppermute | solution.py:268
  55.6 17.0 %collective-permute-start.25 = (f32[16,16,256]{2,1,0:T(8,128)S(1)}, f32[16,16,256]{2,1,0:T(8,128)S(1)}, u32[]{:S(2)}, u32[]{:S(2)}) collective-permute-start(f32[16,16,256]{2,1,0:T(8,128)S(1)} %shard_map.160), channel_id=1, source_target_pairs={{0,248},{8,0},{16,8},{24,16},{32,24},{40,32},{48,40},{56,48},{64,5... | collective-permute-start | bytes 786440 | tf_op jit(solution)/shard_map/ppermute | solution.py:317
  56.3 6.8 %collective-permute-start.20 = (f32[16,256]{1,0:T(8,128)S(1)}, f32[16,256]{1,0:T(8,128)S(1)}, u32[]{:S(2)}, u32[]{:S(2)}) collective-permute-start(f32[16,256]{1,0:T(8,128)S(1)} %get-tuple-element.96), channel_id=1, source_target_pairs={{0,16},{8,24},{16,0},{24,8},{32,48},{40,56},{48,32},{56,40},{64,80... | collective-permute-start | bytes 49160 | tf_op jit(solution)/shard_map/ppermute | solution.py:313
  62.0 4.7 %collective-permute-start.18 = (f32[2,4,16,256]{3,2,1,0:T(8,128)S(1)}, f32[2,4,16,256]{3,2,1,0:T(8,128)S(1)}, u32[]{:S(2)}, u32[]{:S(2)}) collective-permute-start(f32[2,4,16,256]{3,2,1,0:T(8,128)S(1)} %get-tuple-element.91), channel_id=1, source_target_pairs={{0,8},{8,0},{16,24},{24,16},{32,40},{40,32},{48,56},{56,48},{64,72... | collective-permute-start | bytes 393224 | tf_op jit(solution)/shard_map/ppermute | solution.py:266
  63.0 9.6 %collective-permute-start.22 = (f32[2,4,16,256]{3,2,1,0:T(8,128)S(1)}, f32[2,4,16,256]{3,2,1,0:T(8,128)S(1)}, u32[]{:S(2)}, u32[]{:S(2)}) collective-permute-start(f32[2,4,16,256]{3,2,1,0:T(8,128)S(1)} %get-tuple-element.105), channel_id=1, source_target_pairs={{0,248},{8,16},{16,8},{24,32},{32,24},{40,48},{48,40},{56,64},{64,... | collective-permute-start | bytes 393224 | tf_op jit(solution)/shard_map/ppermute | solution.py:267
  63.1 9.5 %collective-permute-start.23 = (f32[2,8,8,256]{3,2,1,0:T(8,128)S(1)}, f32[2,8,8,256]{3,2,1,0:T(8,128)S(1)}, u32[]{:S(2)}, u32[]{:S(2)}) collective-permute-start(f32[2,8,8,256]{3,2,1,0:T(8,128)S(1)} %get-tuple-element.106), channel_id=1, source_target_pairs={{0,1},{1,0},{2,3},{3,2},{4,5},{5,4},{6,7},{7,6},{8,9},{9,8},{10,11... | collective-permute-start | bytes 393224 | tf_op jit(solution)/shard_map/ppermute | solution.py:269
  63.1 9.5 %collective-permute-start.24 = (f32[2,8,8,256]{3,2,1,0:T(8,128)S(1)}, f32[2,8,8,256]{3,2,1,0:T(8,128)S(1)}, u32[]{:S(2)}, u32[]{:S(2)}) collective-permute-start(f32[2,8,8,256]{3,2,1,0:T(8,128)S(1)} %get-tuple-element.107), channel_id=1, source_target_pairs={{0,7},{1,2},{2,1},{3,4},{4,3},{5,6},{6,5},{7,0},{8,15},{9,10},{10,... | collective-permute-start | bytes 393224 | tf_op jit(solution)/shard_map/ppermute | solution.py:268
  66.6 3.8 %collective-permute-start.21 = (f32[8,256]{1,0:T(8,128)S(1)}, f32[8,256]{1,0:T(8,128)S(1)}, u32[]{:S(2)}, u32[]{:S(2)}) collective-permute-start(f32[8,256]{1,0:T(8,128)S(1)} %get-tuple-element.98), channel_id=1, source_target_pairs={{0,8},{8,0},{16,24},{24,16},{32,40},{40,32},{48,56},{56,48},{64,72... | collective-permute-start | bytes 24584 | tf_op jit(solution)/shard_map/ppermute | solution.py:313
  69.2 1.2 %copy-start.6 = (f32[16,16,256]{2,1,0:T(8,128)S(1)}, f32[16,16,256]{2,1,0:T(8,128)}, u32[]{:S(2)}) copy-start(f32[16,16,256]{2,1,0:T(8,128)} %base.1) | copy-start | bytes 786436

commit v6 on v5

--- a/solution.py
+++ b/solution.py
@@ -130,8 +130,65 @@
     mask[...] = jnp.where(flags == 1, F32(1.0), F32(0.0))
 
 
-def first_kernel(vel, image, out):
-    out[...] = jnp.where(place()[0] == 0, image[...], vel[...])
+RIM = (0, 1, 2, 3, 12, 13, 14, 15)
+
+
+def rim_kernel(s, r, vel, image, s_out, r_out, vel_out):
+    first = place()[0] == 0
+    for j, x in enumerate(RIM):
+        rows = slice(16 * j, 16 * j + 16)
+        s_out[rows] = s[x]
+        r_out[rows] = jnp.where(first, image[12 + j], r[x]) if j < 4 else r[x]
+        vel_out[rows] = jnp.where(first, image[j], vel[x])
+    for j in range(8):
+        x, at, row = 4 + j, 128 + 8 * j, 8 * (j % 2)
+        for part, y in ((0, 0), (4, 12)):
+            rows = slice(at + part, at + part + 4)
+            s_out[rows] = s[x, y : y + 4]
+            r_out[rows] = r[x, y : y + 4]
+            vel_out[rows] = jnp.where(
+                first, image[8 + j // 2, row + part : row + part + 4], vel[x, y : y + 4]
+            )
+
+
+def rim_plane(rim, x):
+    if x in RIM:
+        at = 16 * RIM.index(x)
+        return rim[at : at + 16]
+    block = rim[128 + 8 * (x - 4) : 136 + 8 * (x - 4)]
+    return jnp.concatenate([block, block], axis=0)
+
+
+def core_kernel(after, s, r, vel, out):
+    for i, ref in enumerate((s, r, vel)):
+        out[i, :, 4:8, :] = ref[4:12, 4:8, :]
+        out[i, :, 0:4, :] = ref[4:12, 8:12, :]
+
+
+def patch_kernel(
+    moves, s, r, s_lap, r_lap, s_prev, r_prev, vel_own, vel_end, come,
+    s_new, r_new, vel, picture, s_out, r_out, vel_out, picture_out,
+):
+    moved = moves[...] == 1.0
+    arrives = place()[0] < 31
+    row = lax.broadcasted_iota(jnp.int32, (16, 256), 0)
+    core = (row >= 4) & (row < 12)
+    for x in range(16):
+        if x in RIM:
+            s_out[x] = s_new[x]
+            r_out[x] = r_new[x]
+            vel_out[x] = vel[x]
+            picture_out[x] = picture[x]
+            continue
+        full = [jnp.concatenate([come[i, x - 4]] * 2, axis=0) for i in range(3)]
+        new = jnp.where(moved, jnp.where(arrives, full[2], vel_end[x]), vel_own[x])
+        vel_out[x] = jnp.where(core, new, vel[x])
+        for f, (field, lap, prev, old, out) in enumerate(
+            ((s, s_lap, s_prev, s_new, s_out), (r, r_lap, r_prev, r_new, r_out))
+        ):
+            before = jnp.where(moved, jnp.where(arrives, full[f], F32(0.0)), prev[x])
+            out[x] = jnp.where(core, 2.0 * field[x] - before + new * lap[x], old[x])
+        picture_out[x] = jnp.where(core, s_out[x] * r_out[x], picture[x])
 
 
 def copy_kernel(after, a, out):
@@ -167,7 +224,7 @@
         r_before[...] = r[...]
     if step == 0:
         for x in range(16):
-            new = jnp.where(arrives, vel_come[x], vel_end[x])
+            new = jnp.where(arrives, rim_plane(vel_come, x), vel_end[x])
             vel[x] = jnp.where(moved, new, vel_own[x])
     if step > 0:
         s_come = r_come = None
@@ -177,7 +234,7 @@
         planes, lows, highs = face_terms(halos, f)
         for x in range(16):
             if step == 0:
-                old = jnp.where(moved, jnp.where(arrives, come[x], F32(0.0)), prev[x])
+                old = jnp.where(moved, jnp.where(arrives, rim_plane(come, x), F32(0.0)), prev[x])
             else:
                 old = prev[x]
             ends = jnp.concatenate([lows[x // 8][x % 8], highs[x // 8][x % 8]], axis=0)
@@ -210,7 +267,7 @@
     high[...] = jnp.where(holds, held[half:], got[half:])
 
 
-def scatter_kernel(after, moves, owner, image, come, low, high):
+def scatter_kernel(after, moves, owner, image, most, rest, low, high):
     upper = lax.axis_index("gx") >= 16
     z = lax.broadcasted_iota(jnp.int32, (8, 256), 1)
     target = jnp.zeros((8, 256), jnp.int32)
@@ -219,8 +276,10 @@
     target = jnp.where(upper, 31 - target, target) * 8 + lax.rem(z, 8)
     rows = lax.broadcasted_iota(jnp.int32, (128, 256), 0)
     pick = jnp.where(rows == target[0:1, :], F32(1.0), F32(0.0))
-    tile = jnp.where(upper, come[...], image[...])
-    leaving = jnp.where((moves[...] == 1.0)[None], tile, F32(0.0)).reshape(256, 256)
+    end = jnp.concatenate([most[...], rest[:64]], axis=0)
+    tile = jnp.where(upper, end, image[...].reshape(256, 256))
+    leaves = jnp.broadcast_to((moves[...] == 1.0)[None], (16, 16, 256)).reshape(256, 256)
+    leaving = jnp.where(leaves, tile, F32(0.0))
     slabs = lax.dot_general(
         pick, leaving, (((1,), (1,)), ((), ())), precision=HIGHEST, preferred_element_type=F32
     )
@@ -276,10 +335,8 @@
 
     s_come = lax.ppermute(src_cur, "gx", west)
     r_come = lax.ppermute(rcv_cur, "gx", west)
-    sp_come = lax.ppermute(src_prev, "gx", west)
-    rp_come = lax.ppermute(rcv_prev, "gx", west)
-    (vel_send,) = call(first_kernel, [tile], [], courant, image)
-    vel_come = lax.ppermute(vel_send, "gx", west)
+    rims = call(rim_kernel, [sds(192, 256)] * 3, [], src_prev, rcv_prev, courant, image)
+    vel_come, sp_come, rp_come = [lax.ppermute(rims[i], "gx", west) for i in (2, 0, 1)]
     s_own, r_own, mask = call(
         own_kernel, [tile] * 2 + [sds(16, 256)], [], shift_map, src_cur, rcv_cur
     )
@@ -299,6 +356,7 @@
                 owner,
                 image,
                 vel_come,
+                rp_come,
                 after=(halos[0],),
             )
         else:
@@ -311,7 +369,32 @@
                 after=(halos[1] if step in (1, 2,) else halos[0],),
             )
         got = lax.ppermute(high, "gx", [(i, i ^ (8 >> step)) for i in range(n)])
+        if step == 1:
+            s, r, velocity, picture = call(
+                patch_kernel,
+                [tile] * 4,
+                [],
+                mask,
+                s_old,
+                r_old,
+                s_lap,
+                r_lap,
+                src_prev,
+                rcv_prev,
+                courant,
+                vel_entering,
+                core_come,
+                s,
+                r,
+                velocity,
+                picture,
+            )
         s_lap, r_lap = call(interior_kernel, [tile, tile], scratch, s, r)
+        if step == 0:
+            (core,) = call(
+                core_kernel, [sds(3, 8, 8, 256)], [], src_prev, rcv_prev, courant, after=(s_lap,)
+            )
+            core_come = lax.ppermute(core, "gx", west)
         if step == 2:
             (image_send,) = call(copy_kernel, [tile], [], image, after=(s_lap,))
             image_come = lax.ppermute(image_send, "gx", west)

time: 74.1 us -> 73.9 us (level); the launches traced: 73.9 us -> 72.6 us
  waiting for transfers between devices: 13.6 us -> 9.61 us
  local copies, waits for them, and re-layouts: 2.75 us -> 4.08 us
  starting transfers between devices: 45.6 us -> 46.8 us
    ppermute x4, waiting for transfers between devices: 5.53 us -> 0.56 us  [swap(): y1 = lax.ppermute(y1, 'gy', pair_y)]
    ppermute x4, waiting for transfers between devices: 1.88 us -> 6.05 us  [swap(): od = lax.ppermute(od, 'gx', odd_x)]
    ppermute x3 -> x4, waiting for transfers between devices: 6.14 us -> 2.96 us  [the longest x3 2.96 us: body(): lax.ppermute(rims[i], 'gx', west)]
    ppermute x4, starting transfers between devices: 7.9 us -> 10.6 us  [swap(): od = lax.ppermute(od, 'gx', odd_x)]
    ppermute x4, starting transfers between devices: 4.9 us -> 3.03 us  [body(): got = lax.ppermute(high, 'gx', [(i, i ^ 8 >> step) for i in range(n)])]
    ppermute x3 -> x4, starting transfers between devices: 1.52 us -> 3.04 us  [the longest x1 1.83 us: body(): core_come = lax.ppermute(core, 'gx', west)]
    ppermute x4, starting transfers between devices: 6.7 us -> 5.32 us  [swap(): x1 = lax.ppermute(x1, 'gx', pair_x)]
    unnamed x24 -> x28, local copies, waits for them, and re-layouts: 2.75 us -> 4.08 us
  transfers between devices with their start and end apart: 26 -> 27, of which waited for: 6 -> 6; matrix products, arithmetic and copies ran while one was open for 0% -> 0% of each run, Pallas kernels for 12% -> 14%
where the time goes in v6:
time: 73.9 us; the launch traced here: 72.6 us
  starting transfers between devices  46.8 us (63%)
  Pallas kernels  11.2 us (15%)
  waiting for transfers between devices  9.61 us (13%)
  local copies, waits for them, and re-layouts  4.08 us (6%)
  between operations  0.94 us (1%)
    ppermute x4, starting transfers between devices, swap(): yo = lax.ppermute(yo, 'gy', odd_y)  13.7 us
    pallas_call x19, Pallas kernels, call(): pl.pallas_call(kernel, out_shape=outs, in_specs=specs, out_specs=[pl.Bloc...  11.2 us
    ppermute x4, starting transfers between devices, swap(): od = lax.ppermute(od, 'gx', odd_x)  10.6 us
    ppermute x1, starting transfers between devices, body(): r_come = lax.ppermute(rcv_cur, 'gx', west)  6.19 us
    ppermute x4, waiting for transfers between devices, swap(): od = lax.ppermute(od, 'gx', odd_x)  6.05 us
    ppermute x4, starting transfers between devices, swap(): x1 = lax.ppermute(x1, 'gx', pair_x)  5.32 us
    unnamed x28, local copies, waits for them, and re-layouts  4.08 us
    ppermute x1, starting transfers between devices, body(): s_come = lax.ppermute(src_cur, 'gx', west)  3.32 us
  transfers between devices with their start and end apart: 27, of which 6 were waited for; matrix products, arithmetic and copies ran while one was open for 0% of the time, Pallas kernels for 14%

profile of v6, /device:TPU:1, one launch (start us, length us, event | category | flops | bytes accessed | tf_op | source)
XLA Modules:
  0.0 72.6 jit_solution(8423856975953505985)
XLA Ops:
  0.6 3.3 %collective-permute-start = (f32[16,16,256]{2,1,0:T(8,128)}, f32[16,16,256]{2,1,0:T(8,128)S(1)}, u32[]{:S(2)}, u32[]{:S(2)}) collective-permute-start(f32[16,16,256]{2,1,0:T(8,128)} %s.3), channel_id=1, source_target_pairs={{0,248},{8,0},{16,8},{24,16},{32,24},{40,32},{48,40},{56,48},{64,5... | collective-permute-start | bytes 786440 | tf_op jit(solution)/shard_map/ppermute | solution.py:336
  4.0 6.2 %collective-permute-start.1 = (f32[16,16,256]{2,1,0:T(8,128)}, f32[16,16,256]{2,1,0:T(8,128)S(1)}, u32[]{:S(2)}, u32[]{:S(2)}) collective-permute-start(f32[16,16,256]{2,1,0:T(8,128)} %r.3), channel_id=1, source_target_pairs={{0,248},{8,0},{16,8},{24,16},{32,24},{40,32},{48,40},{56,48},{64,5... | collective-permute-start | bytes 786440 | tf_op jit(solution)/shard_map/ppermute | solution.py:337
  10.1 0.9 %copy-done = f32[16,16,256]{2,1,0:T(8,128)S(1)} copy-done((f32[16,16,256]{2,1,0:T(8,128)S(1)}, f32[16,16,256]{2,1,0:T(8,128)}, u32[]{:S(2)}) %copy-start) | copy-done | bytes 262168
  11.1 0.9 %copy-done.2 = f32[16,16,256]{2,1,0:T(8,128)S(1)} copy-done((f32[16,16,256]{2,1,0:T(8,128)S(1)}, f32[16,16,256]{2,1,0:T(8,128)}, u32[]{:S(2)}) %copy-start.2) | copy-done | bytes 262168
  12.0 0.9 %copy-done.4 = f32[16,16,256]{2,1,0:T(8,128)S(1)} copy-done((f32[16,16,256]{2,1,0:T(8,128)S(1)}, f32[16,16,256]{2,1,0:T(8,128)}, u32[]{:S(2)}) %copy-start.4) | copy-done | bytes 262168
  13.0 0.9 %copy-done.6 = f32[16,16,256]{2,1,0:T(8,128)S(1)} copy-done((f32[16,16,256]{2,1,0:T(8,128)S(1)}, f32[16,16,256]{2,1,0:T(8,128)}, u32[]{:S(2)}) %copy-start.6) | copy-done | bytes 262168
  13.9 0.1 shard_map.149
  14.0 0.8 %collective-permute-start.4 = (f32[192,256]{1,0:T(8,128)S(1)}, f32[192,256]{1,0:T(8,128)S(1)}, u32[]{:S(2)}, u32[]{:S(2)}) collective-permute-start(f32[192,256]{1,0:T(8,128)S(1)} %get-tuple-element.75), channel_id=1, source_target_pairs={{0,248},{8,0},{16,8},{24,16},{32,24},{40,32},{48,40},{56,48},{64,5... | collective-permute-start | bytes 589832 | tf_op jit(solution)/shard_map/ppermute | solution.py:339
  14.8 0.1 collective-permute-start.5
  14.9 0.3 collective-permute-start.10
  15.2 0.2 copy-done.13
  15.5 0.6 shard_map.145
  16.1 0.0 copy-start.7
  16.1 0.2 shard_map.146
  16.3 2.9 %collective-permute-start.3 = (f32[2,4,16,256]{3,2,1,0:T(8,128)S(1)}, f32[2,4,16,256]{3,2,1,0:T(8,128)S(1)}, u32[]{:S(2)}, u32[]{:S(2)}) collective-permute-start(f32[2,4,16,256]{3,2,1,0:T(8,128)S(1)} %get-tuple-element.74), channel_id=1, source_target_pairs={{0,8},{8,0},{16,24},{24,16},{32,40},{40,32},{48,56},{56,48},{64,72... | collective-permute-start | bytes 393224 | tf_op jit(solution)/shard_map/ppermute | solution.py:325
  19.2 0.2 collective-permute-start.7
  19.5 1.2 %collective-permute-done.4.most.refs_16_ = f32[192,256]{1,0:T(8,128)S(1)} collective-permute-done((f32[192,256]{1,0:T(8,128)S(1)}, f32[192,256]{1,0:T(8,128)S(1)}, u32[]{:S(2)}, u32[]{:S(2)}) %collective-permute-start.4) | collective-permute-done | bytes 196640 | tf_op jit(solution)/shard_map/ppermute | solution.py:339
  20.7 0.4 collective-permute-start.8
  21.1 1.7 %collective-permute-done.5.rest.refs_15_ = f32[192,256]{1,0:T(8,128)S(1)} collective-permute-done((f32[192,256]{1,0:T(8,128)S(1)}, f32[192,256]{1,0:T(8,128)S(1)}, u32[]{:S(2)}, u32[]{:S(2)}) %collective-permute-start.5) | collective-permute-done | bytes 196640 | tf_op jit(solution)/shard_map/ppermute | solution.py:339
  22.8 2.6 %collective-permute-start.9 = (f32[2,8,8,256]{3,2,1,0:T(8,128)S(1)}, f32[2,8,8,256]{3,2,1,0:T(8,128)S(1)}, u32[]{:S(2)}, u32[]{:S(2)}) collective-permute-start(f32[2,8,8,256]{3,2,1,0:T(8,128)S(1)} %get-tuple-element.80), channel_id=1, source_target_pairs={{0,7},{1,2},{2,1},{3,4},{4,3},{5,6},{6,5},{7,0},{8,15},{9,10},{10,... | collective-permute-start | bytes 393224 | tf_op jit(solution)/shard_map/ppermute | solution.py:327
  25.4 0.0 collective-permute-done.3.after.refs_5_
  25.4 0.0 copy-start.5
  25.4 0.9 %shard_map.150 = (f32[64,256]{1,0:T(8,128)S(1)}, f32[64,256]{1,0:T(8,128)S(1)}) custom-call(f32[2,4,16,256]{3,2,1,0:T(8,128)S(1)} %collective-permute-done.3.after.refs_5_, f32[16,256]{1,0:T(8,128)S(1)} %get-tuple-element.67.moves.refs_9_.refs_13_, s32[32]{0:T(128)S(1)} %bitcast.1, f32[16,16,256]{2,1,0:T(8,128)S(1)} %copy-done.7, ...), custom_call_target="tpu_custom_call" | custom-call | flops 1048576 | bytes 1048576 | tf_op jit(solution)/shard_map/pallas_call | solution.py:27
  26.4 0.1 collective-permute-start.6
  26.5 0.0 copy-start.1
  26.5 0.0 copy-start.3
  26.5 1.2 %shard_map.147 = (f32[16,16,256]{2,1,0:T(8,128)S(1)}, f32[16,16,256]{2,1,0:T(8,128)S(1)}) custom-call(f32[16,16,256]{2,1,0:T(8,128)S(1)} %get-tuple-element.70.s.refs_1_.refs_8_, f32[16,16,256]{2,1,0:T(8,128)S(1)} %get-tuple-element.71.r.refs_2_.refs_9_), custom_call_target="tpu_custom_call" | custom-call | flops 1048576 | bytes 1048576 | tf_op jit(solution)/shard_map/pallas_call | solution.py:27
  27.8 0.0 copy-start.8
  27.8 1.8 %collective-permute-start.2 = (f32[3,8,8,256]{3,2,1,0:T(8,128)S(1)}, f32[3,8,8,256]{3,2,1,0:T(8,128)S(1)}, u32[]{:S(2)}, u32[]{:S(2)}) collective-permute-start(f32[3,8,8,256]{3,2,1,0:T(8,128)S(1)} %shard_map.148), channel_id=1, source_target_pairs={{0,248},{8,0},{16,8},{24,16},{32,24},{40,32},{48,40},{56,48},{64,5... | collective-permute-start | bytes 589832 | tf_op jit(solution)/shard_map/ppermute | solution.py:397
  29.7 2.3 %collective-permute-done.7.refs_6_ = f32[2,4,16,256]{3,2,1,0:T(8,128)S(1)} collective-permute-done((f32[2,4,16,256]{3,2,1,0:T(8,128)S(1)}, f32[2,4,16,256]{3,2,1,0:T(8,128)S(1)}, u32[]{:S(2)}, u32[]{:S(2)}) %collective-permute-start.7) | collective-permute-done | bytes 131104 | tf_op jit(solution)/shard_map/ppermute | solution.py:326
  31.9 0.0 collective-permute-done.9.refs_8_
  31.9 0.0 collective-permute-done.6.refs_0_.got
  32.0 0.5 shard_map.151
  32.5 3.1 %collective-permute-start.12 = (f32[2,4,16,256]{3,2,1,0:T(8,128)S(1)}, f32[2,4,16,256]{3,2,1,0:T(8,128)S(1)}, u32[]{:S(2)}, u32[]{:S(2)}) collective-permute-start(f32[2,4,16,256]{3,2,1,0:T(8,128)S(1)} %get-tuple-element.91), channel_id=1, source_target_pairs={{0,248},{8,16},{16,8},{24,32},{32,24},{40,48},{48,40},{56,64},{64,... | collective-permute-start | bytes 393224 | tf_op jit(solution)/shard_map/ppermute | solution.py:326
  35.5 0.7 collective-permute-start.11
  36.2 0.0 collective-permute-start.13
  36.2 3.0 %collective-permute-start.14 = (f32[2,8,8,256]{3,2,1,0:T(8,128)S(1)}, f32[2,8,8,256]{3,2,1,0:T(8,128)S(1)}, u32[]{:S(2)}, u32[]{:S(2)}) collective-permute-start(f32[2,8,8,256]{3,2,1,0:T(8,128)S(1)} %get-tuple-element.93), channel_id=1, source_target_pairs={{0,7},{1,2},{2,1},{3,4},{4,3},{5,6},{6,5},{7,0},{8,15},{9,10},{10,... | collective-permute-start | bytes 393224 | tf_op jit(solution)/shard_map/ppermute | solution.py:327
  39.2 3.8 %collective-permute-done.12.refs_5_.after = f32[2,4,16,256]{3,2,1,0:T(8,128)S(1)} collective-permute-done((f32[2,4,16,256]{3,2,1,0:T(8,128)S(1)}, f32[2,4,16,256]{3,2,1,0:T(8,128)S(1)}, u32[]{:S(2)}, u32[]{:S(2)}) %collective-permute-start.12) | collective-permute-done | bytes 131104 | tf_op jit(solution)/shard_map/ppermute | solution.py:326
  43.0 0.3 collective-permute-start.20
  43.3 0.0 collective-permute-done.2.come
  43.3 0.1 shard_map.152
  43.4 1.2 %shard_map.153 = (f32[16,16,256]{2,1,0:T(8,128)S(1)}, f32[16,16,256]{2,1,0:T(8,128)S(1)}) custom-call(f32[16,16,256]{2,1,0:T(8,128)S(1)} %get-tuple-element.86.s.refs_0_.refs_8_, f32[16,16,256]{2,1,0:T(8,128)S(1)} %get-tuple-element.87.r.refs_1_.refs_9_), custom_call_target="tpu_custom_call" | custom-call | flops 1048576 | bytes 1048576 | tf_op jit(solution)/shard_map/pallas_call | solution.py:27
  44.6 0.0 collective-permute-done.11.refs_4_
  44.7 0.0 collective-permute-done.14.refs_7_
  44.7 0.5 shard_map.154
  45.1 4.1 %collective-permute-start.16 = (f32[2,4,16,256]{3,2,1,0:T(8,128)S(1)}, f32[2,4,16,256]{3,2,1,0:T(8,128)S(1)}, u32[]{:S(2)}, u32[]{:S(2)}) collective-permute-start(f32[2,4,16,256]{3,2,1,0:T(8,128)S(1)} %get-tuple-element.101), channel_id=1, source_target_pairs={{0,248},{8,16},{16,8},{24,32},{32,24},{40,48},{48,40},{56,64},{64,... | collective-permute-start | bytes 393224 | tf_op jit(solution)/shard_map/ppermute | solution.py:326
  49.2 4.0 %collective-permute-start.18 = (f32[2,8,8,256]{3,2,1,0:T(8,128)S(1)}, f32[2,8,8,256]{3,2,1,0:T(8,128)S(1)}, u32[]{:S(2)}, u32[]{:S(2)}) collective-permute-start(f32[2,8,8,256]{3,2,1,0:T(8,128)S(1)} %get-tuple-element.103), channel_id=1, source_target_pairs={{0,7},{1,2},{2,1},{3,4},{4,3},{5,6},{6,5},{7,0},{8,15},{9,10},{10,... | collective-permute-start | bytes 393224 | tf_op jit(solution)/shard_map/ppermute | solution.py:327
  53.2 1.2 %shard_map.155 = (f32[16,16,256]{2,1,0:T(8,128)S(1)}, f32[16,16,256]{2,1,0:T(8,128)S(1)}) custom-call(f32[16,16,256]{2,1,0:T(8,128)S(1)} %get-tuple-element.96.s.refs_0_.refs_9_, f32[16,16,256]{2,1,0:T(8,128)S(1)} %get-tuple-element.97.r.refs_1_.refs_10_), custom_call_target="tpu_custom_call" | custom-call | flops 1048576 | bytes 1048576 | tf_op jit(solution)/shard_map/pallas_call | solution.py:27
  54.4 0.0 collective-permute-done.20.got
  54.4 1.0 %collective-permute-start.26 = (f32[16,16,256]{2,1,0:T(8,128)S(1)}, f32[16,16,256]{2,1,0:T(8,128)S(1)}, u32[]{:S(2)}, u32[]{:S(2)}) collective-permute-start(f32[16,16,256]{2,1,0:T(8,128)S(1)} %shard_map.162), channel_id=1, source_target_pairs={{0,248},{8,0},{16,8},{24,16},{32,24},{40,32},{48,40},{56,48},{64,5... | collective-permute-start | bytes 786440 | tf_op jit(solution)/shard_map/ppermute | solution.py:400
  55.4 0.0 collective-permute-done.16.refs_5_.after
  55.5 0.9 %collective-permute-start.21 = (f32[16,256]{1,0:T(8,128)S(1)}, f32[16,256]{1,0:T(8,128)S(1)}, u32[]{:S(2)}, u32[]{:S(2)}) collective-permute-start(f32[16,256]{1,0:T(8,128)S(1)} %get-tuple-element.110), channel_id=1, source_target_pairs={{0,16},{8,24},{16,0},{24,8},{32,48},{40,56},{48,32},{56,40},{64,80... | collective-permute-start | bytes 49160 | tf_op jit(solution)/shard_map/ppermute | solution.py:371
  56.4 0.0 collective-permute-done.15.refs_4_
  56.4 0.3 collective-permute-done.17.refs_6_
  56.7 0.4 shard_map.156
  57.2 1.7 %collective-permute-start.19 = (f32[2,4,16,256]{3,2,1,0:T(8,128)S(1)}, f32[2,4,16,256]{3,2,1,0:T(8,128)S(1)}, u32[]{:S(2)}, u32[]{:S(2)}) collective-permute-start(f32[2,4,16,256]{3,2,1,0:T(8,128)S(1)} %get-tuple-element.105), channel_id=1, source_target_pairs={{0,8},{8,0},{16,24},{24,16},{32,40},{40,32},{48,56},{56,48},{64,72... | collective-permute-start | bytes 393224 | tf_op jit(solution)/shard_map/ppermute | solution.py:325
  58.9 3.2 %collective-permute-start.23 = (f32[2,4,16,256]{3,2,1,0:T(8,128)S(1)}, f32[2,4,16,256]{3,2,1,0:T(8,128)S(1)}, u32[]{:S(2)}, u32[]{:S(2)}) collective-permute-start(f32[2,4,16,256]{3,2,1,0:T(8,128)S(1)} %get-tuple-element.119), channel_id=1, source_target_pairs={{0,248},{8,16},{16,8},{24,32},{32,24},{40,48},{48,40},{56,64},{64,... | collective-permute-start | bytes 393224 | tf_op jit(solution)/shard_map/ppermute | solution.py:326
  62.1 0.2 collective-permute-start.24
  62.3 4.2 %collective-permute-start.25 = (f32[2,8,8,256]{3,2,1,0:T(8,128)S(1)}, f32[2,8,8,256]{3,2,1,0:T(8,128)S(1)}, u32[]{:S(2)}, u32[]{:S(2)}) collective-permute-start(f32[2,8,8,256]{3,2,1,0:T(8,128)S(1)} %get-tuple-element.121), channel_id=1, source_target_pairs={{0,7},{1,2},{2,1},{3,4},{4,3},{5,6},{6,5},{7,0},{8,15},{9,10},{10,... | collective-permute-start | bytes 393224 | tf_op jit(solution)/shard_map/ppermute | solution.py:327
  66.5 1.7 %collective-permute-start.22 = (f32[8,256]{1,0:T(8,128)S(1)}, f32[8,256]{1,0:T(8,128)S(1)}, u32[]{:S(2)}, u32[]{:S(2)}) collective-permute-start(f32[8,256]{1,0:T(8,128)S(1)} %get-tuple-element.112), channel_id=1, source_target_pairs={{0,8},{8,0},{16,24},{24,16},{32,40},{40,32},{48,56},{56,48},{64,72... | collective-permute-start | bytes 24584 | tf_op jit(solution)/shard_map/ppermute | solution.py:371
  68.2 1.2 %shard_map.161 = (f32[16,16,256]{2,1,0:T(8,128)S(1)}, f32[16,16,256]{2,1,0:T(8,128)S(1)}) custom-call(f32[16,16,256]{2,1,0:T(8,128)S(1)} %get-tuple-element.115.s.refs_1_, f32[16,16,256]{2,1,0:T(8,128)S(1)} %get-tuple-element.116.r.refs_2_), custom_call_target="tpu_custom_call" | custom-call | flops 1048576 | bytes 1048576 | tf_op jit(solution)/shard_map/pallas_call | solution.py:27
  69.5 1.7 %shard_map.160 = (f32[16,16,256]{2,1,0:T(8,128)}, f32[8,128]{1,0:T(8,128)S(1)}) custom-call(s32[32]{0:T(128)S(1)} %bitcast.2, f32[8,256]{1,0:T(8,128)S(1)} %get-tuple-element.111.held, f32[8,256]{1,0:T(8,128)S(1)} %collective-permute-done.22.got, f32[16,16,256]{2,1,0:T(8,128)S(1)} %copy-done.11), custom_call_target="tpu_custom_call" | custom-call | flops 1048576 | bytes 1048576 | tf_op jit(solution)/shard_map/pallas_call | solution.py:27
  71.2 0.2 collective-permute-done.24.refs_7_
  71.4 1.3 %shard_map.163 = (f32[16,16,256]{2,1,0:T(8,128)}, f32[16,16,256]{2,1,0:T(8,128)}, f32[16,16,256]{2,1,0:T(8,128)}, f32[16,16,256]{2,1,0:T(8,128)}, f32[16,16,256]{2,1,0:T(8,128)}) custom-call(f32[8,128]{1,0:T(8,128)S(1)} %get-tuple-element.114.refs_0_, f32[16,16,256]{2,1,0:T(8,128)S(1)} %get-tuple-element.115.s.refs_1_, ...), custom_call_target="tpu_custom_call" | custom-call | flops 1048576 | bytes 1048576 | tf_op jit(solution)/shard_map/pallas_call | solution.py:27
  (37 shorter events, 0.2 us)
Async XLA Ops:
  0.6 15.4 %collective-permute-start = (f32[16,16,256]{2,1,0:T(8,128)}, f32[16,16,256]{2,1,0:T(8,128)S(1)}, u32[]{:S(2)}, u32[]{:S(2)}) collective-permute-start(f32[16,16,256]{2,1,0:T(8,128)} %s.3), channel_id=1, source_target_pairs={{0,248},{8,0},{16,8},{24,16},{32,24},{40,32},{48,40},{56,48},{64,5... | collective-permute-start | bytes 786440 | tf_op jit(solution)/shard_map/ppermute | solution.py:336
  4.0 12.1 %collective-permute-start.1 = (f32[16,16,256]{2,1,0:T(8,128)}, f32[16,16,256]{2,1,0:T(8,128)S(1)}, u32[]{:S(2)}, u32[]{:S(2)}) collective-permute-start(f32[16,16,256]{2,1,0:T(8,128)} %r.3), channel_id=1, source_target_pairs={{0,248},{8,0},{16,8},{24,16},{32,24},{40,32},{48,40},{56,48},{64,5... | collective-permute-start | bytes 786440 | tf_op jit(solution)/shard_map/ppermute | solution.py:337
  10.1 0.9 %copy-start = (f32[16,16,256]{2,1,0:T(8,128)S(1)}, f32[16,16,256]{2,1,0:T(8,128)}, u32[]{:S(2)}) copy-start(f32[16,16,256]{2,1,0:T(8,128)} %s_prev.1) | copy-start | bytes 786436
  11.1 0.9 %copy-start.2 = (f32[16,16,256]{2,1,0:T(8,128)S(1)}, f32[16,16,256]{2,1,0:T(8,128)}, u32[]{:S(2)}) copy-start(f32[16,16,256]{2,1,0:T(8,128)} %r_prev.1) | copy-start | bytes 786436
  12.0 0.9 %copy-start.4 = (f32[16,16,256]{2,1,0:T(8,128)S(1)}, f32[16,16,256]{2,1,0:T(8,128)}, u32[]{:S(2)}) copy-start(f32[16,16,256]{2,1,0:T(8,128)} %vel_own.1) | copy-start | bytes 786436
  13.0 0.9 %copy-start.6 = (f32[16,16,256]{2,1,0:T(8,128)S(1)}, f32[16,16,256]{2,1,0:T(8,128)}, u32[]{:S(2)}) copy-start(f32[16,16,256]{2,1,0:T(8,128)} %refs_14_.1) | copy-start | bytes 786436
  13.9 1.3 %copy-start.9 = (f32[16,16,256]{2,1,0:T(8,128)S(1)}, f32[16,16,256]{2,1,0:T(8,128)}, u32[]{:S(2)}) copy-start(f32[16,16,256]{2,1,0:T(8,128)} %s.3) | copy-start | bytes 786436
  13.9 1.3 %copy-start.10 = (f32[16,16,256]{2,1,0:T(8,128)S(1)}, f32[16,16,256]{2,1,0:T(8,128)}, u32[]{:S(2)}) copy-start(f32[16,16,256]{2,1,0:T(8,128)} %r.3) | copy-start | bytes 786436
  14.0 6.7 %collective-permute-start.4 = (f32[192,256]{1,0:T(8,128)S(1)}, f32[192,256]{1,0:T(8,128)S(1)}, u32[]{:S(2)}, u32[]{:S(2)}) collective-permute-start(f32[192,256]{1,0:T(8,128)S(1)} %get-tuple-element.75), channel_id=1, source_target_pairs={{0,248},{8,0},{16,8},{24,16},{32,24},{40,32},{48,40},{56,48},{64,5... | collective-permute-start | bytes 589832 | tf_op jit(solution)/shard_map/ppermute | solution.py:339
  14.8 0.7 copy-start.13
  14.8 8.0 %collective-permute-start.5 = (f32[192,256]{1,0:T(8,128)S(1)}, f32[192,256]{1,0:T(8,128)S(1)}, u32[]{:S(2)}, u32[]{:S(2)}) collective-permute-start(f32[192,256]{1,0:T(8,128)S(1)} %get-tuple-element.76), channel_id=1, source_target_pairs={{0,248},{8,0},{16,8},{24,16},{32,24},{40,32},{48,40},{56,48},{64,5... | collective-permute-start | bytes 589832 | tf_op jit(solution)/shard_map/ppermute | solution.py:339
  14.9 12.9 %collective-permute-start.10 = (f32[192,256]{1,0:T(8,128)S(1)}, f32[192,256]{1,0:T(8,128)S(1)}, u32[]{:S(2)}, u32[]{:S(2)}) collective-permute-start(f32[192,256]{1,0:T(8,128)S(1)} %get-tuple-element.81), channel_id=1, source_target_pairs={{0,248},{8,0},{16,8},{24,16},{32,24},{40,32},{48,40},{56,48},{64,5... | collective-permute-start | bytes 589832 | tf_op jit(solution)/shard_map/ppermute | solution.py:339
  16.1 9.3 %copy-start.7 = (f32[16,16,256]{2,1,0:T(8,128)S(1)}, f32[16,16,256]{2,1,0:T(8,128)}, u32[]{:S(2)}) copy-start(f32[16,16,256]{2,1,0:T(8,128)} %refs_14_.1) | copy-start | bytes 786436
  16.3 9.1 %collective-permute-start.3 = (f32[2,4,16,256]{3,2,1,0:T(8,128)S(1)}, f32[2,4,16,256]{3,2,1,0:T(8,128)S(1)}, u32[]{:S(2)}, u32[]{:S(2)}) collective-permute-start(f32[2,4,16,256]{3,2,1,0:T(8,128)S(1)} %get-tuple-element.74), channel_id=1, source_target_pairs={{0,8},{8,0},{16,24},{24,16},{32,40},{40,32},{48,56},{56,48},{64,72... | collective-permute-start | bytes 393224 | tf_op jit(solution)/shard_map/ppermute | solution.py:325
  19.2 12.7 %collective-permute-start.7 = (f32[2,4,16,256]{3,2,1,0:T(8,128)S(1)}, f32[2,4,16,256]{3,2,1,0:T(8,128)S(1)}, u32[]{:S(2)}, u32[]{:S(2)}) collective-permute-start(f32[2,4,16,256]{3,2,1,0:T(8,128)S(1)} %get-tuple-element.78), channel_id=1, source_target_pairs={{0,248},{8,16},{16,8},{24,32},{32,24},{40,48},{48,40},{56,64},{64,... | collective-permute-start | bytes 393224 | tf_op jit(solution)/shard_map/ppermute | solution.py:326
  20.7 11.2 %collective-permute-start.8 = (f32[2,8,8,256]{3,2,1,0:T(8,128)S(1)}, f32[2,8,8,256]{3,2,1,0:T(8,128)S(1)}, u32[]{:S(2)}, u32[]{:S(2)}) collective-permute-start(f32[2,8,8,256]{3,2,1,0:T(8,128)S(1)} %get-tuple-element.79), channel_id=1, source_target_pairs={{0,1},{1,0},{2,3},{3,2},{4,5},{5,4},{6,7},{7,6},{8,9},{9,8},{10,11... | collective-permute-start | bytes 393224 | tf_op jit(solution)/shard_map/ppermute | solution.py:328
  22.8 2.6 %copy-start.12 = (s32[1,32]{1,0:T(1,128)S(1)}, s32[1,32]{1,0:T(1,128)}, u32[]{:S(2)}) copy-start(s32[1,32]{1,0:T(1,128)} %param.19) | copy-start | bytes 388
  22.8 9.1 %collective-permute-start.9 = (f32[2,8,8,256]{3,2,1,0:T(8,128)S(1)}, f32[2,8,8,256]{3,2,1,0:T(8,128)S(1)}, u32[]{:S(2)}, u32[]{:S(2)}) collective-permute-start(f32[2,8,8,256]{3,2,1,0:T(8,128)S(1)} %get-tuple-element.80), channel_id=1, source_target_pairs={{0,7},{1,2},{2,1},{3,4},{4,3},{5,6},{6,5},{7,0},{8,15},{9,10},{10,... | collective-permute-start | bytes 393224 | tf_op jit(solution)/shard_map/ppermute | solution.py:327
  25.4 2.3 %copy-start.5 = (f32[16,16,256]{2,1,0:T(8,128)S(1)}, f32[16,16,256]{2,1,0:T(8,128)}, u32[]{:S(2)}) copy-start(f32[16,16,256]{2,1,0:T(8,128)} %vel_own.1) | copy-start | bytes 786436
  26.4 5.6 %collective-permute-start.6 = (f32[64,256]{1,0:T(8,128)S(1)}, f32[64,256]{1,0:T(8,128)S(1)}, u32[]{:S(2)}, u32[]{:S(2)}) collective-permute-start(f32[64,256]{1,0:T(8,128)S(1)} %get-tuple-element.77), channel_id=1, source_target_pairs={{0,64},{8,72},{16,80},{24,88},{32,96},{40,104},{48,112},{56,120},{... | collective-permute-start | bytes 196616 | tf_op jit(solution)/shard_map/ppermute | solution.py:371
  26.5 1.3 %copy-start.1 = (f32[16,16,256]{2,1,0:T(8,128)S(1)}, f32[16,16,256]{2,1,0:T(8,128)}, u32[]{:S(2)}) copy-start(f32[16,16,256]{2,1,0:T(8,128)} %s_prev.1) | copy-start | bytes 786436
  26.5 1.3 %copy-start.3 = (f32[16,16,256]{2,1,0:T(8,128)S(1)}, f32[16,16,256]{2,1,0:T(8,128)}, u32[]{:S(2)}) copy-start(f32[16,16,256]{2,1,0:T(8,128)} %r_prev.1) | copy-start | bytes 786436
  27.8 4.2 %copy-start.8 = (f32[16,16,256]{2,1,0:T(8,128)S(1)}, f32[16,16,256]{2,1,0:T(8,128)}, u32[]{:S(2)}) copy-start(f32[16,16,256]{2,1,0:T(8,128)} %vel_end.1) | copy-start | bytes 786436
  27.8 15.4 %collective-permute-start.2 = (f32[3,8,8,256]{3,2,1,0:T(8,128)S(1)}, f32[3,8,8,256]{3,2,1,0:T(8,128)S(1)}, u32[]{:S(2)}, u32[]{:S(2)}) collective-permute-start(f32[3,8,8,256]{3,2,1,0:T(8,128)S(1)} %shard_map.148), channel_id=1, source_target_pairs={{0,248},{8,0},{16,8},{24,16},{32,24},{40,32},{48,40},{56,48},{64,5... | collective-permute-start | bytes 589832 | tf_op jit(solution)/shard_map/ppermute | solution.py:397
  32.5 10.5 %collective-permute-start.12 = (f32[2,4,16,256]{3,2,1,0:T(8,128)S(1)}, f32[2,4,16,256]{3,2,1,0:T(8,128)S(1)}, u32[]{:S(2)}, u32[]{:S(2)}) collective-permute-start(f32[2,4,16,256]{3,2,1,0:T(8,128)S(1)} %get-tuple-element.91), channel_id=1, source_target_pairs={{0,248},{8,16},{16,8},{24,32},{32,24},{40,48},{48,40},{56,64},{64,... | collective-permute-start | bytes 393224 | tf_op jit(solution)/shard_map/ppermute | solution.py:326
  35.5 9.1 %collective-permute-start.11 = (f32[2,4,16,256]{3,2,1,0:T(8,128)S(1)}, f32[2,4,16,256]{3,2,1,0:T(8,128)S(1)}, u32[]{:S(2)}, u32[]{:S(2)}) collective-permute-start(f32[2,4,16,256]{3,2,1,0:T(8,128)S(1)} %get-tuple-element.90), channel_id=1, source_target_pairs={{0,8},{8,0},{16,24},{24,16},{32,40},{40,32},{48,56},{56,48},{64,72... | collective-permute-start | bytes 393224 | tf_op jit(solution)/shard_map/ppermute | solution.py:325
  36.2 8.5 %collective-permute-start.13 = (f32[2,8,8,256]{3,2,1,0:T(8,128)S(1)}, f32[2,8,8,256]{3,2,1,0:T(8,128)S(1)}, u32[]{:S(2)}, u32[]{:S(2)}) collective-permute-start(f32[2,8,8,256]{3,2,1,0:T(8,128)S(1)} %get-tuple-element.92), channel_id=1, source_target_pairs={{0,1},{1,0},{2,3},{3,2},{4,5},{5,4},{6,7},{7,6},{8,9},{9,8},{10,11... | collective-permute-start | bytes 393224 | tf_op jit(solution)/shard_map/ppermute | solution.py:328
  36.2 8.5 %collective-permute-start.14 = (f32[2,8,8,256]{3,2,1,0:T(8,128)S(1)}, f32[2,8,8,256]{3,2,1,0:T(8,128)S(1)}, u32[]{:S(2)}, u32[]{:S(2)}) collective-permute-start(f32[2,8,8,256]{3,2,1,0:T(8,128)S(1)} %get-tuple-element.93), channel_id=1, source_target_pairs={{0,7},{1,2},{2,1},{3,4},{4,3},{5,6},{6,5},{7,0},{8,15},{9,10},{10,... | collective-permute-start | bytes 393224 | tf_op jit(solution)/shard_map/ppermute | solution.py:327
  43.0 11.4 %collective-permute-start.20 = (f32[32,256]{1,0:T(8,128)S(1)}, f32[32,256]{1,0:T(8,128)S(1)}, u32[]{:S(2)}, u32[]{:S(2)}) collective-permute-start(f32[32,256]{1,0:T(8,128)S(1)} %get-tuple-element.108), channel_id=1, source_target_pairs={{0,32},{8,40},{16,48},{24,56},{32,0},{40,8},{48,16},{56,24},{64,96... | collective-permute-start | bytes 98312 | tf_op jit(solution)/shard_map/ppermute | solution.py:371
  45.1 10.3 %collective-permute-start.16 = (f32[2,4,16,256]{3,2,1,0:T(8,128)S(1)}, f32[2,4,16,256]{3,2,1,0:T(8,128)S(1)}, u32[]{:S(2)}, u32[]{:S(2)}) collective-permute-start(f32[2,4,16,256]{3,2,1,0:T(8,128)S(1)} %get-tuple-element.101), channel_id=1, source_target_pairs={{0,248},{8,16},{16,8},{24,32},{32,24},{40,48},{48,40},{56,64},{64,... | collective-permute-start | bytes 393224 | tf_op jit(solution)/shard_map/ppermute | solution.py:326
  49.2 7.2 %collective-permute-start.15 = (f32[2,4,16,256]{3,2,1,0:T(8,128)S(1)}, f32[2,4,16,256]{3,2,1,0:T(8,128)S(1)}, u32[]{:S(2)}, u32[]{:S(2)}) collective-permute-start(f32[2,4,16,256]{3,2,1,0:T(8,128)S(1)} %get-tuple-element.100), channel_id=1, source_target_pairs={{0,8},{8,0},{16,24},{24,16},{32,40},{40,32},{48,56},{56,48},{64,72... | collective-permute-start | bytes 393224 | tf_op jit(solution)/shard_map/ppermute | solution.py:325
  49.2 7.5 %collective-permute-start.17 = (f32[2,8,8,256]{3,2,1,0:T(8,128)S(1)}, f32[2,8,8,256]{3,2,1,0:T(8,128)S(1)}, u32[]{:S(2)}, u32[]{:S(2)}) collective-permute-start(f32[2,8,8,256]{3,2,1,0:T(8,128)S(1)} %get-tuple-element.102), channel_id=1, source_target_pairs={{0,1},{1,0},{2,3},{3,2},{4,5},{5,4},{6,7},{7,6},{8,9},{9,8},{10,11... | collective-permute-start | bytes 393224 | tf_op jit(solution)/shard_map/ppermute | solution.py:328
  49.2 7.5 %collective-permute-start.18 = (f32[2,8,8,256]{3,2,1,0:T(8,128)S(1)}, f32[2,8,8,256]{3,2,1,0:T(8,128)S(1)}, u32[]{:S(2)}, u32[]{:S(2)}) collective-permute-start(f32[2,8,8,256]{3,2,1,0:T(8,128)S(1)} %get-tuple-element.103), channel_id=1, source_target_pairs={{0,7},{1,2},{2,1},{3,4},{4,3},{5,6},{6,5},{7,0},{8,15},{9,10},{10,... | collective-permute-start | bytes 393224 | tf_op jit(solution)/shard_map/ppermute | solution.py:327
  54.4 16.9 %collective-permute-start.26 = (f32[16,16,256]{2,1,0:T(8,128)S(1)}, f32[16,16,256]{2,1,0:T(8,128)S(1)}, u32[]{:S(2)}, u32[]{:S(2)}) collective-permute-start(f32[16,16,256]{2,1,0:T(8,128)S(1)} %shard_map.162), channel_id=1, source_target_pairs={{0,248},{8,0},{16,8},{24,16},{32,24},{40,32},{48,40},{56,48},{64,5... | collective-permute-start | bytes 786440 | tf_op jit(solution)/shard_map/ppermute | solution.py:400
  55.5 6.8 %collective-permute-start.21 = (f32[16,256]{1,0:T(8,128)S(1)}, f32[16,256]{1,0:T(8,128)S(1)}, u32[]{:S(2)}, u32[]{:S(2)}) collective-permute-start(f32[16,256]{1,0:T(8,128)S(1)} %get-tuple-element.110), channel_id=1, source_target_pairs={{0,16},{8,24},{16,0},{24,8},{32,48},{40,56},{48,32},{56,40},{64,80... | collective-permute-start | bytes 49160 | tf_op jit(solution)/shard_map/ppermute | solution.py:371
  57.2 9.3 %collective-permute-start.19 = (f32[2,4,16,256]{3,2,1,0:T(8,128)S(1)}, f32[2,4,16,256]{3,2,1,0:T(8,128)S(1)}, u32[]{:S(2)}, u32[]{:S(2)}) collective-permute-start(f32[2,4,16,256]{3,2,1,0:T(8,128)S(1)} %get-tuple-element.105), channel_id=1, source_target_pairs={{0,8},{8,0},{16,24},{24,16},{32,40},{40,32},{48,56},{56,48},{64,72... | collective-permute-start | bytes 393224 | tf_op jit(solution)/shard_map/ppermute | solution.py:325
  58.9 12.2 %collective-permute-start.23 = (f32[2,4,16,256]{3,2,1,0:T(8,128)S(1)}, f32[2,4,16,256]{3,2,1,0:T(8,128)S(1)}, u32[]{:S(2)}, u32[]{:S(2)}) collective-permute-start(f32[2,4,16,256]{3,2,1,0:T(8,128)S(1)} %get-tuple-element.119), channel_id=1, source_target_pairs={{0,248},{8,16},{16,8},{24,32},{32,24},{40,48},{48,40},{56,64},{64,... | collective-permute-start | bytes 393224 | tf_op jit(solution)/shard_map/ppermute | solution.py:326
  62.1 9.2 %collective-permute-start.24 = (f32[2,8,8,256]{3,2,1,0:T(8,128)S(1)}, f32[2,8,8,256]{3,2,1,0:T(8,128)S(1)}, u32[]{:S(2)}, u32[]{:S(2)}) collective-permute-start(f32[2,8,8,256]{3,2,1,0:T(8,128)S(1)} %get-tuple-element.120), channel_id=1, source_target_pairs={{0,1},{1,0},{2,3},{3,2},{4,5},{5,4},{6,7},{7,6},{8,9},{9,8},{10,11... | collective-permute-start | bytes 393224 | tf_op jit(solution)/shard_map/ppermute | solution.py:328
  62.3 9.1 %collective-permute-start.25 = (f32[2,8,8,256]{3,2,1,0:T(8,128)S(1)}, f32[2,8,8,256]{3,2,1,0:T(8,128)S(1)}, u32[]{:S(2)}, u32[]{:S(2)}) collective-permute-start(f32[2,8,8,256]{3,2,1,0:T(8,128)S(1)} %get-tuple-element.121), channel_id=1, source_target_pairs={{0,7},{1,2},{2,1},{3,4},{4,3},{5,6},{6,5},{7,0},{8,15},{9,10},{10,... | collective-permute-start | bytes 393224 | tf_op jit(solution)/shard_map/ppermute | solution.py:327
  66.5 3.0 %collective-permute-start.22 = (f32[8,256]{1,0:T(8,128)S(1)}, f32[8,256]{1,0:T(8,128)S(1)}, u32[]{:S(2)}, u32[]{:S(2)}) collective-permute-start(f32[8,256]{1,0:T(8,128)S(1)} %get-tuple-element.112), channel_id=1, source_target_pairs={{0,8},{8,0},{16,24},{24,16},{32,40},{40,32},{48,56},{56,48},{64,72... | collective-permute-start | bytes 24584 | tf_op jit(solution)/shard_map/ppermute | solution.py:371
  68.2 1.2 %copy-start.11 = (f32[16,16,256]{2,1,0:T(8,128)S(1)}, f32[16,16,256]{2,1,0:T(8,128)}, u32[]{:S(2)}) copy-start(f32[16,16,256]{2,1,0:T(8,128)} %base.1) | copy-start | bytes 786436
